TPU v7x, 32 devices: a whole 2x2x4 slice. The times are simulated.
32 devices in a mesh: ctx: 8 (over z, x), fsdp: 4 (over y, core).
Axes of the slice: x: 2, y: 2, z: 4, core: 2. Of those that a mesh axis runs over, the one named last changes fastest.
Arguments:
- tokens: bfloat16 [4, 1024, 2048], P('fsdp', 'ctx'), may hold values from -6 to 6
- cotangent: bfloat16 [4, 1024, 2048], P('fsdp', 'ctx'), may hold values from -6 to 6
- lengths: int32 [4, 3], P('fsdp'), may hold values from 1 to 512, 1024 in all within a row
- deal: int32 [4, 8, 8], P('fsdp'), may hold values from 0 to 7, each once within a row
- norm1_gain: float32 [2048], P('fsdp'), may hold values from 0.1 to 1.9
- w_qkv: float32 [2048, 6144], P('fsdp'), may hold values from -0.125 to 0.125
- w_out: float32 [2048, 2048], P('fsdp'), may hold values from -2 to 2
- norm2_gain: float32 [2048], P('fsdp'), may hold values from 0.1 to 1.9
- w_gate_up: float32 [2048, 11008], P('fsdp'), may hold values from -0.125 to 0.125
- w_down: float32 [5504, 2048], P('fsdp'), may hold values from -0.078125 to 0.078125
Outputs:
- block_out: bfloat16 [4, 1024, 2048], P('fsdp', 'ctx')
- grad_tokens: bfloat16 [4, 1024, 2048], P('fsdp', 'ctx')
- grad_norm1: float32 [2048], P('fsdp')
- grad_qkv: float32 [2048, 6144], P('fsdp')
- grad_out: float32 [2048, 2048], P('fsdp')
- grad_norm2: float32 [2048], P('fsdp')
- grad_gate_up: float32 [2048, 11008], P('fsdp')
- grad_down: float32 [5504, 2048], P('fsdp')
Inputs may be any that keep to these rules, and one draw needn't show every extreme that they name: `lengths`: the 3 documents of a group fill its 1024 tokens in order; the longest has exactly 512. deal[f, d] lists, for the 16-token pieces of ctx device d of group f in order, the ctx device each piece goes to; each row names every device once.
All inputs are finite; a program needn't handle non-finite values.
Results may differ from a plain program's by a relative error of at most 0.019.
The roundings to bfloat16 on the way count: a program that leaves them out, or rounds other values in their place, can miss the bound.
Values may be sent and summed in bfloat16 or wider, within the bound.
A program may use at most 512 MiB of HBM per device.

v0:
```python
import math

import jax
import jax.numpy as jnp
from jax import lax
from jax.sharding import PartitionSpec as P

H = 16
HD = 128
FF = 5504


epsilon = 1e-06
rope_base = 10000.0
masked_score = -1e30


def rope_tables(within):
    freq_index = jnp.arange(HD // 2, dtype=jnp.float32)
    inverse = rope_base ** (-2.0 * freq_index / HD)
    angles = within.astype(jnp.float32)[:, None] * inverse[None, :]
    cosine_table = jnp.concatenate([jnp.cos(angles), jnp.cos(angles)], -1)
    sine_table = jnp.concatenate([jnp.sin(angles), jnp.sin(angles)], -1)
    return (cosine_table, sine_table)


def rotate(values, cosine_table, sine_table):
    half_size = values.shape[-1] // 2
    turned = jnp.concatenate([-values[..., half_size:], values[..., :half_size]], -1)
    return values * cosine_table[:, None, :] + turned * sine_table[:, None, :]


def unrotate(grads, cosine_table, sine_table):
    half_size = grads.shape[-1] // 2
    scaled = grads * sine_table[:, None, :]
    turned = jnp.concatenate([-scaled[..., half_size:], scaled[..., :half_size]], -1)
    return grads * cosine_table[:, None, :] - turned


def rms_scale(values):
    return lax.rsqrt(jnp.mean(values * values, -1, keepdims=True) + epsilon)


def norm_back(grad_norm, values, scale_rows, gain_float):
    scaled = grad_norm * gain_float[None, :]
    cubed = scale_rows * scale_rows * scale_rows
    return scale_rows * scaled - values * cubed * jnp.mean(scaled * values, -1, keepdims=True)


def source_pieces(deal_table, ctx_count):
    device_index = jnp.arange(ctx_count, dtype=jnp.int32)
    marks = (deal_table[:, :, None] == device_index[None, None, :]).astype(jnp.int32)
    return jnp.sum(marks * device_index[None, :, None], 1)


def shards(
    tokens, cotangent, lengths, deal, norm1_gain, w_qkv, w_out, norm2_gain, w_gate_up, w_down
):
    ctx_count = lax.axis_size("ctx")
    my_index = lax.axis_index("ctx")
    tok_rows = tokens.shape[1]
    width = tokens.shape[2]
    piece_rows = tok_rows // ctx_count
    all_rows = tok_rows * ctx_count
    deal_table = deal[0]
    source_piece = source_pieces(deal_table, ctx_count)
    send_order = lax.dynamic_index_in_dim(source_piece, my_index, 0, keepdims=False)
    own_row = lax.dynamic_index_in_dim(deal_table, my_index, 0, keepdims=False)
    given_pieces = tokens[0].reshape(ctx_count, piece_rows, width)
    arrived = lax.all_to_all(
        jnp.take(given_pieces, send_order, axis=0), "ctx", split_axis=0, concat_axis=0, tiled=True
    )
    inputs = arrived.reshape(tok_rows, width).astype(jnp.float32)
    device_index = jnp.arange(ctx_count, dtype=jnp.int32)
    slot_places = (
        device_index[None, :, None] * tok_rows
        + jnp.transpose(source_piece)[:, :, None] * piece_rows
        + jnp.arange(piece_rows, dtype=jnp.int32)[None, None, :]
    ).reshape(ctx_count, tok_rows)
    doc_lengths = lengths[0]
    ends = jnp.cumsum(doc_lengths)
    starts = ends - doc_lengths
    doc_ids = jnp.sum((slot_places[:, :, None] >= ends[None, None, :]).astype(jnp.int32), -1)
    doc_index = jnp.arange(doc_lengths.shape[0], dtype=jnp.int32)
    firsts = jnp.sum(
        jnp.where(doc_ids[:, :, None] == doc_index[None, None, :], starts[None, None, :], 0), -1
    )
    within_all = slot_places - firsts
    key_places = slot_places.reshape(all_rows)
    key_docs = doc_ids.reshape(all_rows)
    query_places = lax.dynamic_index_in_dim(slot_places, my_index, 0, keepdims=False)
    query_docs = lax.dynamic_index_in_dim(doc_ids, my_index, 0, keepdims=False)
    query_within = lax.dynamic_index_in_dim(within_all, my_index, 0, keepdims=False)
    allowed = (key_docs[None, :] == query_docs[:, None]) & (
        key_places[None, :] <= query_places[:, None]
    )
    cosine_table, sine_table = rope_tables(query_within)
    factor = 1.0 / math.sqrt(HD)
    gain_one, weight_qkv, weight_out, gain_two, weight_gate_up, weight_down = (
        lax.all_gather(norm1_gain.astype(jnp.bfloat16), "fsdp", axis=0, tiled=True),
        lax.all_gather(w_qkv.astype(jnp.bfloat16), "fsdp", axis=0, tiled=True),
        lax.all_gather(w_out.astype(jnp.bfloat16), "fsdp", axis=0, tiled=True),
        lax.all_gather(norm2_gain.astype(jnp.bfloat16), "fsdp", axis=0, tiled=True),
        lax.all_gather(w_gate_up.astype(jnp.bfloat16), "fsdp", axis=0, tiled=True),
        lax.all_gather(w_down.astype(jnp.bfloat16), "fsdp", axis=0, tiled=True),
    )
    scale_one = rms_scale(inputs)
    normed_one = (inputs * scale_one * gain_one.astype(jnp.float32)[None, :]).astype(jnp.bfloat16)
    projected = jnp.dot(normed_one, weight_qkv, preferred_element_type=jnp.float32)
    queries = rotate(
        projected[:, :width].reshape(tok_rows, H, HD), cosine_table, sine_table
    ).astype(jnp.bfloat16)
    keys = rotate(
        projected[:, width : 2 * width].reshape(tok_rows, H, HD), cosine_table, sine_table
    ).astype(jnp.bfloat16)
    values = projected[:, 2 * width :].astype(jnp.bfloat16)
    key_all, value_all = (
        lax.all_gather(keys.reshape(tok_rows, width), "ctx", axis=0, tiled=True),
        lax.all_gather(values, "ctx", axis=0, tiled=True),
    )
    key_heads = key_all.reshape(all_rows, H, HD)
    value_heads = value_all.reshape(all_rows, H, HD)
    logits = jnp.einsum("qhd,khd->hqk", queries, key_heads, preferred_element_type=jnp.float32)
    scaled = jnp.where(allowed[None], logits * factor, masked_score)
    row_top = jnp.max(scaled, -1, keepdims=True)
    raised = jnp.exp(scaled - row_top)
    row_total = jnp.sum(raised, -1, keepdims=True)
    probs = raised / row_total
    log_total = row_top + jnp.log(row_total)
    mixed = (
        jnp.einsum(
            "hqk,khd->qhd",
            probs.astype(jnp.bfloat16),
            value_heads,
            preferred_element_type=jnp.float32,
        )
        .reshape(tok_rows, width)
        .astype(jnp.bfloat16)
    )
    hidden = inputs + jnp.dot(mixed, weight_out, preferred_element_type=jnp.float32)
    scale_two = rms_scale(hidden)
    gain_float = gain_two.astype(jnp.float32)
    normed_two = (hidden * scale_two * gain_float[None, :]).astype(jnp.bfloat16)
    both = jnp.dot(normed_two, weight_gate_up, preferred_element_type=jnp.float32)
    gate_part = both[:, :FF]
    up_part = both[:, FF:]
    gate_sigma = jax.nn.sigmoid(gate_part)
    gate_act = gate_part * gate_sigma
    activated = (gate_act * up_part).astype(jnp.bfloat16)
    output = hidden + jnp.dot(activated, weight_down, preferred_element_type=jnp.float32)
    block_out = output.astype(jnp.bfloat16)[None]
    gain_one, weight_qkv, weight_out, gain_two, weight_gate_up, weight_down = (
        lax.all_gather(norm1_gain.astype(jnp.bfloat16), "fsdp", axis=0, tiled=True),
        lax.all_gather(w_qkv.astype(jnp.bfloat16), "fsdp", axis=0, tiled=True),
        lax.all_gather(w_out.astype(jnp.bfloat16), "fsdp", axis=0, tiled=True),
        lax.all_gather(norm2_gain.astype(jnp.bfloat16), "fsdp", axis=0, tiled=True),
        lax.all_gather(w_gate_up.astype(jnp.bfloat16), "fsdp", axis=0, tiled=True),
        lax.all_gather(w_down.astype(jnp.bfloat16), "fsdp", axis=0, tiled=True),
    )
    grad_rows = cotangent[0]
    upstream = grad_rows.astype(jnp.float32)
    grad_down = jnp.einsum("tf,td->fd", activated, grad_rows, preferred_element_type=jnp.float32)
    d_act = jnp.einsum("td,fd->tf", grad_rows, weight_down, preferred_element_type=jnp.float32)
    d_both = jnp.concatenate(
        [d_act * up_part * gate_sigma * (1.0 + gate_part * (1.0 - gate_sigma)), d_act * gate_act],
        -1,
    ).astype(jnp.bfloat16)
    grad_gate_up = jnp.einsum("tc,tf->cf", normed_two, d_both, preferred_element_type=jnp.float32)
    d_two = jnp.einsum("tf,cf->tc", d_both, weight_gate_up, preferred_element_type=jnp.float32)
    grad_norm2 = jnp.sum(d_two * hidden * scale_two, 0)
    d_hidden = upstream + norm_back(d_two, hidden, scale_two, gain_float)
    col_gate_up, col_down = (
        lax.psum_scatter(
            grad_gate_up.astype(jnp.bfloat16), "ctx", scatter_dimension=1, tiled=True
        ).astype(jnp.float32),
        lax.psum_scatter(
            grad_down.astype(jnp.bfloat16), "ctx", scatter_dimension=1, tiled=True
        ).astype(jnp.float32),
    )
    d_branch = d_hidden.astype(jnp.bfloat16)
    grad_out = jnp.einsum("tc,td->cd", mixed, d_branch, preferred_element_type=jnp.float32)
    d_mixed = (
        jnp.einsum("td,cd->tc", d_branch, weight_out, preferred_element_type=jnp.float32)
        .astype(jnp.bfloat16)
        .reshape(tok_rows, H, HD)
    )
    logits_again = jnp.einsum(
        "qhd,khd->hqk", queries, key_heads, preferred_element_type=jnp.float32
    )
    scaled_again = jnp.where(allowed[None], logits_again * factor, masked_score)
    probs_again = jnp.exp(scaled_again - log_total)
    d_probs = jnp.einsum("qhd,khd->hqk", d_mixed, value_heads, preferred_element_type=jnp.float32)
    row_inner = jnp.sum(probs_again * d_probs, -1, keepdims=True)
    d_scores = (probs_again * (d_probs - row_inner) * factor).astype(jnp.bfloat16)
    d_queries = jnp.einsum("hqk,khd->qhd", d_scores, key_heads, preferred_element_type=jnp.float32)
    key_term = jnp.einsum(
        "hqk,qhd->khd", d_scores, queries, preferred_element_type=jnp.float32
    ).reshape(all_rows, width)
    value_term = jnp.einsum(
        "hqk,qhd->khd",
        probs_again.astype(jnp.bfloat16),
        d_mixed,
        preferred_element_type=jnp.float32,
    ).reshape(all_rows, width)
    d_keys, d_values = (
        lax.psum_scatter(key_term, "ctx", scatter_dimension=0, tiled=True),
        lax.psum_scatter(value_term, "ctx", scatter_dimension=0, tiled=True),
    )
    d_proj = jnp.concatenate(
        [
            unrotate(d_queries, cosine_table, sine_table).reshape(tok_rows, width),
            unrotate(d_keys.reshape(tok_rows, H, HD), cosine_table, sine_table).reshape(
                tok_rows, width
            ),
            d_values,
        ],
        -1,
    ).astype(jnp.bfloat16)
    grad_qkv = jnp.einsum("tc,tf->cf", normed_one, d_proj, preferred_element_type=jnp.float32)
    d_one = jnp.einsum("tf,cf->tc", d_proj, weight_qkv, preferred_element_type=jnp.float32)
    grad_norm1 = jnp.sum(d_one * inputs * scale_one, 0)
    d_tokens = (
        d_hidden + norm_back(d_one, inputs, scale_one, gain_one.astype(jnp.float32))
    ).astype(jnp.bfloat16)
    returned = lax.all_to_all(
        d_tokens.reshape(ctx_count, piece_rows, width),
        "ctx",
        split_axis=0,
        concat_axis=0,
        tiled=True,
    )
    grad_tokens = jnp.take(returned, own_row, axis=0).reshape(1, tok_rows, width)
    col_qkv, col_out = (
        lax.psum_scatter(
            grad_qkv.astype(jnp.bfloat16), "ctx", scatter_dimension=1, tiled=True
        ).astype(jnp.float32),
        lax.psum_scatter(
            grad_out.astype(jnp.bfloat16), "ctx", scatter_dimension=1, tiled=True
        ).astype(jnp.float32),
    )
    row_qkv, row_out, row_gate_up, row_down = (
        lax.psum_scatter(
            col_qkv.astype(jnp.bfloat16), "fsdp", scatter_dimension=0, tiled=True
        ).astype(jnp.float32),
        lax.psum_scatter(
            col_out.astype(jnp.bfloat16), "fsdp", scatter_dimension=0, tiled=True
        ).astype(jnp.float32),
        lax.psum_scatter(
            col_gate_up.astype(jnp.bfloat16), "fsdp", scatter_dimension=0, tiled=True
        ).astype(jnp.float32),
        lax.psum_scatter(
            col_down.astype(jnp.bfloat16), "fsdp", scatter_dimension=0, tiled=True
        ).astype(jnp.float32),
    )
    final_qkv, final_out, final_gate_up, final_down = (
        lax.all_gather(row_qkv.astype(jnp.bfloat16), "ctx", axis=1, tiled=True).astype(
            row_qkv.dtype
        ),
        lax.all_gather(row_out.astype(jnp.bfloat16), "ctx", axis=1, tiled=True).astype(
            row_out.dtype
        ),
        lax.all_gather(row_gate_up.astype(jnp.bfloat16), "ctx", axis=1, tiled=True).astype(
            row_gate_up.dtype
        ),
        lax.all_gather(row_down.astype(jnp.bfloat16), "ctx", axis=1, tiled=True).astype(
            row_down.dtype
        ),
    )
    norm_one_sum, norm_two_sum = lax.psum((grad_norm1, grad_norm2), ("ctx", "fsdp"))
    gain_rows = norm_one_sum.shape[0] // lax.axis_size("fsdp")
    gain_start = lax.axis_index("fsdp") * gain_rows
    final_norm1 = lax.dynamic_slice_in_dim(norm_one_sum, gain_start, gain_rows)
    final_norm2 = lax.dynamic_slice_in_dim(norm_two_sum, gain_start, gain_rows)
    return (
        block_out,
        grad_tokens,
        final_norm1,
        final_qkv,
        final_out,
        final_norm2,
        final_gate_up,
        final_down,
    )


def solution(mesh):
    in_specs = (
        P("fsdp", "ctx", None),
        P("fsdp", "ctx", None),
        P("fsdp", None),
        P("fsdp", None, None),
        P("fsdp"),
        P("fsdp", None),
        P("fsdp", None),
        P("fsdp"),
        P("fsdp", None),
        P("fsdp", None),
    )
    out_specs = (
        P("fsdp", "ctx", None),
        P("fsdp", "ctx", None),
        P("fsdp"),
        P("fsdp", None),
        P("fsdp", None),
        P("fsdp"),
        P("fsdp", None),
        P("fsdp", None),
    )
    return jax.shard_map(shards, mesh=mesh, in_specs=in_specs, out_specs=out_specs, check_vma=False)
```

profile of v0, /device:TPU:0, one launch (start us, length us, event | category | flops | bytes accessed | tf_op | source)
XLA Modules:
  0.0 3442.4 jit_solution(5053355829170065943)
XLA Ops:
  7.2 8.3 convert_element_type.151
  17.2 7.3 all-to-all-start
  31.2 7.7 all-to-all-done
  39.4 133.8 %all-gather.13.cloned.1.call-done = bf16[2048,6144]{1,0:T(8,128)(2,1)} async-done(((bf16[512,6144]{1,0:T(8,128)(2,1)}), bf16[2048,6144]{1,0:T(8,128)(2,1)}) %all-gather.13.cloned.1.call-update) | async-done | bytes 25165840 | tf_op jit(solution)/shard_map/all_gather | solution.py:101
  173.2 10.0 fusion.98
  198.2 12.3 convert_element_type.165
  210.6 7.6 convert_element_type.167
  224.5 41.0 %all-gather.17.cloned.1.call-done = bf16[1024,2048]{1,0:T(8,128)(2,1)} async-done(((bf16[128,2048]{1,0:T(8,128)(2,1)}), bf16[1024,2048]{1,0:T(8,128)(2,1)}) %all-gather.17.cloned.1.call-update) | async-done | bytes 4194320 | tf_op jit(solution)/shard_map/all_gather | solution.py:118
  265.5 6.6 copy.91
  282.0 57.9 %all-gather.15.cloned.1.call-done = bf16[1024,2048]{1,0:T(8,128)(2,1)} async-done(((bf16[128,2048]{1,0:T(8,128)(2,1)}), bf16[1024,2048]{1,0:T(8,128)(2,1)}) %all-gather.15.cloned.1.call-update) | async-done | bytes 4194320 | tf_op jit(solution)/shard_map/all_gather | solution.py:119
  339.9 7.9 fusion.49
  347.8 50.1 %all-gather.19.cloned.1.call-done = bf16[2048,2048]{1,0:T(8,128)(2,1)} async-done(((bf16[512,2048]{1,0:T(8,128)(2,1)}), bf16[2048,2048]{1,0:T(8,128)(2,1)}) %all-gather.19.cloned.1.call-update) | async-done | bytes 8388624 | tf_op jit(solution)/shard_map/all_gather | solution.py:102
  402.7 265.1 %all-gather.21.cloned.1.call-done = bf16[2048,11008]{1,0:T(8,128)(2,1)} async-done(((bf16[512,11008]{1,0:T(8,128)(2,1)}), bf16[2048,11008]{1,0:T(8,128)(2,1)}) %all-gather.21.cloned.1.call-update) | async-done | bytes 45088784 | tf_op jit(solution)/shard_map/all_gather | solution.py:104
  667.8 23.5 fusion.95
  691.3 118.9 %all-gather.23.cloned.1.call-done = bf16[5504,2048]{1,0:T(8,128)(2,1)} async-done(((bf16[1376,2048]{1,0:T(8,128)(2,1)}), bf16[5504,2048]{1,0:T(8,128)(2,1)}) %all-gather.23.cloned.1.call-update) | async-done | bytes 22544400 | tf_op jit(solution)/shard_map/all_gather | solution.py:105
  810.1 15.0 multiply_convert_fusion.2
  825.1 21.9 multiply_reduce_fusion.1
  848.8 7.1 convolution_convert_fusion.4
  857.9 7.0 fusion.17
  864.9 25.1 fusion.8
  890.0 9.2 copy.85
  899.2 9.7 fusion.13
  909.0 9.2 copy.88
  918.3 6.8 convolution_convert_fusion.3
  925.1 12.3 convolution_convert_fusion.1
  937.5 110.8 %reduce-scatter.13.cloned.1.call-done = f32[128,2048]{1,0:T(8,128)} async-done(((f32[1024,2048]{1,0:T(8,128)}), f32[128,2048]{1,0:T(8,128)}) %reduce-scatter.13.cloned.1.call-update) | async-done | bytes 1048592 | tf_op jit(solution)/shard_map/reduce_scatter | solution.py:206
  1049.9 25.4 broadcast_multiply_fusion.1
  1085.8 114.6 %reduce-scatter.15.cloned.1.call-done = f32[128,2048]{1,0:T(8,128)} async-done(((f32[1024,2048]{1,0:T(8,128)}), f32[128,2048]{1,0:T(8,128)}) %reduce-scatter.15.cloned.1.call-update) | async-done | bytes 1048592 | tf_op jit(solution)/shard_map/reduce_scatter | solution.py:207
  1205.0 13.6 convolution_convert_fusion.2
  1219.9 19.7 convolution_convert_fusion
  1239.8 113.3 %reduce-scatter.21.cloned.1.call-done = bf16[2048,256]{1,0:T(8,128)(2,1)} async-done(((bf16[2048,2048]{1,0:T(8,128)(2,1)}), bf16[2048,256]{1,0:T(8,128)(2,1)}) %reduce-scatter.21.cloned.1.call-update) | async-done | bytes 1048592 | tf_op jit(solution)/shard_map/reduce_scatter | solution.py:237
  1353.1 370.6 %reduce-scatter.27.cloned.1.call-done = bf16[5504,256]{1,0:T(8,128)(2,1)} async-done(((bf16[5504,2048]{1,0:T(8,128)(2,1)}), bf16[5504,256]{1,0:T(8,128)(2,1)}) %reduce-scatter.27.cloned.1.call-update) | async-done | bytes 2818064 | tf_op jit(solution)/shard_map/reduce_scatter | solution.py:176
  1723.8 406.7 %reduce-scatter.17.cloned.1.call-done = bf16[2048,768]{1,0:T(8,128)(2,1)} async-done(((bf16[2048,6144]{1,0:T(8,128)(2,1)}), bf16[2048,768]{1,0:T(8,128)(2,1)}) %reduce-scatter.17.cloned.1.call-update) | async-done | bytes 3145744 | tf_op jit(solution)/shard_map/reduce_scatter | solution.py:234
  2130.5 714.6 %reduce-scatter.31.cloned.1.call-done = bf16[2048,1376]{0,1:T(8,128)(2,1)} async-done(((bf16[2048,11008]{0,1:T(8,128)(2,1)}), bf16[2048,1376]{0,1:T(8,128)(2,1)}) %reduce-scatter.31.cloned.1.call-update) | async-done | bytes 5636112
  2845.2 26.5 reduce-scatter.23.cloned.1.call-done
  2871.8 38.5 %reduce-scatter.29.cloned.1.call-done = bf16[1376,256]{1,0:T(8,128)(2,1)} async-done(((bf16[5504,256]{1,0:T(8,128)(2,1)}), bf16[1376,256]{1,0:T(8,128)(2,1)}) %reduce-scatter.29.cloned.1.call-update) | async-done | bytes 704528 | tf_op jit(solution)/shard_map/reduce_scatter | solution.py:251
  2910.3 40.3 %reduce-scatter.19.cloned.1.call-done = bf16[512,768]{1,0:T(8,128)(2,1)} async-done(((bf16[2048,768]{1,0:T(8,128)(2,1)}), bf16[512,768]{1,0:T(8,128)(2,1)}) %reduce-scatter.19.cloned.1.call-update) | async-done | bytes 786448 | tf_op jit(solution)/shard_map/reduce_scatter | solution.py:242
  2950.7 56.5 %reduce-scatter.25.cloned.1.call-done = bf16[512,1376]{0,1:T(8,128)(2,1)} async-done(((bf16[2048,1376]{0,1:T(8,128)(2,1)}), bf16[512,1376]{0,1:T(8,128)(2,1)}) %reduce-scatter.25.cloned.1.call-update) | async-done | bytes 1409040 | tf_op jit(solution)/shard_map/reduce_scatter | solution.py:248
  3008.0 14.5 fusion.64
  3025.1 5.5 all-to-all-start.1
  3030.6 11.8 fusion.44
  3042.4 41.5 %all-reduce.1 = (f32[2048]{0:T(1024)S(1)}, f32[2048]{0:T(1024)S(1)}) all-reduce(f32[2048]{0:T(1024)S(1)} %get-tuple-element.35, f32[2048]{0:T(1024)S(1)} %get-tuple-element.33), channel_id=1, replica_groups=mesh['ctx'=8,'fsdp'=4] {'ctx','fsdp'}, use_global_device_ids=true, to_apply=%region_14.16 | all-reduce | flops 4096 | bytes 32768 | tf_op jit(solution)/shard_map/psum | solution.py:269
  3090.9 68.1 %all-gather.31.cloned.1.call-done = bf16[1376,2048]{1,0:T(8,128)(2,1)} async-done(((bf16[1376,256]{1,0:T(8,128)(2,1)}), bf16[1376,2048]{1,0:T(8,128)(2,1)}) %all-gather.31.cloned.1.call-update) | async-done | bytes 5636112 | tf_op jit(solution)/shard_map/all_gather | solution.py:265
  3159.0 8.5 convert_element_type.182
  3167.5 90.9 %all-gather.25.cloned.1.call-done = bf16[512,6144]{1,0:T(8,128)(2,1)} async-done(((bf16[512,768]{1,0:T(8,128)(2,1)}), bf16[512,6144]{1,0:T(8,128)(2,1)}) %all-gather.25.cloned.1.call-update) | async-done | bytes 6291472 | tf_op jit(solution)/shard_map/all_gather | solution.py:256
  3258.4 9.6 convert_element_type.176
  3268.0 151.2 %all-gather.29.cloned.1.call-done = bf16[512,11008]{0,1:T(8,128)(2,1)} async-done(((bf16[512,1376]{0,1:T(8,128)(2,1)}), bf16[512,11008]{0,1:T(8,128)(2,1)}) %all-gather.29.cloned.1.call-update) | async-done | bytes 11272208 | tf_op jit(solution)/shard_map/all_gather | solution.py:262
  3419.2 15.9 copy.80
  (177 shorter events, 77.1 us)
Async XLA Ops:
  7.2 8.5 copy-start
  7.2 8.4 copy-start.22
  7.2 166.0 %all-gather.13.cloned.1.call-start = ((), (), s32[]{:S(2)}) async-start(), calls=%async_computation.12 | async-start | bytes 31457280 | tf_op jit(solution)/shard_map/all_gather | solution.py:101
  15.5 9.0 copy-start.27
  15.5 9.7 copy-start.25
  17.2 21.7 all-to-all-start
  24.4 241.0 %all-gather.17.cloned.1.call-start = ((), (), s32[]{:S(2)}) async-start(), calls=%async_computation.14 | async-start | bytes 4718592 | tf_op jit(solution)/shard_map/all_gather | solution.py:118
  30.4 152.8 %copy-start.20 = (f32[4,1,512]{2,1,0:T(1,128)}, f32[4,1,512]{2,1,0:T(1,128)S(1)}, u32[]{:S(2)}) copy-start(f32[4,1,512]{2,1,0:T(1,128)S(1)} %convert_element_type.184) | copy-start | bytes 24580
  30.7 193.6 %copy-start.16 = (f32[128,128]{0,1:T(8,128)}, f32[128,128]{0,1:T(8,128)S(1)}, u32[]{:S(2)}) copy-start(f32[128,128]{0,1:T(8,128)S(1)} %pad_maximum_fusion.7) | copy-start | bytes 196612
  31.1 157.9 %copy-start.6 = (f32[128,2048]{1,0:T(8,128)}, f32[128,2048]{1,0:T(8,128)S(1)}, u32[]{:S(2)}) copy-start(f32[128,2048]{1,0:T(8,128)S(1)} %copy.82) | copy-start | bytes 3145732
  31.2 193.1 %copy-start.18 = (f32[128,128]{0,1:T(8,128)}, f32[128,128]{0,1:T(8,128)S(1)}, u32[]{:S(2)}) copy-start(f32[128,128]{0,1:T(8,128)S(1)} %pad_maximum_fusion.8) | copy-start | bytes 196612
  38.9 359.0 %copy-start.4 = (bf16[8,16,2048]{2,1,0:T(8,128)(2,1)}, bf16[8,16,2048]{2,1,0:T(8,128)(2,1)S(1)}, u32[]{:S(2)}) copy-start(bf16[8,16,2048]{2,1,0:T(8,128)(2,1)S(1)} %all-to-all-done) | copy-start | bytes 1572868
  39.2 144.0 %copy-start.23 = (f32[128]{0:T(128)}, f32[128]{0:T(128)S(1)}, u32[]{:S(2)}) copy-start(f32[128]{0:T(128)S(1)} %rsqrt.26) | copy-start | bytes 1540
  39.4 143.8 %copy-start.9 = (bf16[128,2048]{1,0:T(8,128)(2,1)}, bf16[128,2048]{1,0:T(8,128)(2,1)S(1)}, u32[]{:S(2)}) copy-start(bf16[128,2048]{1,0:T(8,128)(2,1)S(1)} %fusion.57) | copy-start | bytes 1572868
  191.9 148.0 %all-gather.15.cloned.1.call-start = ((), (), s32[]{:S(2)}) async-start(), calls=%async_computation.13 | async-start | bytes 4718592 | tf_op jit(solution)/shard_map/all_gather | solution.py:119
  194.1 203.8 %all-gather.19.cloned.1.call-start = ((), (), s32[]{:S(2)}) async-start(), calls=%async_computation.15 | async-start | bytes 10485760 | tf_op jit(solution)/shard_map/all_gather | solution.py:102
  198.1 469.7 %all-gather.21.cloned.1.call-start = ((), (), s32[]{:S(2)}) async-start(), calls=%async_computation.16 | async-start | bytes 56360960 | tf_op jit(solution)/shard_map/all_gather | solution.py:104
  210.5 7.8 copy-start.26
  210.5 599.6 %all-gather.23.cloned.1.call-start = ((), (), s32[]{:S(2)}) async-start(), calls=%async_computation.17 | async-start | bytes 28180480 | tf_op jit(solution)/shard_map/all_gather | solution.py:105
  218.2 830.1 %reduce-scatter.13.cloned.1.call-start = ((), (), s32[]{:S(2)}) async-start(), calls=%async_computation.18 | async-start | bytes 9437184 | tf_op jit(solution)/shard_map/reduce_scatter | solution.py:206
  223.8 116.0 %copy-start.12 = (pred[128,1024]{1,0:T(8,128)(4,1)}, pred[128,1024]{1,0:T(8,128)(4,1)S(1)}, u32[]{:S(2)}) copy-start(pred[128,1024]{1,0:T(8,128)(4,1)S(1)} %compare_and_fusion) | copy-start | bytes 393220
  224.5 51.9 %copy-start.15 = (bf16[128,16,128]{0,2,1:T(8,128)(2,1)}, bf16[128,16,128]{0,2,1:T(8,128)(2,1)S(1)}, u32[]{:S(2)}) copy-start(bf16[128,16,128]{0,2,1:T(8,128)(2,1)S(1)} %fusion.53) | copy-start | bytes 1572868
  276.4 3.4 copy-start.2
  347.8 54.8 %copy-start.11 = (bf16[16,128,128]{2,1,0:T(8,128)(2,1)}, bf16[16,128,128]{2,1,0:T(8,128)(2,1)S(1)}, u32[]{:S(2)}) copy-start(bf16[16,128,128]{2,1,0:T(8,128)(2,1)S(1)} %fusion.49) | copy-start | bytes 1572868
  667.8 142.4 %copy-start.14 = (bf16[1,128,2048]{2,1,0:T(8,128)(2,1)S(1)}, bf16[1,128,2048]{2,1,0:T(8,128)(2,1)}, u32[]{:S(2)}) copy-start(bf16[1,128,2048]{2,1,0:T(8,128)(2,1)} %param.13) | copy-start | bytes 1572868
  825.1 100.0 %copy-start.8 = (bf16[128,5504]{1,0:T(8,128)(2,1)}, bf16[128,5504]{1,0:T(8,128)(2,1)S(1)}, u32[]{:S(2)}) copy-start(bf16[128,5504]{1,0:T(8,128)(2,1)S(1)} %get-tuple-element.45) | copy-start | bytes 4227076
  899.2 301.2 %reduce-scatter.15.cloned.1.call-start = ((), (), s32[]{:S(2)}) async-start(), calls=%async_computation.19 | async-start | bytes 9437184 | tf_op jit(solution)/shard_map/reduce_scatter | solution.py:207
  918.2 434.8 %reduce-scatter.21.cloned.1.call-start = ((), (), s32[]{:S(2)}) async-start(), calls=%async_computation.23 | async-start | bytes 9437184 | tf_op jit(solution)/shard_map/reduce_scatter | solution.py:237
  925.1 798.7 %reduce-scatter.27.cloned.1.call-start = ((), (), s32[]{:S(2)}) async-start(), calls=%async_computation.28 | async-start | bytes 25362432 | tf_op jit(solution)/shard_map/reduce_scatter | solution.py:176
  937.4 112.4 %copy-start.19 = (f32[128,128]{0,1:T(8,128)S(1)}, f32[128,128]{0,1:T(8,128)}, u32[]{:S(2)}) copy-start(f32[128,128]{0,1:T(8,128)} %copy-done.18) | copy-start | bytes 196612
  937.5 1193.0 %reduce-scatter.17.cloned.1.call-start = ((), (), s32[]{:S(2)}) async-start(), calls=%async_computation.20 | async-start | bytes 28311552 | tf_op jit(solution)/shard_map/reduce_scatter | solution.py:234
  1049.9 26.8 copy-start.17
  1075.2 127.2 %copy-start.7 = (f32[128,2048]{1,0:T(8,128)S(1)}, f32[128,2048]{1,0:T(8,128)}, u32[]{:S(2)}) copy-start(f32[128,2048]{1,0:T(8,128)} %copy-done.6) | copy-start | bytes 3145732
  1218.6 1626.5 %reduce-scatter.31.cloned.1.call-start = ((), (), s32[]{:S(2)}) async-start(), calls=%async_computation.31 | async-start | bytes 50724864
  1239.7 1768.3 %copy-start.24 = (f32[128]{0:T(128)S(1)}, f32[128]{0:T(128)}, u32[]{:S(2)}) copy-start(f32[128]{0:T(128)} %copy-done.23) | copy-start | bytes 1540
  1239.7 1768.3 %copy-start.5 = (bf16[8,16,2048]{2,1,0:T(8,128)(2,1)S(1)}, bf16[8,16,2048]{2,1,0:T(8,128)(2,1)}, u32[]{:S(2)}) copy-start(bf16[8,16,2048]{2,1,0:T(8,128)(2,1)} %copy-done.4) | copy-start | bytes 1572868
  1239.7 1768.3 %copy-start.13 = (bf16[128,2048]{1,0:T(8,128)(2,1)S(1)}, bf16[128,2048]{1,0:T(8,128)(2,1)}, u32[]{:S(2)}) copy-start(bf16[128,2048]{1,0:T(8,128)(2,1)} %convert.25) | copy-start | bytes 1572868
  1239.7 1768.3 %copy-start.21 = (f32[4,1,512]{2,1,0:T(1,128)S(1)}, f32[4,1,512]{2,1,0:T(1,128)}, u32[]{:S(2)}) copy-start(f32[4,1,512]{2,1,0:T(1,128)} %copy-done.20) | copy-start | bytes 24580
  1239.7 1632.0 %reduce-scatter.23.cloned.1.call-start = ((), (), s32[]{:S(2)}) async-start(), calls=%async_computation.24 | async-start | bytes 1310720 | tf_op jit(solution)/shard_map/reduce_scatter | solution.py:245
  1353.1 1557.2 %reduce-scatter.29.cloned.1.call-start = ((), (), s32[]{:S(2)}) async-start(), calls=%async_computation.29 | async-start | bytes 3522560 | tf_op jit(solution)/shard_map/reduce_scatter | solution.py:251
  1723.8 1226.9 %reduce-scatter.19.cloned.1.call-start = ((), (), s32[]{:S(2)}) async-start(), calls=%async_computation.21 | async-start | bytes 3932160 | tf_op jit(solution)/shard_map/reduce_scatter | solution.py:242
  2130.5 876.7 %reduce-scatter.25.cloned.1.call-start = ((), (), s32[]{:S(2)}) async-start(), calls=%async_computation.26 | async-start | bytes 7045120 | tf_op jit(solution)/shard_map/reduce_scatter | solution.py:248
  2845.1 241.6 %all-gather.27.cloned.1.call-start = ((), (), s32[]{:S(2)}) async-start(), calls=%async_computation.25 | async-start | bytes 2359296 | tf_op jit(solution)/shard_map/all_gather | solution.py:259
  2871.7 287.2 %all-gather.31.cloned.1.call-start = ((), (), s32[]{:S(2)}) async-start(), calls=%async_computation.30 | async-start | bytes 6340608 | tf_op jit(solution)/shard_map/all_gather | solution.py:265
  2910.3 348.1 %all-gather.25.cloned.1.call-start = ((), (), s32[]{:S(2)}) async-start(), calls=%async_computation.22 | async-start | bytes 7077888 | tf_op jit(solution)/shard_map/all_gather | solution.py:256
  2950.6 468.6 %all-gather.29.cloned.1.call-start = ((), (), s32[]{:S(2)}) async-start(), calls=%async_computation.27 | async-start | bytes 12681216 | tf_op jit(solution)/shard_map/all_gather | solution.py:262
  3025.1 60.2 %all-to-all-start.1 = ((bf16[8,16,2048]{2,1,0:T(8,128)(2,1)}), bf16[8,16,2048]{2,1,0:T(8,128)(2,1)S(1)}, u32[]{:S(2)}, u32[]{:S(2)}) async-start(bf16[8,16,2048]{2,1,0:T(8,128)(2,1)} %bitcast.29), calls=%async_computation.3 | async-start | bytes 1048576 | tf_op jit(solution)/shard_map/all_to_all | solution.py:225
  3419.2 15.9 copy-start.1
  (2 other events, 3.0 us)
Sparse Core Ops, SparseCore 0:
  15.7 157.4 all-gather.12
  192.0 73.3 all-gather.16
  268.2 71.6 all-gather.14
  341.3 56.5 all-gather.18
  399.9 267.8 all-gather.20
  669.8 140.3 all-gather.22
  899.3 148.9 reduce-scatter.12
  1052.4 147.9 reduce-scatter.14
  1204.6 148.3 reduce-scatter.20
  1358.0 365.7 reduce-scatter.26
  1727.6 402.8 reduce-scatter.16
  2134.3 710.7 reduce-scatter.30
  2847.6 24.0 reduce-scatter.22
  2874.3 35.8 reduce-scatter.28
  2912.6 37.9 reduce-scatter.18
  2953.2 53.9 reduce-scatter.24
  3009.1 55.9 all-gather.26
  3067.1 91.8 all-gather.30
  3161.2 97.2 all-gather.24
  3260.5 158.7 all-gather.28
where the time goes:
time: 3450 us; the launch traced here: 3440 us
  waiting for transfers between devices  2980 us (86%)
  matrix products  240 us (7%)
  other arithmetic  78.6 us (2%)
  local copies, waits for them, and re-layouts  65.3 us (2%)
  blocking collectives  51.9 us (2%)
    unnamed x21, waiting for transfers between devices  715 us
    reduce_scatter x1, waiting for transfers between devices, shards(): lax.psum_scatter(grad_qkv.astype(jnp.bfloat16), 'ctx', scatter_dimension=...  407 us
    reduce_scatter x1, waiting for transfers between devices, shards(): lax.psum_scatter(grad_down.astype(jnp.bfloat16), 'ctx', scatter_dimension...  371 us
    all_gather x1, waiting for transfers between devices, shards(): lax.all_gather(w_gate_up.astype(jnp.bfloat16), 'fsdp', axis=0, tiled=True)  265 us
    all_gather x1, waiting for transfers between devices, shards(): lax.all_gather(row_gate_up.astype(jnp.bfloat16), 'ctx', axis=1, tiled=True)  151 us
    all_gather x1, waiting for transfers between devices, shards(): lax.all_gather(w_qkv.astype(jnp.bfloat16), 'fsdp', axis=0, tiled=True)  134 us
    all_gather x1, waiting for transfers between devices, shards(): lax.all_gather(w_down.astype(jnp.bfloat16), 'fsdp', axis=0, tiled=True)  119 us
    reduce_scatter x1, waiting for transfers between devices, shards(): lax.psum_scatter(value_term, 'ctx', scatter_dimension=0, tiled=True)  115 us
  transfers between devices with their start and end apart: 22, of which 20 were waited for; matrix products, arithmetic and copies ran while one was open for 7% of the time, Pallas kernels for 0%

commit v1 on v0

v1 whole, which is shorter than its diff:
```python
import math

import jax
import jax.numpy as jnp
from jax import lax
from jax.sharding import PartitionSpec as P

H = 16
HD = 128

epsilon = 1e-06
rope_base = 10000.0
masked_score = -1e30
f32 = jnp.float32
bf16 = jnp.bfloat16


def rope_tables(within):
    freq_index = jnp.arange(HD // 2, dtype=f32)
    inverse = rope_base ** (-2.0 * freq_index / HD)
    angles = within.astype(f32)[:, None] * inverse[None, :]
    cosine_table = jnp.concatenate([jnp.cos(angles), jnp.cos(angles)], -1)
    sine_table = jnp.concatenate([jnp.sin(angles), jnp.sin(angles)], -1)
    return (cosine_table, sine_table)


def rotate(values, cosine_table, sine_table):
    half_size = values.shape[-1] // 2
    turned = jnp.concatenate([-values[..., half_size:], values[..., :half_size]], -1)
    return values * cosine_table[:, None, :] + turned * sine_table[:, None, :]


def unrotate(grads, cosine_table, sine_table):
    half_size = grads.shape[-1] // 2
    scaled = grads * sine_table[:, None, :]
    turned = jnp.concatenate([-scaled[..., half_size:], scaled[..., :half_size]], -1)
    return grads * cosine_table[:, None, :] - turned


def rms_scale(values):
    return lax.rsqrt(jnp.mean(values * values, -1, keepdims=True) + epsilon)


def norm_back(grad_norm, values, scale_rows, gain_float):
    scaled = grad_norm * gain_float[None, :]
    cubed = scale_rows * scale_rows * scale_rows
    return scale_rows * scaled - values * cubed * jnp.mean(scaled * values, -1, keepdims=True)


def dot(a, b, dims):
    return lax.dot_general(a, b, (dims, ((), ())), preferred_element_type=f32)


NN = ((1,), (0,))
NT = ((1,), (1,))
TN = ((0,), (0,))


def shards(
    tokens, cotangent, lengths, deal, norm1_gain, w_qkv, w_out, norm2_gain, w_gate_up, w_down
):
    n_ctx = lax.axis_size("ctx")
    n_fsdp = lax.axis_size("fsdp")
    me = lax.axis_index("ctx")
    mine = lax.axis_index("fsdp")
    rows = tokens.shape[1]
    width = tokens.shape[2]
    piece = rows // n_ctx
    all_rows = rows * n_ctx
    pieces = all_rows // piece
    heads = H // n_ctx
    hw = heads * HD
    kr = w_qkv.shape[0]
    ff = w_gate_up.shape[1] // 2
    ffs = ff // n_ctx
    ff_rows = w_down.shape[0]
    ratio = n_ctx // n_fsdp

    x_own = tokens[0]
    x_all = lax.all_gather(x_own, "ctx", axis=0, tiled=True)

    qkv_own = lax.dynamic_slice(w_qkv.reshape(kr, 3, width), (0, 0, me * hw), (kr, 3, hw))
    wq = lax.all_gather(qkv_own.reshape(kr, 3 * hw).astype(bf16), "fsdp", axis=0, tiled=True)
    gains = lax.all_gather(
        jnp.stack([norm1_gain, norm2_gain]).astype(bf16), "fsdp", axis=1, tiled=True
    )
    gain_one = gains[0].astype(f32)
    gain_two = gains[1].astype(f32)
    wo = lax.all_gather(w_out.astype(bf16), "fsdp", axis=0, tiled=True)
    wg_own = jnp.concatenate(
        [
            lax.dynamic_slice(w_gate_up, (0, me * ffs), (kr, ffs)),
            lax.dynamic_slice(w_gate_up, (0, ff + me * ffs), (kr, ffs)),
        ],
        -1,
    ).astype(bf16)
    wgu = lax.all_gather(wg_own, "fsdp", axis=0, tiled=True)
    down_own = lax.dynamic_slice(w_down, ((me % ratio) * ffs, 0), (ffs, width)).astype(bf16)
    wd = lax.psum(jnp.where(mine == me // ratio, down_own, jnp.zeros_like(down_own)), "fsdp")
    g_all = lax.all_gather(cotangent[0], "ctx", axis=0, tiled=True)

    deal_table = deal[0]
    device_index = jnp.arange(n_ctx, dtype=jnp.int32)
    marks = (deal_table[:, :, None] == device_index[None, None, :]).astype(jnp.int32)
    source_piece = jnp.sum(marks * device_index[None, :, None], 1)
    dealt_from = (device_index[None, :] * n_ctx + source_piece.T).reshape(pieces)
    given_from = (deal_table * n_ctx + device_index[:, None]).reshape(pieces)
    own_dealt = lax.dynamic_slice(dealt_from, (me * n_ctx,), (n_ctx,))
    own_given = lax.dynamic_slice(given_from, (me * n_ctx,), (n_ctx,))
    places = jnp.arange(all_rows, dtype=jnp.int32)
    doc_lengths = lengths[0]
    ends = jnp.cumsum(doc_lengths)
    starts = ends - doc_lengths
    docs = jnp.sum((places[:, None] >= ends[None, :]).astype(jnp.int32), -1)
    doc_index = jnp.arange(doc_lengths.shape[0], dtype=jnp.int32)
    firsts = jnp.sum(jnp.where(docs[:, None] == doc_index[None, :], starts[None, :], 0), -1)
    within = places - firsts
    allowed = (docs[None, :] == docs[:, None]) & (places[None, :] <= places[:, None])
    cosine_table, sine_table = rope_tables(within)
    factor = 1.0 / math.sqrt(HD)

    x_float = x_all.astype(f32)
    normed_one = (x_float * rms_scale(x_float) * gain_one[None, :]).astype(bf16)
    projected = dot(normed_one, wq, NN)
    queries = rotate(projected[:, :hw].reshape(all_rows, heads, HD), cosine_table, sine_table)
    queries = queries.astype(bf16)
    keys = rotate(projected[:, hw : 2 * hw].reshape(all_rows, heads, HD), cosine_table, sine_table)
    keys = keys.astype(bf16)
    values = projected[:, 2 * hw :].astype(bf16).reshape(all_rows, heads, HD)
    logits = jnp.einsum("qhd,khd->hqk", queries, keys, preferred_element_type=f32)
    scaled = jnp.where(allowed[None], logits * factor, masked_score)
    row_top = jnp.max(scaled, -1, keepdims=True)
    raised = jnp.exp(scaled - row_top)
    row_total = jnp.sum(raised, -1, keepdims=True)
    probs = raised / row_total
    probs_low = probs.astype(bf16)
    mixed = jnp.einsum("hqk,khd->qhd", probs_low, values, preferred_element_type=f32)
    mixed = mixed.astype(bf16).reshape(pieces, piece, hw)
    mixed_dealt = jnp.take(mixed, dealt_from, axis=0)
    mixed_own = lax.all_to_all(
        mixed_dealt.reshape(n_ctx, rows, hw), "ctx", split_axis=0, concat_axis=2, tiled=True
    ).reshape(rows, width)
    mixed_dealt = mixed_dealt.reshape(all_rows, hw)

    x_dealt = jnp.take(x_all.reshape(pieces, piece, width), own_dealt, axis=0)
    hidden = x_dealt.reshape(rows, width).astype(f32) + dot(mixed_own, wo, NN)
    scale_two = rms_scale(hidden)
    normed_two = (hidden * scale_two * gain_two[None, :]).astype(bf16)
    n2_all = lax.all_gather(normed_two, "ctx", axis=0, tiled=True)

    both = dot(n2_all, wgu, NN)
    gate = both[:, :ffs]
    up = both[:, ffs:]
    sigma = jax.nn.sigmoid(gate)
    gate_act = gate * sigma
    activated = (gate_act * up).astype(bf16)
    down_part = dot(activated, wd, NN).astype(bf16)
    down_own_rows = lax.psum_scatter(down_part, "ctx", scatter_dimension=0, tiled=True)
    block_out = (hidden + down_own_rows.astype(f32)).astype(bf16)[None]

    d_act = dot(g_all, wd, NT)
    d_both = jnp.concatenate(
        [d_act * up * sigma * (1.0 + gate * (1.0 - sigma)), d_act * gate_act], -1
    ).astype(bf16)
    d_two_part = dot(d_both, wgu, NT).astype(bf16)
    d_two = lax.psum_scatter(d_two_part, "ctx", scatter_dimension=0, tiled=True).astype(f32)
    grad_down = dot(activated, g_all, TN).astype(bf16)
    grad_gate_up = dot(n2_all, d_both, TN).astype(bf16)
    row_gate_up = lax.psum_scatter(grad_gate_up, "fsdp", scatter_dimension=0, tiled=True)
    all_gate_up = lax.all_gather(row_gate_up, "ctx", axis=0)
    final_gate_up = (
        all_gate_up.reshape(n_ctx, kr, 2, ffs).transpose(1, 2, 0, 3).reshape(kr, 2 * ff).astype(f32)
    )

    grad_norm2 = jnp.sum(d_two * hidden * scale_two, 0)
    d_hidden = cotangent[0].astype(f32) + norm_back(d_two, hidden, scale_two, gain_two)
    d_branch = d_hidden.astype(bf16)
    db_all = lax.all_gather(d_branch, "ctx", axis=0, tiled=True)

    grad_out = dot(mixed_dealt, db_all, TN).astype(bf16)
    wo_own = lax.dynamic_slice(wo, (me * hw, 0), (hw, width))
    d_mixed = dot(db_all, wo_own, NT).astype(bf16)
    d_mixed = jnp.take(d_mixed.reshape(pieces, piece, hw), given_from, axis=0)
    d_mixed = d_mixed.reshape(all_rows, heads, HD)
    d_probs = jnp.einsum("qhd,khd->hqk", d_mixed, values, preferred_element_type=f32)
    row_inner = jnp.sum(probs * d_probs, -1, keepdims=True)
    d_scores = (probs * (d_probs - row_inner) * factor).astype(bf16)
    d_queries = jnp.einsum("hqk,khd->qhd", d_scores, keys, preferred_element_type=f32)
    d_keys = jnp.einsum("hqk,qhd->khd", d_scores, queries, preferred_element_type=f32)
    d_values = jnp.einsum("hqk,qhd->khd", probs_low, d_mixed, preferred_element_type=f32)
    d_proj = jnp.concatenate(
        [
            unrotate(d_queries, cosine_table, sine_table).reshape(all_rows, hw),
            unrotate(d_keys, cosine_table, sine_table).reshape(all_rows, hw),
            d_values.reshape(all_rows, hw),
        ],
        -1,
    ).astype(bf16)
    d_one_part = dot(d_proj, wq, NT).astype(bf16)
    d_one = lax.psum_scatter(d_one_part, "ctx", scatter_dimension=0, tiled=True).astype(f32)
    grad_qkv = dot(normed_one, d_proj, TN).astype(bf16)
    row_qkv = lax.psum_scatter(grad_qkv, "fsdp", scatter_dimension=0, tiled=True)
    all_qkv = lax.all_gather(row_qkv, "ctx", axis=0)
    final_qkv = (
        all_qkv.reshape(n_ctx, kr, 3, hw).transpose(1, 2, 0, 3).reshape(kr, 3 * width).astype(f32)
    )

    own_float = x_own.astype(f32)
    scale_one = rms_scale(own_float)
    grad_norm1 = jnp.sum(d_one * own_float * scale_one, 0)
    dh_own = jnp.take(db_all.reshape(pieces, piece, width), own_given, axis=0)
    dh_own = dh_own.reshape(rows, width).astype(f32)
    grad_tokens = (dh_own + norm_back(d_one, own_float, scale_one, gain_one)).astype(bf16)[None]

    grad_rows = jnp.concatenate([grad_down, grad_out], 0)
    col_rows = lax.psum_scatter(grad_rows, "fsdp", scatter_dimension=1, tiled=True)
    all_cols = lax.all_gather(col_rows, "ctx", axis=0)
    owner_rows = all_cols.reshape(n_fsdp, ratio * (ffs + hw), width // n_fsdp)
    swapped = lax.all_to_all(owner_rows, "fsdp", split_axis=0, concat_axis=2, tiled=True)
    swapped = swapped.reshape(ratio, ffs + hw, width)
    final_down = swapped[:, :ffs].reshape(ff_rows, width).astype(f32)
    final_out = swapped[:, ffs:].reshape(ratio * hw, width).astype(f32)

    sums = lax.psum(jnp.stack([grad_norm1, grad_norm2]), ("ctx", "fsdp"))
    gain_rows = norm1_gain.shape[0]
    final_norms = lax.dynamic_slice_in_dim(sums, mine * gain_rows, gain_rows, 1)
    return (
        block_out,
        grad_tokens,
        final_norms[0],
        final_qkv,
        final_out,
        final_norms[1],
        final_gate_up,
        final_down,
    )


def solution(mesh):
    in_specs = (
        P("fsdp", "ctx", None),
        P("fsdp", "ctx", None),
        P("fsdp", None),
        P("fsdp", None, None),
        P("fsdp"),
        P("fsdp", None),
        P("fsdp", None),
        P("fsdp"),
        P("fsdp", None),
        P("fsdp", None),
    )
    out_specs = (
        P("fsdp", "ctx", None),
        P("fsdp", "ctx", None),
        P("fsdp"),
        P("fsdp", None),
        P("fsdp", None),
        P("fsdp"),
        P("fsdp", None),
        P("fsdp", None),
    )
    return jax.shard_map(shards, mesh=mesh, in_specs=in_specs, out_specs=out_specs, check_vma=False)
```

time: 3450 us -> 1460 us (0.42)
  waiting for transfers between devices: 2980 us -> 976 us
  local copies, waits for them, and re-layouts: 65.3 us -> 199 us
  matrix products: 240 us -> 140 us
    reduce_scatter x9 -> x6, waiting for transfers between devices: 1280 us -> 317 us  [the longest x1 90.7 us: shards(): lax.psum_scatter(down_part, 'ctx', scatter_dimension=0, tiled=True)]
    unnamed x21 -> x17, waiting for transfers between devices: 715 us -> 2.1 us
    all_gather x10, waiting for transfers between devices: 977 us -> 592 us  [the longest x1 119 us: shards(): all_cols = lax.all_gather(col_rows, 'ctx', axis=0)]
    dot_general x18 -> x17, matrix products: 240 us -> 132 us  [the longest x12 88.6 us: dot(): return lax.dot_general(a, b, (dims, ((), ())), preferred_element_type=f32)]
    unnamed x59 -> x33, local copies, waits for them, and re-layouts: 22.4 us -> 94.7 us
    psum x0 -> x1, waiting for transfers between devices: none -> 53.1 us  [shards(): lax.psum(jnp.where(mine == me // ratio, down_own, jnp.zeros_like(down_own...]
    convert_element_type x0 -> x5, local copies, waits for them, and re-layouts: none -> 51.6 us  [the longest x2 25.9 us: shards(): all_qkv.reshape(n_ctx, kr, 3, hw).transpose(1, 2, 0, 3)]
    convert_element_type x16 -> x8, other arithmetic: 60.3 us -> 25 us  [the longest x1 6.62 us: shards(): all_gate_up.reshape(n_ctx, kr, 2, ffs).transpose(1, 2, 0, 3)]
  transfers between devices with their start and end apart: 22 -> 19, of which waited for: 20 -> 17; matrix products, arithmetic and copies ran while one was open for 7% -> 21% of each run, Pallas kernels for 0% -> 0%
where the time goes in v1:
time: 1460 us; the launch traced here: 1450 us
  waiting for transfers between devices  976 us (67%)
  local copies, waits for them, and re-layouts  199 us (14%)
  matrix products  140 us (10%)
  blocking collectives  55.5 us (4%)
  other arithmetic  49.7 us (3%)
  between operations  14.9 us (1%)
    all_gather x1, waiting for transfers between devices, shards(): all_cols = lax.all_gather(col_rows, 'ctx', axis=0)  119 us
    all_gather x1, waiting for transfers between devices, shards(): all_gate_up = lax.all_gather(row_gate_up, 'ctx', axis=0)  109 us
    unnamed x33, local copies, waits for them, and re-layouts  94.7 us
    reduce_scatter x1, waiting for transfers between devices, shards(): lax.psum_scatter(down_part, 'ctx', scatter_dimension=0, tiled=True)  90.7 us
    dot_general x12, matrix products, dot(): return lax.dot_general(a, b, (dims, ((), ())), preferred_element_type=f32)  88.6 us
    reduce_scatter x1, waiting for transfers between devices, shards(): lax.psum_scatter(d_one_part, 'ctx', scatter_dimension=0, tiled=True)  81.3 us
    reduce_scatter x1, waiting for transfers between devices, shards(): lax.psum_scatter(d_two_part, 'ctx', scatter_dimension=0, tiled=True)  78.2 us
    all_gather x1, waiting for transfers between devices, shards(): n2_all = lax.all_gather(normed_two, 'ctx', axis=0, tiled=True)  76 us
  transfers between devices with their start and end apart: 19, of which 17 were waited for; matrix products, arithmetic and copies ran while one was open for 21% of the time, Pallas kernels for 0%

profile of v1, /device:TPU:0, one launch (start us, length us, event | category | flops | bytes accessed | tf_op | source)
XLA Modules:
  0.0 1448.8 jit_solution(1712624644535826120)
XLA Ops:
  8.0 10.0 copy.82
  29.1 6.1 all_gather.43
  37.1 49.2 %all-gather.26.cloned.1.call-done = bf16[1,1024,2048]{2,1,0:T(8,128)(2,1)} async-done(((bf16[1,128,2048]{2,1,0:T(8,128)(2,1)}), bf16[1,1024,2048]{2,1,0:T(8,128)(2,1)}) %all-gather.26.cloned.1.call-update) | async-done | bytes 4194320 | tf_op jit(solution)/shard_map/all_gather | solution.py:80
  89.3 25.9 %all-gather.16.cloned.1.call-done = bf16[2048,768]{0,1:T(8,128)(2,1)} async-done(((bf16[512,768]{0,1:T(8,128)(2,1)}), bf16[2048,768]{0,1:T(8,128)(2,1)}) %all-gather.16.cloned.1.call-update) | async-done | bytes 3145744 | tf_op jit(solution)/shard_map/all_gather | solution.py:83
  115.2 6.6 fusion.55
  124.1 8.1 fusion.96
  138.7 5.5 all-to-all-start
  148.2 10.9 all-to-all-done
  159.4 16.3 %all-gather.18.cloned.1.call-done = bf16[2048,2048]{1,0:T(8,128)(2,1)} async-done(((bf16[512,2048]{1,0:T(8,128)(2,1)}), bf16[2048,2048]{1,0:T(8,128)(2,1)}) %all-gather.18.cloned.1.call-update) | async-done | bytes 8388624 | tf_op jit(solution)/shard_map/all_gather | solution.py:89
  175.7 4.8 multiply_reduce_fusion.1
  181.5 5.1 fusion.26
  187.5 33.6 %all-gather.22.cloned.1.call-done = bf16[2048,1376]{1,0:T(8,128)(2,1)} async-done(((bf16[512,1376]{1,0:T(8,128)(2,1)}), bf16[2048,1376]{1,0:T(8,128)(2,1)}) %all-gather.22.cloned.1.call-update) | async-done | bytes 5636112 | tf_op jit(solution)/shard_map/all_gather | solution.py:97
  221.1 76.0 %all-gather.20.cloned.1.call-done = bf16[1024,2048]{1,0:T(8,128)(2,1)} async-done(((bf16[128,2048]{1,0:T(8,128)(2,1)}), bf16[1024,2048]{1,0:T(8,128)(2,1)}) %all-gather.20.cloned.1.call-update) | async-done | bytes 4194320 | tf_op jit(solution)/shard_map/all_gather | solution.py:149
  297.1 11.1 fusion.99
  308.2 53.1 %all-reduce.2.cloned.1.call-done = bf16[688,2048]{1,0:T(8,128)(2,1)} async-done(((bf16[688,2048]{1,0:T(8,128)(2,1)}), bf16[688,2048]{1,0:T(8,128)(2,1)}) %all-reduce.2.cloned.1.call-update) | async-done | bytes 2818064 | tf_op jit(solution)/shard_map/psum | solution.py:99
  361.3 75.9 %all-gather.28.cloned.1.call-done = bf16[1,1024,2048]{2,1,0:T(8,128)(2,1)} async-done(((bf16[1,128,2048]{2,1,0:T(8,128)(2,1)}), bf16[1,1024,2048]{2,1,0:T(8,128)(2,1)}) %all-gather.28.cloned.1.call-update) | async-done | bytes 4194320 | tf_op jit(solution)/shard_map/all_gather | solution.py:100
  437.2 9.9 fusion.29
  448.6 11.0 convolution_convert_fusion.1
  460.1 7.7 convolution_convert_fusion.2
  467.9 78.2 %reduce-scatter.9.cloned.1.call-done = bf16[128,2048]{1,0:T(8,128)(2,1)} async-done(((bf16[1024,2048]{1,0:T(8,128)(2,1)}), bf16[128,2048]{1,0:T(8,128)(2,1)}) %reduce-scatter.9.cloned.1.call-update) | async-done | bytes 524304 | tf_op jit(solution)/shard_map/reduce_scatter | solution.py:166
  547.5 90.7 %reduce-scatter.7.cloned.1.call-done = bf16[128,2048]{1,0:T(8,128)(2,1)} async-done(((bf16[1024,2048]{1,0:T(8,128)(2,1)}), bf16[128,2048]{1,0:T(8,128)(2,1)}) %reduce-scatter.7.cloned.1.call-update) | async-done | bytes 524304 | tf_op jit(solution)/shard_map/reduce_scatter | solution.py:158
  640.8 7.3 fusion.23
  648.1 66.0 %all-gather.24.cloned.1.call-done = bf16[1024,2048]{1,0:T(8,128)(2,1)} async-done(((bf16[128,2048]{1,0:T(8,128)(2,1)}), bf16[1024,2048]{1,0:T(8,128)(2,1)}) %all-gather.24.cloned.1.call-update) | async-done | bytes 4194320 | tf_op jit(solution)/shard_map/all_gather | solution.py:178
  720.4 10.2 convolution_convert_fusion
  740.9 13.6 fusion.39
  754.4 15.4 %broadcast_multiply_fusion.1 = (f32[1024,2,128]{0,2,1:T(8,128)}, f32[1024,2,128]{0,2,1:T(8,128)S(1)}, f32[1024,2,128]{0,2,1:T(8,128)}) fusion(f32[1024,128]{0,1:T(8,128)S(1)} %get-tuple-element.91, f32[1024,2,128]{0,2,1:T(8,128)} %fusion.39, bf16[1024,2,128]{0,2,1:T(8,128)(2,1)S(1)} %copy-done.6, f32[2,1024,1024]{1,2,0:T(8,128)} %fusion.100, ...), kind=kOutput, calls=%fused_computation.117 | convolution fusion | flops 552078336 | bytes 22028288 | tf_op jit(solution)/shard_map/hqk,khd->qhd/dot_general | solution.py:188
  772.6 6.0 fusion.45
  778.6 5.5 convolution_convert_fusion.4
  785.2 7.0 convolution_convert_fusion.3
  792.3 26.0 %reduce-scatter.17.cloned.1.call-done = bf16[512,1376]{0,1:T(8,128)(2,1)} async-done(((bf16[2048,1376]{0,1:T(8,128)(2,1)}), bf16[512,1376]{0,1:T(8,128)(2,1)}) %reduce-scatter.17.cloned.1.call-update) | async-done | bytes 1409040 | tf_op jit(solution)/shard_map/reduce_scatter | solution.py:169
  818.3 41.2 %reduce-scatter.13.cloned.1.call-done = bf16[512,768]{1,0:T(8,128)(2,1)} async-done(((bf16[2048,768]{1,0:T(8,128)(2,1)}), bf16[512,768]{1,0:T(8,128)(2,1)}) %reduce-scatter.13.cloned.1.call-update) | async-done | bytes 786448 | tf_op jit(solution)/shard_map/reduce_scatter | solution.py:202
  859.5 118.9 %all-gather.32.cloned.1.call-done = bf16[7552,512]{1,0:T(8,128)(2,1)} async-done(((bf16[944,512]{1,0:T(8,128)(2,1)}), bf16[7552,512]{1,0:T(8,128)(2,1)}) %all-gather.32.cloned.1.call-update) | async-done | bytes 7733264 | tf_op jit(solution)/shard_map/all_gather | solution.py:217
  978.4 5.6 all-to-all-start.1
  987.2 81.3 %reduce-scatter.11.cloned.1.call-done = bf16[128,2048]{1,0:T(8,128)(2,1)} async-done(((bf16[1024,2048]{1,0:T(8,128)(2,1)}), bf16[128,2048]{1,0:T(8,128)(2,1)}) %reduce-scatter.11.cloned.1.call-update) | async-done | bytes 524304 | tf_op jit(solution)/shard_map/reduce_scatter | solution.py:200
  1069.9 49.5 %psum.15 = f32[2,2048]{1,0:T(2,128)S(1)} all-reduce(f32[2,2048]{1,0:T(2,128)S(1)} %pad_maximum_fusion.10), channel_id=1, replica_groups=mesh['ctx'=8,'fsdp'=4] {'ctx','fsdp'}, use_global_device_ids=true, to_apply=%region_18.21 | all-reduce | flops 4096 | bytes 32768 | tf_op jit(solution)/shard_map/psum | solution.py:224
  1122.4 109.0 %all-gather.34.cloned.1.call-done = bf16[4096,1376]{0,1:T(8,128)(2,1)} async-done(((bf16[512,1376]{0,1:T(8,128)(2,1)}), bf16[4096,1376]{0,1:T(8,128)(2,1)}) %all-gather.34.cloned.1.call-update) | async-done | bytes 11272208 | tf_op jit(solution)/shard_map/all_gather | solution.py:170
  1231.5 6.6 convert_element_type.219
  1238.1 25.6 %copy.108 = f32[172,8,8,512]{3,2,1,0:T(8,128)} copy(f32[172,8,8,512]{3,1,2,0:T(8,128)S(1)} %bitcast.137) | data formatting | bytes 45088768
  1263.7 23.2 %copy.97 = f32[8,512,2,688]{1,3,0,2:T(8,128)} copy(f32[8,512,2,688]{1,0,3,2:T(8,128)} %bitcast.138) | data formatting | bytes 45088768 | tf_op jit(solution)/shard_map/convert_element_type | solution.py:172
  1286.9 22.7 %copy.99 = f32[512,11008]{1,0:T(8,128)} copy(f32[512,11008]{0,1:T(8,128)} %bitcast.139) | data formatting | bytes 45088768
  1309.6 21.3 %all-gather.30.cloned.1.call-done = bf16[4096,768]{1,0:T(8,128)(2,1)} async-done(((bf16[512,768]{1,0:T(8,128)(2,1)}), bf16[4096,768]{1,0:T(8,128)(2,1)}) %all-gather.30.cloned.1.call-update) | async-done | bytes 6291472 | tf_op jit(solution)/shard_map/all_gather | solution.py:203
  1331.0 9.6 copy.94
  1340.5 21.7 %copy.107 = f32[96,8,8,512]{3,2,1,0:T(8,128)} copy(f32[96,8,8,512]{3,1,2,0:T(8,128)} %bitcast.140) | data formatting | bytes 25165824
  1362.3 16.4 %copy.95 = f32[512,3,8,256]{0,3,2,1:T(8,128)} copy(f32[512,3,8,256]{0,2,3,1:T(8,128)} %bitcast.141) | data formatting | bytes 25165824 | tf_op jit(solution)/shard_map/convert_element_type | solution.py:205
  1378.6 12.6 copy.98
  1391.2 22.7 %copy.96 = bf16[1,1888,4,512]{3,2,1,0:T(4,128)(2,1)} copy(bf16[1,1888,4,512]{3,1,2,0:T(8,128)(2,1)} %bitcast.46) | data formatting | bytes 15466496 | tf_op jit(solution)/shard_map/all_to_all | solution.py:219
  1413.9 15.9 %reshape.252 = bf16[2,944,2048]{2,1,0:T(8,128)(2,1)} reshape(bf16[1,1888,4,512]{3,2,1,0:T(4,128)(2,1)} %copy.96) | data formatting | bytes 15466496 | tf_op jit(solution)/shard_map/reshape | solution.py:220
  1435.5 6.3 bitcast_convert_fusion
  (146 shorter events, 71.1 us)
Async XLA Ops:
  7.2 79.1 %all-gather.26.cloned.1.call-start = ((), (), s32[]{:S(2)}) async-start(), calls=%async_computation.20 | async-start | bytes 4718592 | tf_op jit(solution)/shard_map/all_gather | solution.py:80
  7.9 107.3 %all-gather.16.cloned.1.call-start = ((), (), s32[]{:S(2)}) async-start(), calls=%async_computation.8 | async-start | bytes 3932160 | tf_op jit(solution)/shard_map/all_gather | solution.py:83
  20.0 155.7 %all-gather.18.cloned.1.call-start = ((), (), s32[]{:S(2)}) async-start(), calls=%async_computation.9 | async-start | bytes 10485760 | tf_op jit(solution)/shard_map/all_gather | solution.py:89
  24.2 4.2 copy-start.9
  24.2 4.3 copy-start.10
  24.2 4.3 copy-start.11
  24.2 4.5 copy-start.8
  24.2 196.9 %all-gather.22.cloned.1.call-start = ((), (), s32[]{:S(2)}) async-start(), calls=%async_computation.11 | async-start | bytes 7208960 | tf_op jit(solution)/shard_map/all_gather | solution.py:97
  138.7 20.4 %all-to-all-start = ((bf16[8,128,256]{2,1,0:T(8,128)(2,1)}), bf16[8,128,256]{2,1,0:T(8,128)(2,1)S(1)}, u32[]{:S(2)}, u32[]{:S(2)}) async-start(bf16[8,128,256]{2,1,0:T(8,128)(2,1)} %bitcast.17), calls=%async_computation | async-start | bytes 1048576 | tf_op jit(solution)/shard_map/all_to_all | solution.py:140
  144.2 152.9 %all-gather.20.cloned.1.call-start = ((), (), s32[]{:S(2)}) async-start(), calls=%async_computation.10 | async-start | bytes 4718592 | tf_op jit(solution)/shard_map/all_gather | solution.py:149
  181.5 179.9 %all-reduce.2.cloned.1.call-start = ((), (), s32[]{:S(2)}) async-start(), calls=%async_computation.12 | async-start | bytes 5636096 | tf_op jit(solution)/shard_map/psum | solution.py:99
  186.7 250.5 %all-gather.28.cloned.1.call-start = ((), (), s32[]{:S(2)}) async-start(), calls=%async_computation.21 | async-start | bytes 4718592 | tf_op jit(solution)/shard_map/all_gather | solution.py:100
  187.4 358.7 %reduce-scatter.9.cloned.1.call-start = ((), (), s32[]{:S(2)}) async-start(), calls=%async_computation.14 | async-start | bytes 4718592 | tf_op jit(solution)/shard_map/reduce_scatter | solution.py:166
  447.1 1.1 copy-start.12
  447.1 1.5 copy-start.13
  459.6 178.6 %reduce-scatter.7.cloned.1.call-start = ((), (), s32[]{:S(2)}) async-start(), calls=%async_computation.13 | async-start | bytes 4718592 | tf_op jit(solution)/shard_map/reduce_scatter | solution.py:158
  467.8 170.4 %copy-start.3 = (bf16[1,128,2048]{2,1,0:T(8,128)(2,1)S(1)}, bf16[1,128,2048]{2,1,0:T(8,128)(2,1)}, u32[]{:S(2)}) copy-start(bf16[1,128,2048]{2,1,0:T(8,128)(2,1)} %param.15) | copy-start | bytes 1572868
  467.8 246.3 %all-gather.24.cloned.1.call-start = ((), (), s32[]{:S(2)}) async-start(), calls=%async_computation.15 | async-start | bytes 4718592 | tf_op jit(solution)/shard_map/all_gather | solution.py:178
  640.8 143.5 %reduce-scatter.15.cloned.1.call-start = ((), (), s32[]{:S(2)}) async-start(), calls=%async_computation.18 | async-start | bytes 4833280 | tf_op jit(solution)/shard_map/reduce_scatter | solution.py:216
  714.1 3.8 copy-start.2
  720.4 97.9 %reduce-scatter.17.cloned.1.call-start = ((), (), s32[]{:S(2)}) async-start(), calls=%async_computation.19 | async-start | bytes 7045120 | tf_op jit(solution)/shard_map/reduce_scatter | solution.py:169
  730.6 128.9 %reduce-scatter.13.cloned.1.call-start = ((), (), s32[]{:S(2)}) async-start(), calls=%async_computation.17 | async-start | bytes 3932160 | tf_op jit(solution)/shard_map/reduce_scatter | solution.py:202
  736.1 4.7 copy-start.7
  740.8 13.6 copy-start.6
  769.8 1.8 copy-start.4
  769.8 2.1 copy-start.5
  772.5 6.1 copy-start.1
  784.2 194.2 %all-gather.32.cloned.1.call-start = ((), (), s32[]{:S(2)}) async-start(), calls=%async_computation.23 | async-start | bytes 8699904 | tf_op jit(solution)/shard_map/all_gather | solution.py:217
  784.7 283.8 %reduce-scatter.11.cloned.1.call-start = ((), (), s32[]{:S(2)}) async-start(), calls=%async_computation.16 | async-start | bytes 4718592 | tf_op jit(solution)/shard_map/reduce_scatter | solution.py:200
  792.2 439.2 %all-gather.34.cloned.1.call-start = ((), (), s32[]{:S(2)}) async-start(), calls=%async_computation.24 | async-start | bytes 12681216 | tf_op jit(solution)/shard_map/all_gather | solution.py:170
  818.3 512.7 %all-gather.30.cloned.1.call-start = ((), (), s32[]{:S(2)}) async-start(), calls=%async_computation.22 | async-start | bytes 7077888 | tf_op jit(solution)/shard_map/all_gather | solution.py:203
  978.4 5.7 copy-start
  978.4 412.9 %all-to-all-start.1 = ((bf16[4,1888,512]{2,1,0:T(8,128)(2,1)}), bf16[4,1888,512]{2,1,0:T(8,128)(2,1)}, u32[]{:S(2)}, u32[]{:S(2)}) async-start(bf16[4,1888,512]{2,1,0:T(8,128)(2,1)} %bitcast.148), calls=%async_computation.6 | async-start | bytes 15466496 | tf_op jit(solution)/shard_map/all_to_all | solution.py:219
  1429.8 1.6 slice-start
  1431.4 4.1 slice-start.1
Sparse Core Ops, SparseCore 0:
  10.1 76.0 all-gather.25
  88.4 26.7 all-gather.15
  117.4 58.2 all-gather.17
  177.7 43.3 all-gather.21
  223.7 73.3 all-gather.19
  299.9 61.3 all-reduce.1
  363.7 73.4 all-gather.27
  459.7 86.3 reduce-scatter.8
  550.3 87.8 reduce-scatter.6
  640.9 73.1 all-gather.23
  720.5 40.7 reduce-scatter.14
  764.2 54.0 reduce-scatter.16
  821.5 37.9 reduce-scatter.12
  861.5 116.7 all-gather.31
  982.4 86.0 reduce-scatter.10
  1070.6 160.7 all-gather.33
  1233.7 97.1 all-gather.29

commit v2 on v1

--- a/solution.py
+++ b/solution.py
@@ -1,9 +1,15 @@
+import functools
 import math
 
 import jax
 import jax.numpy as jnp
 from jax import lax
+from jax.experimental import pallas as pl
+from jax.experimental.pallas import tpu as pltpu
 from jax.sharding import PartitionSpec as P
+
+MESH = pl.DeviceIdType.MESH
+LINE = 4
 
 H = 16
 HD = 128
@@ -13,6 +19,298 @@
 masked_score = -1e30
 f32 = jnp.float32
 bf16 = jnp.bfloat16
+
+
+def greet(a, b, A, B, f):
+    bar = pltpu.get_barrier_semaphore()
+    conds = ((a > 0, a - 1, b), (a < A - 1, a + 1, b), (b > 0, a, b - 1), (b < B - 1, a, b + 1))
+    for cond, aa, bb in conds:
+
+        @pl.when(cond)
+        def _():
+            pl.semaphore_signal(bar, inc=1, device_id=(aa * B + bb, f), device_id_type=MESH)
+
+    low = (a + A - 1) // A + (b + B - 1) // B
+    high = (2 * A - 2 - a) // A + (2 * B - 2 - b) // B
+    pl.semaphore_wait(bar, low + high)
+
+
+def ag_kernel(n, q, x_ref, out_ref, lsem, sa, ra, sb, rb):
+    A = LINE
+    B = n // A
+    c = lax.axis_index("ctx")
+    f = lax.axis_index("fsdp")
+    a = c // B
+    b = c % B
+    rows = x_ref.shape[0]
+    cr = rows // q
+
+    def dev(aa, bb):
+        return (aa * B + bb, f)
+
+    left, right = a > 0, a < A - 1
+    low, high = b > 0, b < B - 1
+    greet(a, b, A, B, f)
+
+    def src(s, bb, i, own):
+        if own:
+            return x_ref.at[pl.ds(i * cr, cr)]
+        return out_ref.at[s * B + bb, pl.ds(i * cr, cr)]
+
+    def copy_a(k, d, i, own=False):
+        s = a - k if d == 0 else a + k
+        to = a + 1 if d == 0 else a - 1
+        return pltpu.make_async_remote_copy(
+            src_ref=src(s, b, i, own), dst_ref=out_ref.at[s * B + b, pl.ds(i * cr, cr)],
+            send_sem=sa.at[d, k, i], recv_sem=ra.at[d, k, i], device_id=dev(to, b), device_id_type=MESH)
+
+    def copy_b(j, s, m, d, i, own=False):
+        bb = b - m if d == 0 else b + m
+        to = b + 1 if d == 0 else b - 1
+        return pltpu.make_async_remote_copy(
+            src_ref=src(s, bb, i, own), dst_ref=out_ref.at[s * B + bb, pl.ds(i * cr, cr)],
+            send_sem=sb.at[d, m, j, i], recv_sem=rb.at[d, m, j, i], device_id=dev(a, to), device_id_type=MESH)
+
+    lst = [(0, 0, None)]
+    for k in range(1, A):
+        lst += [(k, k, 0), (A - 1 + k, k, 1)]
+
+    def valid(k, side):
+        if side is None:
+            return True
+        return (a >= k) if side == 0 else (a + k < A)
+
+    def when(cond):
+        if cond is True:
+            return lambda fn: fn()
+        return pl.when(cond)
+
+    local = pltpu.make_async_copy(x_ref, out_ref.at[c], lsem)
+    for i in range(q):
+        @pl.when(right)
+        def _():
+            copy_a(0, 0, i, True).start()
+        @pl.when(left)
+        def _():
+            copy_a(0, 1, i, True).start()
+        @pl.when(high)
+        def _():
+            copy_b(0, a, 0, 0, i, True).start()
+        @pl.when(low)
+        def _():
+            copy_b(0, a, 0, 1, i, True).start()
+    local.start()
+    for j, k, side in lst[1:]:
+        s = a - k if side == 0 else a + k
+        for i in range(q):
+            @pl.when(valid(k, side))
+            def _():
+                copy_a(k - 1, side, i).wait_recv()
+                if k < A - 1:
+                    onward = right if side == 0 else left
+                    @pl.when(onward)
+                    def _():
+                        copy_a(k, side, i).start()
+                @pl.when(high)
+                def _():
+                    copy_b(j, s, 0, 0, i).start()
+                @pl.when(low)
+                def _():
+                    copy_b(j, s, 0, 1, i).start()
+    for m in range(1, B):
+        for d, has, on in ((0, b >= m, high), (1, b + m < B, low)):
+            for j, k, side in lst:
+                s = a if side is None else (a - k if side == 0 else a + k)
+                for i in range(q):
+                    @pl.when(has if side is None else has & valid(k, side))
+                    def _():
+                        copy_b(j, s, m - 1, d, i).wait_recv()
+                        if m < B - 1:
+                            @pl.when(on)
+                            def _():
+                                copy_b(j, s, m, d, i).start()
+    local.wait()
+    for j, k, side in lst:
+        s = a if side is None else (a - k if side == 0 else a + k)
+        for i in range(q):
+            for d, cond in ((0, right), (1, left)):
+                if k == A - 1 or (side is not None and d != side):
+                    continue
+                @pl.when(cond if side is None else cond & valid(k, side))
+                def _():
+                    copy_a(k, d, i, side is None).wait_send()
+            for m in range(B - 1):
+                for d, on, has in ((0, high, b >= m), (1, low, b + m < B)):
+                    @pl.when(on & has if side is None else on & has & valid(k, side))
+                    def _():
+                        copy_b(j, s, m, d, i, side is None and m == 0).wait_send()
+
+
+def all_gather_ctx(x, n, q=1, cid=0):
+    A, B = LINE, n // LINE
+    return pl.pallas_call(
+        functools.partial(ag_kernel, n, q),
+        out_shape=jax.ShapeDtypeStruct((n,) + x.shape, x.dtype),
+        in_specs=[pl.BlockSpec(memory_space=pl.ANY)],
+        out_specs=pl.BlockSpec(memory_space=pl.ANY),
+        scratch_shapes=[
+            pltpu.SemaphoreType.DMA,
+            pltpu.SemaphoreType.DMA((2, A, q)), pltpu.SemaphoreType.DMA((2, A, q)),
+            pltpu.SemaphoreType.DMA((2, B, 2 * A - 1, q)), pltpu.SemaphoreType.DMA((2, B, 2 * A - 1, q)),
+        ],
+        compiler_params=pltpu.CompilerParams(collective_id=cid, has_side_effects=True),
+        name=f"ag{cid}",
+    )(x)
+
+
+def rs_kernel(n, q, x_ref, o_ref, part, rb, ra, sbs, sbr, sas, sar, lsem):
+    A = LINE
+    B = n // A
+    c = lax.axis_index("ctx")
+    f = lax.axis_index("fsdp")
+    a = c // B
+    b = c % B
+    rows = o_ref.shape[0]
+    cr = rows // q
+    h = a // 2
+    slots = (3 - 3 * h, 2 - h, 1 - a + 4 * h, a)
+
+    def ds(i):
+        return pl.ds(i * cr, cr)
+
+    def add(t, got):
+        r = part.at[t]
+        r[...] = (r[...].astype(jnp.float32) + got[...].astype(jnp.float32)).astype(r.dtype)
+
+    def copy_b(j, d, k, i):
+        s = slots[j]
+        t = b + k if d == 0 else b - k
+        to = b + 1 if d == 0 else b - 1
+        return pltpu.make_async_remote_copy(
+            src_ref=part.at[s * B + t, ds(i)], dst_ref=rb.at[d, k - 1, j, ds(i)],
+            send_sem=sbs.at[d, k, j, i], recv_sem=sbr.at[d, k - 1, j, i],
+            device_id=(a * B + to, f), device_id_type=MESH)
+
+    def come_b(j, d, k, i):
+        return pltpu.make_async_remote_copy(
+            src_ref=part.at[c, ds(i)], dst_ref=rb.at[d, k, j, ds(i)],
+            send_sem=sbs.at[d, k, j, i], recv_sem=sbr.at[d, k, j, i],
+            device_id=(c, f), device_id_type=MESH)
+
+    def copy_a(t, d, i):
+        k = t - a if d == 0 else a - t
+        to = a + 1 if d == 0 else a - 1
+        return pltpu.make_async_remote_copy(
+            src_ref=part.at[t * B + b, ds(i)], dst_ref=ra.at[d, k - 1, ds(i)],
+            send_sem=sas.at[d, k, i], recv_sem=sar.at[d, k - 1, i],
+            device_id=(to * B + b, f), device_id_type=MESH)
+
+    def come_a(d, k, i):
+        return pltpu.make_async_remote_copy(
+            src_ref=part.at[c, ds(i)], dst_ref=ra.at[d, k, ds(i)],
+            send_sem=sas.at[d, k, i], recv_sem=sar.at[d, k, i],
+            device_id=(c, f), device_id_type=MESH)
+
+    def has_b(d, k):
+        return (b + k < B) if d == 0 else (b >= k)
+
+    load = pltpu.make_async_copy(x_ref, part, lsem)
+    load.start()
+    greet(a, b, A, B, f)
+    load.wait()
+    from_b = (b > 0, b < B - 1)
+    from_a = (a > 0, a < A - 1)
+    for j in range(A):
+        for i in range(q):
+            for d in (0, 1):
+                for k in range(B - 1, 0, -1):
+                    @pl.when(jnp.logical_and(has_b(d, k), jnp.logical_not(from_b[d])))
+                    def _():
+                        copy_b(j, d, k, i).start()
+    for j in range(A):
+        s = slots[j]
+        for i in range(q):
+            for k in range(B - 1, 0, -1):
+                for d in (0, 1):
+                    if k < B - 1:
+                        @pl.when(jnp.logical_and(has_b(d, k), from_b[d]))
+                        def _():
+                            come_b(j, d, k, i).wait_recv()
+                            add((s * B + (b + k if d == 0 else b - k), ds(i)), rb.at[d, k, j, ds(i)])
+                            copy_b(j, d, k, i).start()
+            for d in (0, 1):
+                @pl.when(from_b[d])
+                def _():
+                    come_b(j, d, 0, i).wait_recv()
+                    add((s * B + b, ds(i)), rb.at[d, 0, j, ds(i)])
+            if j < A - 1:
+                for d in (0, 1):
+                    @pl.when((s > a) if d == 0 else (s < a))
+                    def _():
+                        @pl.when(from_a[d])
+                        def _():
+                            k = s - a if d == 0 else a - s
+                            come_a(d, k, i).wait_recv()
+                            add((s * B + b, ds(i)), ra.at[d, k, ds(i)])
+                        copy_a(s, d, i).start()
+    for i in range(q):
+        for d in (0, 1):
+            @pl.when(from_a[d])
+            def _():
+                come_a(d, 0, i).wait_recv()
+                add((c, ds(i)), ra.at[d, 0, ds(i)])
+    o_ref[...] = part[c]
+    for j in range(A):
+        for i in range(q):
+            for d in (0, 1):
+                for k in range(B - 1, 0, -1):
+                    @pl.when(has_b(d, k))
+                    def _():
+                        copy_b(j, d, k, i).wait_send()
+                if j < A - 1:
+                    @pl.when((slots[j] > a) if d == 0 else (slots[j] < a))
+                    def _():
+                        copy_a(slots[j], d, i).wait_send()
+
+
+def reduce_scatter_ctx(x, n, q=1, cid=0):
+    A, B = LINE, n // LINE
+    rows = x.shape[0] // n
+    w = x.shape[1]
+    return pl.pallas_call(
+        functools.partial(rs_kernel, n, q),
+        out_shape=jax.ShapeDtypeStruct((rows, w), x.dtype),
+        in_specs=[pl.BlockSpec(memory_space=pl.ANY)],
+        out_specs=pl.BlockSpec(memory_space=pltpu.VMEM),
+        scratch_shapes=[
+            pltpu.VMEM((n, rows, w), x.dtype),
+            pltpu.VMEM((2, B - 1, A, rows, w), x.dtype),
+            pltpu.VMEM((2, A - 1, rows, w), x.dtype),
+            pltpu.SemaphoreType.DMA((2, B, A, q)), pltpu.SemaphoreType.DMA((2, B, A, q)),
+            pltpu.SemaphoreType.DMA((2, A, q)), pltpu.SemaphoreType.DMA((2, A, q)),
+            pltpu.SemaphoreType.DMA,
+        ],
+        compiler_params=pltpu.CompilerParams(collective_id=cid, has_side_effects=True, vmem_limit_bytes=60 << 20),
+        name=f"rs{cid}",
+    )(x.reshape(n, rows, w))
+
+
+def assemble(parts, n_groups, block=64):
+    n, rows, gw = parts.shape
+    w = gw // n_groups
+
+    def body(i_ref, o_ref):
+        for g in range(n_groups):
+            for c in range(n):
+                o_ref[:, (g * n + c) * w:(g * n + c + 1) * w] = i_ref[c, :, g * w:(g + 1) * w].astype(jnp.float32)
+
+    return pl.pallas_call(
+        body, grid=(rows // block,),
+        out_shape=jax.ShapeDtypeStruct((rows, n * gw), jnp.float32),
+        in_specs=[pl.BlockSpec((n, block, gw), lambda i: (0, i, 0))],
+        out_specs=pl.BlockSpec((block, n * gw), lambda i: (i, 0)),
+        compiler_params=pltpu.CompilerParams(vmem_limit_bytes=60 << 20),
+        name="assemble")(parts)
 
 
 def rope_tables(within):
@@ -77,7 +375,7 @@
     ratio = n_ctx // n_fsdp
 
     x_own = tokens[0]
-    x_all = lax.all_gather(x_own, "ctx", axis=0, tiled=True)
+    x_all = all_gather_ctx(x_own, n_ctx, 2, 0).reshape(all_rows, width)
 
     qkv_own = lax.dynamic_slice(w_qkv.reshape(kr, 3, width), (0, 0, me * hw), (kr, 3, hw))
     wq = lax.all_gather(qkv_own.reshape(kr, 3 * hw).astype(bf16), "fsdp", axis=0, tiled=True)
@@ -97,7 +395,7 @@
     wgu = lax.all_gather(wg_own, "fsdp", axis=0, tiled=True)
     down_own = lax.dynamic_slice(w_down, ((me % ratio) * ffs, 0), (ffs, width)).astype(bf16)
     wd = lax.psum(jnp.where(mine == me // ratio, down_own, jnp.zeros_like(down_own)), "fsdp")
-    g_all = lax.all_gather(cotangent[0], "ctx", axis=0, tiled=True)
+    g_all = all_gather_ctx(cotangent[0], n_ctx, 2, 1).reshape(all_rows, width)
 
     deal_table = deal[0]
     device_index = jnp.arange(n_ctx, dtype=jnp.int32)
@@ -146,7 +444,7 @@
     hidden = x_dealt.reshape(rows, width).astype(f32) + dot(mixed_own, wo, NN)
     scale_two = rms_scale(hidden)
     normed_two = (hidden * scale_two * gain_two[None, :]).astype(bf16)
-    n2_all = lax.all_gather(normed_two, "ctx", axis=0, tiled=True)
+    n2_all = all_gather_ctx(normed_two, n_ctx, 2, 2).reshape(all_rows, width)
 
     both = dot(n2_all, wgu, NN)
     gate = both[:, :ffs]
@@ -155,7 +453,7 @@
     gate_act = gate * sigma
     activated = (gate_act * up).astype(bf16)
     down_part = dot(activated, wd, NN).astype(bf16)
-    down_own_rows = lax.psum_scatter(down_part, "ctx", scatter_dimension=0, tiled=True)
+    down_own_rows = reduce_scatter_ctx(down_part, n_ctx, 2, 4)
     block_out = (hidden + down_own_rows.astype(f32)).astype(bf16)[None]
 
     d_act = dot(g_all, wd, NT)
@@ -163,19 +461,17 @@
         [d_act * up * sigma * (1.0 + gate * (1.0 - sigma)), d_act * gate_act], -1
     ).astype(bf16)
     d_two_part = dot(d_both, wgu, NT).astype(bf16)
-    d_two = lax.psum_scatter(d_two_part, "ctx", scatter_dimension=0, tiled=True).astype(f32)
+    d_two = reduce_scatter_ctx(d_two_part, n_ctx, 2, 5).astype(f32)
     grad_down = dot(activated, g_all, TN).astype(bf16)
     grad_gate_up = dot(n2_all, d_both, TN).astype(bf16)
     row_gate_up = lax.psum_scatter(grad_gate_up, "fsdp", scatter_dimension=0, tiled=True)
-    all_gate_up = lax.all_gather(row_gate_up, "ctx", axis=0)
-    final_gate_up = (
-        all_gate_up.reshape(n_ctx, kr, 2, ffs).transpose(1, 2, 0, 3).reshape(kr, 2 * ff).astype(f32)
-    )
+    all_gate_up = all_gather_ctx(row_gate_up, n_ctx, 2, 7)
+    final_gate_up = assemble(all_gate_up, 2)
 
     grad_norm2 = jnp.sum(d_two * hidden * scale_two, 0)
     d_hidden = cotangent[0].astype(f32) + norm_back(d_two, hidden, scale_two, gain_two)
     d_branch = d_hidden.astype(bf16)
-    db_all = lax.all_gather(d_branch, "ctx", axis=0, tiled=True)
+    db_all = all_gather_ctx(d_branch, n_ctx, 2, 3).reshape(all_rows, width)
 
     grad_out = dot(mixed_dealt, db_all, TN).astype(bf16)
     wo_own = lax.dynamic_slice(wo, (me * hw, 0), (hw, width))
@@ -197,13 +493,11 @@
         -1,
     ).astype(bf16)
     d_one_part = dot(d_proj, wq, NT).astype(bf16)
-    d_one = lax.psum_scatter(d_one_part, "ctx", scatter_dimension=0, tiled=True).astype(f32)
+    d_one = reduce_scatter_ctx(d_one_part, n_ctx, 2, 6).astype(f32)
     grad_qkv = dot(normed_one, d_proj, TN).astype(bf16)
     row_qkv = lax.psum_scatter(grad_qkv, "fsdp", scatter_dimension=0, tiled=True)
-    all_qkv = lax.all_gather(row_qkv, "ctx", axis=0)
-    final_qkv = (
-        all_qkv.reshape(n_ctx, kr, 3, hw).transpose(1, 2, 0, 3).reshape(kr, 3 * width).astype(f32)
-    )
+    all_qkv = all_gather_ctx(row_qkv, n_ctx, 2, 8)
+    final_qkv = assemble(all_qkv, 3)
 
     own_float = x_own.astype(f32)
     scale_one = rms_scale(own_float)
@@ -214,7 +508,7 @@
 
     grad_rows = jnp.concatenate([grad_down, grad_out], 0)
     col_rows = lax.psum_scatter(grad_rows, "fsdp", scatter_dimension=1, tiled=True)
-    all_cols = lax.all_gather(col_rows, "ctx", axis=0)
+    all_cols = all_gather_ctx(col_rows, n_ctx, 1, 9)
     owner_rows = all_cols.reshape(n_fsdp, ratio * (ffs + hw), width // n_fsdp)
     swapped = lax.all_to_all(owner_rows, "fsdp", split_axis=0, concat_axis=2, tiled=True)
     swapped = swapped.reshape(ratio, ffs + hw, width)

time: 1460 us -> 1010 us (0.69)
  waiting for transfers between devices: 976 us -> 9.75 us
  Pallas kernels: 0 us -> 645 us
  local copies, waits for them, and re-layouts: 199 us -> 74.2 us
    pallas_call x0 -> x12, Pallas kernels: none -> 645 us  [the longest x7 476 us: all_gather_ctx(): pl.pallas_call(functools.partial(ag_kernel, n, q), out_shape=jax.ShapeDty...]
    all_gather x7 -> x0, waiting for transfers between devices: 516 us -> none  [the longest x1 119 us: shards(): all_cols = lax.all_gather(col_rows, 'ctx', axis=0)]
    reduce_scatter x3 -> x0, waiting for transfers between devices: 250 us -> none  [the longest x1 90.7 us: shards(): lax.psum_scatter(down_part, 'ctx', scatter_dimension=0, tiled=True)]
    unnamed x33 -> x41, local copies, waits for them, and re-layouts: 94.7 us -> 10.4 us
    psum x1, waiting for transfers between devices: 53.1 us -> 0.01 us  [shards(): lax.psum(jnp.where(mine == me // ratio, down_own, jnp.zeros_like(down_own...]
    reduce_scatter x1, waiting for transfers between devices: 41.2 us -> 0.01 us  [shards(): lax.psum_scatter(grad_qkv, 'fsdp', scatter_dimension=0, tiled=True)]
    convert_element_type x3 -> x1, local copies, waits for them, and re-layouts: 49.1 us -> 8.36 us  [shards(): grad_gate_up = dot(n2_all, d_both, TN).astype(bf16)]
    all_gather x1, waiting for transfers between devices: 33.6 us -> 0.02 us  [shards(): wgu = lax.all_gather(wg_own, 'fsdp', axis=0, tiled=True)]
  transfers between devices with their start and end apart: 19 -> 9, of which waited for: 17 -> 1; matrix products, arithmetic and copies ran while one was open for 21% -> 15% of each run, Pallas kernels for 0% -> 50%
where the time goes in v2:
time: 1010 us; the launch traced here: 1000 us
  Pallas kernels  645 us (64%)
  matrix products  135 us (13%)
  local copies, waits for them, and re-layouts  74.2 us (7%)
  blocking collectives  63.5 us (6%)
  other arithmetic  47.8 us (5%)
  between operations  15.1 us (1%)
  starting transfers between devices  10.9 us (1%)
    pallas_call x7, Pallas kernels, all_gather_ctx(): pl.pallas_call(functools.partial(ag_kernel, n, q), out_shape=jax.ShapeDty...  476 us
    pallas_call x3, Pallas kernels, reduce_scatter_ctx(): pl.pallas_call(functools.partial(rs_kernel, n, q), out_shape=jax.ShapeDty...  147 us
    dot_general x12, matrix products, dot(): return lax.dot_general(a, b, (dims, ((), ())), preferred_element_type=f32)  82.5 us
    psum x1, blocking collectives, shards(): sums = lax.psum(jnp.stack([grad_norm1, grad_norm2]), ('ctx', 'fsdp'))  57.1 us
    pallas_call x2, Pallas kernels, assemble(): pl.pallas_call(body, grid=(rows // block,), out_shape=jax.ShapeDtypeStruc...  22.5 us
    all_to_all x1, local copies, waits for them, and re-layouts, shards(): lax.all_to_all(owner_rows, 'fsdp', split_axis=0, concat_axis=2, tiled=True)  22.5 us
  transfers between devices with their start and end apart: 9, of which 1 were waited for; matrix products, arithmetic and copies ran while one was open for 15% of the time, Pallas kernels for 50%

profile of v2, /device:TPU:0, one launch (start us, length us, event | category | flops | bytes accessed | tf_op | source)
XLA Modules:
  0.0 1001.0 jit_solution(14929679514140048820)
XLA Ops:
  7.2 10.0 copy.72
  19.3 3.8 convert_element_type.155
  23.2 2.6 dynamic-slice_convert_fusion.2
  27.5 5.3 fusion.18
  33.3 6.4 all_gather.12
  39.8 51.1 %ag0.1 = bf16[8,128,2048]{2,1,0:T(8,128)(2,1)} custom-call(bf16[128,2048]{1,0:T(8,128)(2,1)} %bitcast.128), custom_call_target="tpu_custom_call" | custom-call | tf_op jit(solution)/shard_map/ag0/pallas_call | solution.py:151
  90.8 3.1 multiply_reduce_fusion.1
  95.1 48.8 %ag1.1 = bf16[8,128,2048]{2,1,0:T(8,128)(2,1)} custom-call(bf16[128,2048]{1,0:T(8,128)(2,1)} %bitcast.145), custom_call_target="tpu_custom_call" | custom-call | tf_op jit(solution)/shard_map/ag1/pallas_call | solution.py:151
  143.9 5.2 fusion.3
  150.2 6.3 fusion.88
  158.8 8.0 fusion.85
  166.7 4.1 fusion.43
  173.2 4.6 all-to-all-start
  177.9 2.8 gather_fusion
  181.7 9.6 all-to-all-done
  191.5 4.9 multiply_reduce_fusion.2
  197.4 47.5 %ag2.1 = bf16[8,128,2048]{2,1,0:T(8,128)(2,1)} custom-call(bf16[128,2048]{1,0:T(8,128)(2,1)} %multiply_convert_fusion.2.x_ref), custom_call_target="tpu_custom_call" | custom-call | tf_op jit(solution)/shard_map/ag2/pallas_call | solution.py:151
  244.9 11.1 %fusion.89 = f32[1024,1376]{0,1:T(8,128)} fusion(bf16[1024,2048]{1,0:T(8,128)(2,1)} %bitcast.135, bf16[2048,1376]{1,0:T(8,128)(2,1)} %all-gather.8.cloned.1.call-done), kind=kOutput, calls=%fused_computation.170 | convolution fusion | flops 5771362304 | bytes 15466496 | tf_op jit(solution)/shard_map/dot_general | solution.py:349
  256.0 10.0 fusion.21
  266.0 8.3 convolution_convert_fusion.1
  274.3 48.3 %rs5.1 = bf16[128,2048]{1,0:T(8,128)(2,1)} custom-call(bf16[8,128,2048]{2,1,0:T(8,128)(2,1)} %bitcast.139), custom_call_target="tpu_custom_call" | custom-call | tf_op jit(solution)/shard_map/rs5/pallas_call | solution.py:280
  324.0 7.4 convolution_convert_fusion.5
  331.4 5.0 convolution_convert_fusion.2
  336.4 47.9 %rs4.1 = bf16[128,2048]{1,0:T(8,128)(2,1)} custom-call(bf16[8,128,2048]{2,1,0:T(8,128)(2,1)} %bitcast.138), custom_call_target="tpu_custom_call" | custom-call | tf_op jit(solution)/shard_map/rs4/pallas_call | solution.py:280
  386.7 45.6 %ag3.1 = bf16[8,128,2048]{2,1,0:T(8,128)(2,1)} custom-call(bf16[128,2048]{1,0:T(8,128)(2,1)} %get-tuple-element.31.x_ref), custom_call_target="tpu_custom_call" | custom-call | tf_op jit(solution)/shard_map/ag3/pallas_call | solution.py:151
  432.3 3.8 convolution_convert_fusion.6
  438.8 3.8 convolution_convert_fusion.7
  443.9 5.5 fusion.90
  449.4 14.5 %fusion.31 = f32[1024,2,128]{0,2,1:T(8,128)} fusion(bf16[1024,2,128]{0,2,1:T(8,128)(2,1)S(1)} %copy-done.8, f32[2,1024,1024]{1,2,0:T(8,128)} %fusion.90, f32[2,1024,1024]{1,2,0:T(8,128)} %get-tuple-element.54, f32[2,1024]{1,0:T(2,128)S(1)} %get-tuple-element.53), kind=kOutput, calls=%fused_computation.61 | convolution fusion | flops 551554048 | bytes 18358272 | tf_op jit(solution)/shard_map/hqk,qhd->khd/dot_general | solution.py:485
  463.9 15.3 %broadcast_multiply_fusion.1 = (f32[1024,2,128]{0,2,1:T(8,128)}, f32[1024,2,128]{0,2,1:T(8,128)S(1)}, f32[1024,2,128]{0,2,1:T(8,128)}) fusion(f32[1024,128]{0,1:T(8,128)S(1)} %get-tuple-element.61, f32[1024,2,128]{0,2,1:T(8,128)} %fusion.31, bf16[1024,2,128]{0,2,1:T(8,128)(2,1)S(1)} %copy-done.7, f32[2,1024,1024]{1,2,0:T(8,128)} %fusion.90, ...), kind=kOutput, calls=%fused_computation.111 | convolution fusion | flops 552078336 | bytes 22028288 | tf_op jit(solution)/shard_map/hqk,khd->qhd/dot_general | solution.py:484
  481.8 5.1 fusion.37
  486.9 4.9 convolution_convert_fusion.4
  492.1 10.2 %convolution_convert_fusion = bf16[2048,1376]{0,1:T(8,128)(2,1)} fusion(bf16[1024,2048]{1,0:T(8,128)(2,1)} %bitcast.136, bf16[1024,688]{0,1:T(8,128)(2,1)} %copy-done.19, bf16[1024,688]{0,1:T(8,128)(2,1)} %copy-done.18), kind=kOutput, calls=%fused_computation.15 | convolution fusion | flops 5779816448 | bytes 12648448 | tf_op jit(solution)/shard_map/dot_general | solution.py:349
  502.3 8.4 copy.85
  510.7 85.2 %ag9.1 = bf16[8,944,512]{2,1,0:T(8,128)(2,1)} custom-call(bf16[944,512]{1,0:T(8,128)(2,1)} %reduce-scatter.6.cloned.1.call-done.x_ref), custom_call_target="tpu_custom_call" | custom-call | tf_op jit(solution)/shard_map/ag9/pallas_call | solution.py:151
  595.9 5.7 all-to-all-start.1
  601.8 6.9 convolution_convert_fusion.3
  608.8 50.4 %rs6.1 = bf16[128,2048]{1,0:T(8,128)(2,1)} custom-call(bf16[8,128,2048]{2,1,0:T(8,128)(2,1)} %bitcast.137), custom_call_target="tpu_custom_call" | custom-call | tf_op jit(solution)/shard_map/rs6/pallas_call | solution.py:280
  659.2 2.8 gather_fusion.2
  663.4 57.1 %psum.15 = f32[2,2048]{1,0:T(2,128)S(1)} all-reduce(f32[2,2048]{1,0:T(2,128)S(1)} %pad_maximum_fusion.10), channel_id=1, replica_groups=mesh['ctx'=8,'fsdp'=4] {'ctx','fsdp'}, use_global_device_ids=true, to_apply=%region_15.18 | all-reduce | flops 4096 | bytes 32768 | tf_op jit(solution)/shard_map/psum | solution.py:518
  723.6 71.6 %ag8.1.i_ref = bf16[8,512,768]{2,1,0:T(8,128)(2,1)} custom-call(bf16[512,768]{1,0:T(8,128)(2,1)} %reduce-scatter.4.cloned.1.call-done.x_ref), custom_call_target="tpu_custom_call" | custom-call | tf_op jit(solution)/shard_map/ag8/pallas_call | solution.py:151
  795.2 8.8 assemble.2
  804.0 125.8 %ag7.1.i_ref = bf16[8,512,1376]{2,1,0:T(8,128)(2,1)} custom-call(bf16[512,1376]{1,0:T(8,128)(2,1)} %reduce-scatter.8.cloned.1.call-done.x_ref), custom_call_target="tpu_custom_call" | custom-call | tf_op jit(solution)/shard_map/ag7/pallas_call | solution.py:151
  929.8 13.7 %assemble.3 = f32[512,11008]{1,0:T(8,128)} custom-call(bf16[8,512,1376]{2,1,0:T(8,128)(2,1)} %ag7.1.i_ref), custom_call_target="tpu_custom_call" | custom-call | tf_op jit(solution)/shard_map/assemble/pallas_call | solution.py:307
  943.6 22.5 %copy.84 = bf16[1,1888,4,512]{3,2,1,0:T(4,128)(2,1)} copy(bf16[1,1888,4,512]{3,1,2,0:T(8,128)(2,1)} %bitcast.48) | data formatting | bytes 15466496 | tf_op jit(solution)/shard_map/all_to_all | solution.py:513
  966.0 15.9 %reshape.268 = bf16[2,944,2048]{2,1,0:T(8,128)(2,1)} reshape(bf16[1,1888,4,512]{3,2,1,0:T(4,128)(2,1)} %copy.84) | data formatting | bytes 15466496 | tf_op jit(solution)/shard_map/reshape | solution.py:514
  983.5 2.8 bitcast_convert_fusion.1
  987.6 6.3 bitcast_convert_fusion
  (133 shorter events, 31.5 us)
Async XLA Ops:
  7.2 143.1 %all-gather.4.cloned.1.call-start = ((), (), s32[]{:S(2)}) async-start(), calls=%async_computation.5 | async-start | bytes 3932160 | tf_op jit(solution)/shard_map/all_gather | solution.py:381
  19.3 172.2 %all-gather.6.cloned.1.call-start = ((), (), s32[]{:S(2)}) async-start(), calls=%async_computation.6 | async-start | bytes 10485760 | tf_op jit(solution)/shard_map/all_gather | solution.py:387
  23.2 221.7 %all-gather.8.cloned.1.call-start = ((), (), s32[]{:S(2)}) async-start(), calls=%async_computation.7 | async-start | bytes 7208960 | tf_op jit(solution)/shard_map/all_gather | solution.py:395
  27.4 228.6 %all-reduce.2.cloned.1.call-start = ((), (), s32[]{:S(2)}) async-start(), calls=%async_computation.8 | async-start | bytes 5636096 | tf_op jit(solution)/shard_map/psum | solution.py:397
  27.4 5.4 copy-start.11
  27.5 5.8 copy-start.12
  27.5 5.8 copy-start.13
  39.7 104.2 %copy-start.9 = (f32[1,2048]{1,0:T(1,128)}, f32[1,2048]{1,0:T(1,128)S(1)}, u32[]{:S(2)}) copy-start(f32[1,2048]{1,0:T(1,128)S(1)} %get-tuple-element.46) | copy-start | bytes 24580
  39.7 54.2 %copy-start.16 = (s32[1,3]{1,0:T(1,128)S(1)}, s32[1,3]{1,0:T(1,128)}, u32[]{:S(2)}) copy-start(s32[1,3]{1,0:T(1,128)} %param.16) | copy-start | bytes 40
  173.2 18.0 %all-to-all-start = ((bf16[8,128,256]{2,1,0:T(8,128)(2,1)}), bf16[8,128,256]{2,1,0:T(8,128)(2,1)S(1)}, u32[]{:S(2)}, u32[]{:S(2)}) async-start(bf16[8,128,256]{2,1,0:T(8,128)(2,1)} %bitcast.18), calls=%async_computation | async-start | bytes 1048576 | tf_op jit(solution)/shard_map/all_to_all | solution.py:438
  177.8 333.0 %reduce-scatter.6.cloned.1.call-start = ((), (), s32[]{:S(2)}) async-start(), calls=%async_computation.10 | async-start | bytes 4833280 | tf_op jit(solution)/shard_map/reduce_scatter | solution.py:510
  256.0 10.0 %copy-start.14 = (bf16[2048,1376]{1,0:T(8,128)(2,1)S(1)}, bf16[2048,1376]{1,0:T(8,128)(2,1)}, u32[]{:S(2)}) copy-start(bf16[2048,1376]{1,0:T(8,128)(2,1)} %all-gather.8.cloned.1.call-done) | copy-start | bytes 16908292
  266.0 8.3 copy-start.18
  266.0 8.3 copy-start.19
  324.0 7.4 copy-start.15
  324.0 7.4 copy-start.17
  336.4 47.9 %copy-start.1 = (bf16[128,2048]{1,0:T(8,128)(2,1)S(1)}, bf16[128,2048]{1,0:T(8,128)(2,1)}, u32[]{:S(2)}) copy-start(bf16[128,2048]{1,0:T(8,128)(2,1)} %rs5.1) | copy-start | bytes 1572868
  336.4 47.9 %copy-start.4 = (bf16[1,128,2048]{2,1,0:T(8,128)(2,1)S(1)}, bf16[1,128,2048]{2,1,0:T(8,128)(2,1)}, u32[]{:S(2)}) copy-start(bf16[1,128,2048]{2,1,0:T(8,128)(2,1)} %param.15) | copy-start | bytes 1572868
  432.3 3.8 copy-start.3
  438.5 285.1 %reduce-scatter.4.cloned.1.call-start = ((), (), s32[]{:S(2)}) async-start(), calls=%async_computation.9 | async-start | bytes 3932160 | tf_op jit(solution)/shard_map/reduce_scatter | solution.py:498
  443.9 5.5 copy-start.8
  449.4 14.5 %copy-start.7 = (bf16[1024,2,128]{0,2,1:T(8,128)(2,1)S(1)}, bf16[1024,2,128]{0,2,1:T(8,128)(2,1)}, u32[]{:S(2)}) copy-start(bf16[1024,2,128]{0,2,1:T(8,128)(2,1)} %get-tuple-element.33) | copy-start | bytes 1572868
  479.3 1.5 copy-start.5
  479.3 1.9 copy-start.6
  481.8 5.2 copy-start.2
  491.9 312.1 %reduce-scatter.8.cloned.1.call-start = ((), (), s32[]{:S(2)}) async-start(), calls=%async_computation.11 | async-start | bytes 7208960 | tf_op jit(solution)/shard_map/reduce_scatter | solution.py:467
  595.9 5.7 copy-start
  595.9 347.6 %all-to-all-start.1 = ((bf16[4,1888,512]{2,1,0:T(8,128)(2,1)}), bf16[4,1888,512]{2,1,0:T(8,128)(2,1)}, u32[]{:S(2)}, u32[]{:S(2)}) async-start(bf16[4,1888,512]{2,1,0:T(8,128)(2,1)} %bitcast.123), calls=%async_computation.3 | async-start | bytes 15466496 | tf_op jit(solution)/shard_map/all_to_all | solution.py:513
  608.8 53.2 %copy-start.10 = (f32[1,2048]{1,0:T(1,128)S(1)}, f32[1,2048]{1,0:T(1,128)}, u32[]{:S(2)}) copy-start(f32[1,2048]{1,0:T(1,128)} %copy-done.9) | copy-start | bytes 24580
  981.9 1.6 slice-start
  983.5 4.1 slice-start.1
Sparse Core Ops, SparseCore 0:
  19.4 31.2 all-gather.3
  52.9 58.2 all-gather.5
  112.7 43.3 all-gather.7
  159.0 63.0 all-reduce.1
  438.7 44.7 reduce-scatter.5
  492.0 39.5 reduce-scatter.3
  534.8 54.8 reduce-scatter.7

commit v3 on v1

v3 whole, which is shorter than its diff:
```python
import functools
import math

import jax
import jax.numpy as jnp
from jax import lax
from jax.experimental import pallas as pl
from jax.experimental.pallas import tpu as pltpu
from jax.sharding import PartitionSpec as P

MESH = pl.DeviceIdType.MESH
LINE = 4

H = 16
HD = 128

epsilon = 1e-06
rope_base = 10000.0
masked_score = -1e30
f32 = jnp.float32
bf16 = jnp.bfloat16


def greet(a, b, n_a, n_b, f, fsdp=False):
    bar = pltpu.get_barrier_semaphore()
    conds = ((a > 0, a - 1, b), (a < n_a - 1, a + 1, b), (b > 0, a, b - 1), (b < n_b - 1, a, b + 1))
    for cond, aa, bb in conds:

        @pl.when(cond)
        def _():
            pl.semaphore_signal(bar, inc=1, device_id=(aa * n_b + bb, f), device_id_type=MESH)

    low = (a + n_a - 1) // n_a + (b + n_b - 1) // n_b
    high = (2 * n_a - 2 - a) // n_a + (2 * n_b - 2 - b) // n_b
    total = low + high
    if fsdp:
        n_y = lax.axis_size("fsdp") // 2
        y, core = f // 2, f % 2
        for cond, to in ((y > 0, f - 2), (y < n_y - 1, f + 2), (True, f + 1 - 2 * core)):
            when(cond)(
                lambda to=to: pl.semaphore_signal(
                    bar, inc=1, device_id=(a * n_b + b, to), device_id_type=MESH
                )
            )
        total = total + 1 + (y + n_y - 1) // n_y + (2 * n_y - 2 - y) // n_y
    pl.semaphore_wait(bar, total)


def both(*conds):
    out = True
    for cond in conds:
        if cond is not True:
            out = cond if out is True else jnp.logical_and(out, cond)
    return out


def when(cond):
    return (lambda fn: fn()) if cond is True else pl.when(cond)


def plan(rows, cuts=2):
    unit = rows // 16
    if rows % 16 or unit < 4:
        return ((0, rows, False),)
    swapped = max(1, (unit + 4) // 8)
    rest = unit - swapped
    marks = [rest * i // cuts for i in range(cuts + 1)]
    chunks = [(16 * lo, 16 * (hi - lo), False) for lo, hi in zip(marks, marks[1:])]
    return tuple(chunks) + ((16 * rest, 16 * swapped, True),)


def places(n):
    n_a, n_b = LINE, n // LINE
    c = lax.axis_index("ctx")
    return n_a, n_b, c // n_b, c % n_b, lax.axis_index("fsdp")


def gather_steps(n, x, out, chunk, sems):
    n_a, n_b, a, b, f = places(n)
    first, count, swapped = chunk
    s1, r1, s2, r2 = sems
    (p1, n1), (p2, n2) = ((b, n_b), (a, n_a)) if swapped else ((a, n_a), (b, n_b))

    def slot(q1, q2):
        return q2 * n_b + q1 if swapped else q1 * n_b + q2

    rows = pl.ds(first, count)
    below1, above1, below2, above2 = p1 > 0, p1 < n1 - 1, p2 > 0, p2 < n2 - 1

    def copy1(k, d):
        q1 = p1 - k if d == 0 else p1 + k
        to = p1 + 1 if d == 0 else p1 - 1
        return pltpu.make_async_remote_copy(
            src_ref=x.at[rows] if k == 0 else out.at[slot(q1, p2), rows],
            dst_ref=out.at[slot(q1, p2), rows],
            send_sem=s1.at[d, k],
            recv_sem=r1.at[d, k],
            device_id=(slot(to, p2), f),
            device_id_type=MESH,
        )

    def copy2(j, q1, m, d):
        q2 = p2 - m if d == 0 else p2 + m
        to = p2 + 1 if d == 0 else p2 - 1
        return pltpu.make_async_remote_copy(
            src_ref=x.at[rows] if j == 0 and m == 0 else out.at[slot(q1, q2), rows],
            dst_ref=out.at[slot(q1, q2), rows],
            send_sem=s2.at[d, m, j],
            recv_sem=r2.at[d, m, j],
            device_id=(slot(p1, to), f),
            device_id_type=MESH,
        )

    shards = [(0, 0, None, p1, True)]
    for k in range(1, n1):
        shards.append((k, k, 0, p1 - k, p1 >= k))
        shards.append((n1 - 1 + k, k, 1, p1 + k, p1 + k < n1))

    def own():
        for d, cond in ((0, above1), (1, below1)):
            when(cond)(lambda d=d: copy1(0, d).start())
        for d, cond in ((0, above2), (1, below2)):
            when(cond)(lambda d=d: copy2(0, p1, 0, d).start())

    def line1(k):
        for j, kk, side, q1, there in shards:
            if kk != k:
                continue

            @when(there)
            def _():
                copy1(k - 1, side).wait_recv()
                if k < n1 - 1:
                    when(above1 if side == 0 else below1)(lambda: copy1(k, side).start())
                for d, cond in ((0, above2), (1, below2)):
                    when(cond)(lambda d=d: copy2(j, q1, 0, d).start())

    def line2(m):
        for d, there2, onward in ((0, p2 >= m, above2), (1, p2 + m < n2, below2)):
            for j, _, _, q1, there in shards:

                @when(both(there2, there))
                def _():
                    copy2(j, q1, m - 1, d).wait_recv()
                    if m < n2 - 1:
                        when(onward)(lambda: copy2(j, q1, m, d).start())

    def finish():
        for j, k, side, q1, there in shards:
            for d, onward in ((0, above1), (1, below1)):
                if k < n1 - 1 and side in (None, d):
                    when(both(onward, there))(lambda d=d: copy1(k, d).wait_send())
            for m in range(n2 - 1):
                for d, onward, there2 in ((0, above2, p2 >= m), (1, below2, p2 + m < n2)):
                    when(both(onward, there, True if m == 0 else there2))(
                        lambda d=d, m=m: copy2(j, q1, m, d).wait_send()
                    )

    steps = [own]
    steps += [functools.partial(line1, k) for k in range(1, n1)]
    steps += [functools.partial(line2, m) for m in range(1, n2)]
    return steps, finish


def spread_steps(n, x, out, chunk, sems):
    f = lax.axis_index("fsdp")
    c = lax.axis_index("ctx")
    n_f = lax.axis_size("fsdp")
    n_y = n_f // 2
    y, core = f // 2, f % 2
    owner = c // (n // n_f)
    oy, oc = owner // 2, owner % 2
    first, count = chunk
    rows = pl.ds(first, count)
    up, down, side, come = sems

    def copy(own, sem, to):
        return pltpu.make_async_remote_copy(
            src_ref=x.at[rows] if own else out.at[rows],
            dst_ref=out.at[rows],
            send_sem=sem,
            recv_sem=come,
            device_id=(c, to),
            device_id_type=MESH,
        )

    on = core == oc
    ways = (
        (up, f + 2, jnp.logical_and(on, jnp.logical_and(y >= oy, y < n_y - 1))),
        (down, f - 2, jnp.logical_and(on, jnp.logical_and(y <= oy, y > 0))),
        (side, f + 1 - 2 * core, on),
    )

    def own():
        for sem, to, cond in ways:
            pl.when(jnp.logical_and(cond, f == owner))(lambda sem=sem, to=to: copy(True, sem, to).start())

    def onward():
        @pl.when(f != owner)
        def _():
            copy(False, side, f).wait_recv()
            for sem, to, cond in ways:
                pl.when(cond)(lambda sem=sem, to=to: copy(False, sem, to).start())

    def finish():
        for sem, to, cond in ways:
            pl.when(cond)(lambda sem=sem, to=to: copy(False, sem, to).wait_send())

    return own, onward, finish


def gather_sems(chunks):
    sem = pltpu.SemaphoreType.DMA
    return [sem((chunks, 2, 4)), sem((chunks, 2, 4)), sem((chunks, 2, 4, 7)), sem((chunks, 2, 4, 7))]


def gather_kernel(n, plans, spread, *refs):
    count = len(plans)
    k = count + (1 if spread else 0)
    xs, outs = refs[:k], refs[k : 2 * k]
    held = refs[2 * k : 3 * k]
    local, s1, r1, s2, r2, s3 = refs[3 * k :]
    n_a, n_b, a, b, f = places(n)
    c = a * n_b + b
    greet(a, b, n_a, n_b, f, bool(spread))
    steps, ends, at = [], [], 0
    for x, out, chunks in zip(xs, outs, plans):
        for chunk in chunks:
            sems = (s1.at[at], r1.at[at], s2.at[at], r2.at[at])
            more, end = gather_steps(n, x, out, chunk, sems)
            steps.append(more)
            ends.append(end)
            at += 1
    for i, chunk in enumerate(spread):
        begin, onward, end = spread_steps(n, xs[-1], outs[-1], chunk, [s3.at[i, j] for j in range(4)])
        steps.append([begin] + [lambda: None] * (1 + 2 * i) + [onward])
        ends.append(end)
    mine = f == c // (n // lax.axis_size("fsdp"))
    for t in range(max(map(len, steps))):
        for more in steps:
            if t < len(more):
                more[t]()
        if t < 2:
            for i in range(k):
                out = outs[i].at[c] if i < count else outs[i]

                @when(True if i < count else mine)
                def _():
                    fetch = pltpu.make_async_copy(xs[i], held[i], local.at[i])
                    if t == 0:
                        fetch.start()
                    else:
                        fetch.wait()
                        pltpu.make_async_copy(held[i], out, local.at[i]).start()
    for i in range(k):
        out = outs[i].at[c] if i < count else outs[i]
        when(True if i < count else mine)(pltpu.make_async_copy(held[i], out, local.at[i]).wait)
    for end in ends:
        end()


def gather_ctx(xs, n, cid, cuts=2, spread=None):
    plans = tuple(plan(x.shape[0], cuts) for x in xs)
    shapes = [jax.ShapeDtypeStruct((n,) + x.shape, x.dtype) for x in xs]
    parts = ()
    if spread is not None:
        rows = spread.shape[0]
        half = rows // 32 * 16
        parts = ((0, rows),) if rows % 16 else ((0, half), (half, rows - half))
        xs = xs + [spread]
        shapes = shapes + [jax.ShapeDtypeStruct(spread.shape, spread.dtype)]
    return pl.pallas_call(
        functools.partial(gather_kernel, n, plans, parts),
        out_shape=shapes,
        in_specs=[pl.BlockSpec(memory_space=pl.ANY)] * len(xs),
        out_specs=[pl.BlockSpec(memory_space=pl.ANY)] * len(xs),
        scratch_shapes=[pltpu.VMEM(x.shape, x.dtype) for x in xs]
        + [pltpu.SemaphoreType.DMA((len(xs),))]
        + gather_sems(sum(map(len, plans)))
        + [pltpu.SemaphoreType.DMA((2, 4))],
        compiler_params=pltpu.CompilerParams(
            collective_id=cid, has_side_effects=True, vmem_limit_bytes=60 << 20
        ),
        name=f"gather{cid}",
    )(*xs)


def order_of(p, n):
    if n == 2:
        return (1 - p, p)
    h = p // 2
    return (3 - 3 * h, 2 - h, 1 - p + 4 * h, p)


def reduce_steps(n, part, chunk, bufs, sems):
    n_a, n_b, a, b, f = places(n)
    first, count, swapped = chunk
    g1, g2 = bufs
    s1, r1, s2, r2 = sems
    (p1, n1), (p2, n2) = ((a, n_a), (b, n_b)) if swapped else ((b, n_b), (a, n_a))

    def slot(q1, q2):
        return q1 * n_b + q2 if swapped else q2 * n_b + q1

    rows = pl.ds(first, count)
    from1 = (p1 > 0, p1 < n1 - 1)
    from2 = (p2 > 0, p2 < n2 - 1)
    targets = order_of(p2, n2)

    def has1(d, k):
        return (p1 + k < n1) if d == 0 else (p1 >= k)

    def add(t, got):
        mine = part.at[t, rows]
        mine[...] = (mine[...].astype(f32) + got[...].astype(f32)).astype(mine.dtype)

    def remote(src, dst, send, recv, to):
        return pltpu.make_async_remote_copy(
            src_ref=src, dst_ref=dst, send_sem=send, recv_sem=recv, device_id=(to, f), device_id_type=MESH
        )

    def copy1(j, d, k):
        t = p1 + k if d == 0 else p1 - k
        to = p1 + 1 if d == 0 else p1 - 1
        src = part.at[slot(t, targets[j]), rows]
        return remote(src, g1.at[d, k - 1, j], s1.at[d, k, j], r1.at[d, k - 1, j], slot(to, p2))

    def come1(j, d, k):
        src = part.at[slot(p1, p2), rows]
        return remote(src, g1.at[d, k, j], s1.at[d, k, j], r1.at[d, k, j], slot(p1, p2))

    def copy2(t, d):
        k = t - p2 if d == 0 else p2 - t
        to = p2 + 1 if d == 0 else p2 - 1
        return remote(
            part.at[slot(p1, t), rows], g2.at[d, k - 1], s2.at[d, k], r2.at[d, k - 1], slot(p1, to)
        )

    def come2(d, k):
        src = part.at[slot(p1, p2), rows]
        return remote(src, g2.at[d, k], s2.at[d, k], r2.at[d, k], slot(p1, p2))

    def start(j):
        for d in (0, 1) if j < n2 else ():
            for k in range(n1 - 1, 0, -1):
                when(both(has1(d, k), jnp.logical_not(from1[d])))(
                    lambda d=d, k=k: copy1(j, d, k).start()
                )

    def middle1(j, k):
        for d in (0, 1):

            @when(both(has1(d, k), from1[d]))
            def _():
                come1(j, d, k).wait_recv()
                add(slot(p1 + k if d == 0 else p1 - k, targets[j]), g1.at[d, k, j])
                copy1(j, d, k).start()

    def last1(j):
        for d in (0, 1):

            @when(from1[d])
            def _():
                come1(j, d, 0).wait_recv()
                add(slot(p1, targets[j]), g1.at[d, 0, j])

    def line2(j):
        t = targets[j]
        for d in (0, 1):

            @when((t > p2) if d == 0 else (t < p2))
            def _():
                @when(from2[d])
                def _():
                    k = t - p2 if d == 0 else p2 - t
                    come2(d, k).wait_recv()
                    add(slot(p1, t), g2.at[d, k])

                copy2(t, d).start()

    def last2():
        for d in (0, 1):

            @when(from2[d])
            def _():
                come2(d, 0).wait_recv()
                add(slot(p1, p2), g2.at[d, 0])

    steps = []
    if swapped:
        for k in range(n1 - 2, 0, -1):
            steps.append(lambda k=k: [middle1(j, k) for j in range(n2)])
        steps.append(lambda: [(last1(j), line2(j) if j < n2 - 1 else None) for j in range(n2)])
        steps.append(last2)
    else:

        def item(j):
            for k in range(n1 - 2, 0, -1):
                middle1(j, k)
            last1(j)
            if j < n2 - 1:
                line2(j)

        steps += [functools.partial(item, j) for j in range(n2)] + [last2]

    def finish():
        for j in range(n2):
            for d in (0, 1):
                for k in range(n1 - 1, 0, -1):
                    when(has1(d, k))(lambda j=j, d=d, k=k: copy1(j, d, k).wait_send())
                if j < n2 - 1:
                    t = targets[j]
                    when((t > p2) if d == 0 else (t < p2))(lambda t=t, d=d: copy2(t, d).wait_send())

    return start, steps, finish


def reduce_kernel(n, chunks, nt, x_ref, w_ref, o_ref, part, *refs):
    n_a, n_b, a, b, f = places(n)
    count = len(chunks)
    rows = o_ref.shape[0]
    bufs = [refs[2 * i : 2 * i + 2] for i in range(count)]
    s1, r1, s2, r2 = refs[2 * count :]
    todo = [
        reduce_steps(n, part, chunk, bufs[i], (s1.at[i], r1.at[i], s2.at[i], r2.at[i]))
        for i, chunk in enumerate(chunks)
    ]

    def term(t):
        at = pl.multiple_of(t * rows, rows)
        part[t] = dot(x_ref[pl.ds(at, rows), :], w_ref[...], NT if nt else NN).astype(part.dtype)

    order = order_of(a, n_a)
    greet(a, b, n_a, n_b, f)
    for j in range(n_a):
        for i in range(1, n_b):
            term(order[j] * n_b + (b + i) % n_b)
        for start, _, _ in todo:
            start(j)
    for j in range(n_a):
        term(order[j] * n_b + b)
        for _, steps, _ in todo:
            steps[j]()
    for _, steps, _ in todo:
        steps[n_a]()
    o_ref[...] = part[a * n_b + b]
    for _, _, finish in todo:
        finish()


def reduce_ctx(x, w, n, cid, nt):
    n_a, n_b = LINE, n // LINE
    rows = x.shape[0] // n
    width = w.shape[0] if nt else w.shape[1]
    half = rows // 2
    chunks = ((0, half, False), (half, half, False))
    bufs = []
    for _, count, _ in chunks:
        bufs += [pltpu.VMEM((2, n_b - 1, n_a, count, width), bf16), pltpu.VMEM((2, n_a - 1, count, width), bf16)]
    sem = pltpu.SemaphoreType.DMA
    k = len(chunks)
    return pl.pallas_call(
        functools.partial(reduce_kernel, n, chunks, nt),
        out_shape=jax.ShapeDtypeStruct((rows, width), bf16),
        in_specs=[pl.BlockSpec(memory_space=pltpu.VMEM)] * 2,
        out_specs=pl.BlockSpec(memory_space=pltpu.VMEM),
        scratch_shapes=[pltpu.VMEM((n, rows, width), bf16)] + bufs
        + [sem((k, 2, 4, 4)), sem((k, 2, 4, 4)), sem((k, 2, 4)), sem((k, 2, 4))],
        compiler_params=pltpu.CompilerParams(
            collective_id=cid, has_side_effects=True, vmem_limit_bytes=60 << 20
        ),
        name=f"reduce{cid}",
    )(x, w)


def assemble_rows(parts, ratio, ffs):
    n, rows, w = parts.shape
    each = rows // ratio
    hw = each - ffs

    def body(i_ref, down_ref, out_ref):
        for j in range(ratio):
            down_ref[j * ffs : (j + 1) * ffs, :] = i_ref[0, j * each : j * each + ffs, :].astype(f32)
            out_ref[j * hw : (j + 1) * hw, :] = i_ref[0, j * each + ffs : (j + 1) * each, :].astype(f32)

    return pl.pallas_call(
        body,
        grid=(n,),
        out_shape=[
            jax.ShapeDtypeStruct((ratio * ffs, n * w), f32),
            jax.ShapeDtypeStruct((ratio * hw, n * w), f32),
        ],
        in_specs=[pl.BlockSpec((1, rows, w), lambda i: (i, 0, 0))],
        out_specs=[
            pl.BlockSpec((ratio * ffs, w), lambda i: (0, i)),
            pl.BlockSpec((ratio * hw, w), lambda i: (0, i)),
        ],
        compiler_params=pltpu.CompilerParams(vmem_limit_bytes=60 << 20),
        name="assemble_rows",
    )(parts)


def assemble(parts, n_groups, block=64):
    n, rows, gw = parts.shape
    w = gw // n_groups

    def body(i_ref, o_ref):
        for g in range(n_groups):
            for c in range(n):
                o_ref[:, (g * n + c) * w:(g * n + c + 1) * w] = i_ref[c, :, g * w:(g + 1) * w].astype(jnp.float32)

    return pl.pallas_call(
        body, grid=(rows // block,),
        out_shape=jax.ShapeDtypeStruct((rows, n * gw), jnp.float32),
        in_specs=[pl.BlockSpec((n, block, gw), lambda i: (0, i, 0))],
        out_specs=pl.BlockSpec((block, n * gw), lambda i: (i, 0)),
        compiler_params=pltpu.CompilerParams(vmem_limit_bytes=60 << 20),
        name="assemble")(parts)


def dot(a, b, dims):
    return lax.dot_general(a, b, (dims, ((), ())), preferred_element_type=f32)


NN = ((1,), (0,))
NT = ((1,), (1,))
TN = ((0,), (0,))


def turned(u):
    return pltpu.roll(u, HD // 2, 1)


def masked_probs(q, k, first, at):
    logits = dot(q, k, NT) * (1.0 / math.sqrt(HD))
    keys = lax.broadcasted_iota(jnp.int32, logits.shape, 1)
    queries = lax.broadcasted_iota(jnp.int32, logits.shape, 0) + at
    scaled = jnp.where((keys <= queries) & (keys >= first), logits, masked_score)
    raised = jnp.exp(scaled - jnp.max(scaled, -1, keepdims=True))
    return raised / jnp.sum(raised, -1, keepdims=True)


def attend_kernel(heads, block, n_ref, w_ref, cos_ref, sin_ref, first_ref, q_ref, k_ref, v_ref, o_ref):
    rows = n_ref.shape[0]
    hw = heads * HD
    for at in range(0, rows, block):
        own = slice(at, at + block)
        proj = dot(n_ref[own, :], w_ref[...], NN)
        cos, sin = cos_ref[own, :], sin_ref[own, :]
        for h in range(heads):
            head = slice(h * HD, (h + 1) * HD)
            for ref, base in ((q_ref, 0), (k_ref, hw)):
                u = proj[:, base + h * HD : base + (h + 1) * HD]
                ref[own, head] = (u * cos + turned(u) * sin).astype(bf16)
        v_ref[own, :] = proj[:, 2 * hw :].astype(bf16)
        for h in range(heads):
            head = slice(h * HD, (h + 1) * HD)
            seen = slice(0, at + block)
            probs = masked_probs(q_ref[own, head], k_ref[seen, head], first_ref[own, :], at)
            o_ref[own, head] = dot(probs.astype(bf16), v_ref[seen, head], NN).astype(bf16)


def attend(normed, wq, cos, sin, first, heads, block=256):
    rows = normed.shape[0]
    one = jax.ShapeDtypeStruct((rows, heads * HD), bf16)
    return pl.pallas_call(
        functools.partial(attend_kernel, heads, block),
        out_shape=[one] * 4,
        compiler_params=pltpu.CompilerParams(vmem_limit_bytes=60 << 20),
        name="attend",
    )(normed, wq, cos, sin, first)


def attend_back_kernel(
    heads, block, q_ref, k_ref, v_ref, d_ref, cos_ref, sin_ref, first_ref, o_ref, dk_ref, dv_ref
):
    rows = q_ref.shape[0]
    hw = heads * HD

    def back(w, own):
        return (w * cos_ref[own, :] - turned(w) * sin_ref[own, :]).astype(bf16)

    for h in range(heads):
        head = slice(h * HD, (h + 1) * HD)
        for at in reversed(range(0, rows, block)):
            own = slice(at, at + block)
            seen = slice(0, at + block)
            q, k, v, d = q_ref[own, head], k_ref[seen, head], v_ref[seen, head], d_ref[own, head]
            probs = masked_probs(q, k, first_ref[own, :], at)
            d_probs = dot(d, v, NT)
            inner = jnp.sum(probs * d_probs, -1, keepdims=True)
            d_scores = (probs * (d_probs - inner) * (1.0 / math.sqrt(HD))).astype(bf16)
            o_ref[own, head] = back(dot(d_scores, k, NN), own)
            dk = dot(d_scores, q, TN)
            dv = dot(probs.astype(bf16), d, TN)
            if at + block == rows:
                dk_ref[...] = dk
                dv_ref[...] = dv
            else:
                dk_ref[seen, :] += dk
                dv_ref[seen, :] += dv
        every = slice(0, rows)
        o_ref[:, hw + h * HD : hw + (h + 1) * HD] = back(dk_ref[...], every)
        o_ref[:, 2 * hw + h * HD : 2 * hw + (h + 1) * HD] = dv_ref[...].astype(bf16)


def attend_back(q, k, v, d_mixed, cos, sin, first, heads, block=256):
    rows = q.shape[0]
    return pl.pallas_call(
        functools.partial(attend_back_kernel, heads, block),
        out_shape=jax.ShapeDtypeStruct((rows, 3 * heads * HD), bf16),
        scratch_shapes=[pltpu.VMEM((rows, HD), f32), pltpu.VMEM((rows, HD), f32)],
        compiler_params=pltpu.CompilerParams(vmem_limit_bytes=60 << 20),
        name="attend_back",
    )(q, k, v, d_mixed, cos, sin, first)


def rope_tables(within):
    freq_index = jnp.arange(HD // 2, dtype=f32)
    inverse = rope_base ** (-2.0 * freq_index / HD)
    angles = within.astype(f32)[:, None] * inverse[None, :]
    cos, sin = jnp.cos(angles), jnp.sin(angles)
    return jnp.concatenate([cos, cos], -1), jnp.concatenate([-sin, sin], -1)


def rms_scale(values):
    return lax.rsqrt(jnp.mean(values * values, -1, keepdims=True) + epsilon)


def norm_back(grad_norm, values, scale_rows, gain_float):
    scaled = grad_norm * gain_float[None, :]
    cubed = scale_rows * scale_rows * scale_rows
    return scale_rows * scaled - values * cubed * jnp.mean(scaled * values, -1, keepdims=True)


def shards(
    tokens, cotangent, lengths, deal, norm1_gain, w_qkv, w_out, norm2_gain, w_gate_up, w_down
):
    n_ctx = lax.axis_size("ctx")
    n_fsdp = lax.axis_size("fsdp")
    me = lax.axis_index("ctx")
    mine = lax.axis_index("fsdp")
    rows = tokens.shape[1]
    width = tokens.shape[2]
    piece = rows // n_ctx
    all_rows = rows * n_ctx
    pieces = all_rows // piece
    heads = H // n_ctx
    hw = heads * HD
    kr = w_qkv.shape[0]
    ff = w_gate_up.shape[1] // 2
    ffs = ff // n_ctx
    ff_rows = w_down.shape[0]
    ratio = n_ctx // n_fsdp

    x_own = tokens[0]
    x_all = gather_ctx([x_own], n_ctx, 0)[0].reshape(all_rows, width)

    qkv_own = jnp.concatenate(
        [lax.dynamic_slice(w_qkv, (0, i * width + me * hw), (kr, hw)) for i in range(3)], -1
    )
    wq = lax.all_gather(qkv_own.astype(bf16), "fsdp", axis=0, tiled=True)
    gains = lax.all_gather(
        jnp.stack([norm1_gain, norm2_gain]).astype(bf16), "fsdp", axis=1, tiled=True
    )
    gain_one = gains[0].astype(f32)
    gain_two = gains[1].astype(f32)
    wo = lax.all_gather(w_out.astype(bf16), "fsdp", axis=0, tiled=True)
    wg_own = jnp.concatenate(
        [
            lax.dynamic_slice(w_gate_up, (0, me * ffs), (kr, ffs)),
            lax.dynamic_slice(w_gate_up, (0, ff + me * ffs), (kr, ffs)),
        ],
        -1,
    ).astype(bf16)
    wgu = lax.all_gather(wg_own, "fsdp", axis=0, tiled=True)
    down_own = lax.dynamic_slice(w_down, ((me % ratio) * ffs, 0), (ffs, width)).astype(bf16)
    g_all = gather_ctx([cotangent[0]], n_ctx, 1)[0].reshape(all_rows, width)

    deal_table = deal[0]
    device_index = jnp.arange(n_ctx, dtype=jnp.int32)
    marks = (deal_table[:, :, None] == device_index[None, None, :]).astype(jnp.int32)
    source_piece = jnp.sum(marks * device_index[None, :, None], 1)
    dealt_from = (device_index[None, :] * n_ctx + source_piece.T).reshape(pieces)
    given_from = (deal_table * n_ctx + device_index[:, None]).reshape(pieces)
    own_dealt = lax.dynamic_slice(dealt_from, (me * n_ctx,), (n_ctx,))
    own_given = lax.dynamic_slice(given_from, (me * n_ctx,), (n_ctx,))
    places = jnp.arange(all_rows, dtype=jnp.int32)
    doc_lengths = lengths[0]
    ends = jnp.cumsum(doc_lengths)
    starts = ends - doc_lengths
    docs = jnp.sum((places[:, None] >= ends[None, :]).astype(jnp.int32), -1)
    doc_index = jnp.arange(doc_lengths.shape[0], dtype=jnp.int32)
    firsts = jnp.sum(jnp.where(docs[:, None] == doc_index[None, :], starts[None, :], 0), -1)
    within = places - firsts
    first_key = firsts[:, None]
    cosine_table, sine_table = rope_tables(within)

    x_float = x_all.astype(f32)
    normed_one = (x_float * rms_scale(x_float) * gain_one[None, :]).astype(bf16)
    queries, keys, values, mixed = attend(
        normed_one, wq, cosine_table, sine_table, first_key, heads
    )
    mixed = mixed.reshape(pieces, piece, hw)
    mixed_dealt = jnp.take(mixed, dealt_from, axis=0)
    mixed_own = lax.all_to_all(
        mixed_dealt.reshape(n_ctx, rows, hw), "ctx", split_axis=0, concat_axis=2, tiled=True
    ).reshape(rows, width)
    mixed_dealt = mixed_dealt.reshape(all_rows, hw)

    x_dealt = jnp.take(x_all.reshape(pieces, piece, width), own_dealt, axis=0)
    hidden = x_dealt.reshape(rows, width).astype(f32) + dot(mixed_own, wo, NN)
    scale_two = rms_scale(hidden)
    normed_two = (hidden * scale_two * gain_two[None, :]).astype(bf16)
    n2_all, wd = gather_ctx([normed_two], n_ctx, 2, spread=down_own)
    n2_all = n2_all.reshape(all_rows, width)

    both = dot(n2_all, wgu, NN)
    gate = both[:, :ffs]
    up = both[:, ffs:]
    sigma = jax.nn.sigmoid(gate)
    gate_act = gate * sigma
    activated = (gate_act * up).astype(bf16)
    down_own_rows = reduce_ctx(activated, wd, n_ctx, 4, False)
    block_out = (hidden + down_own_rows.astype(f32)).astype(bf16)[None]

    d_act = dot(g_all, wd, NT)
    d_both = jnp.concatenate(
        [d_act * up * sigma * (1.0 + gate * (1.0 - sigma)), d_act * gate_act], -1
    ).astype(bf16)
    d_two = reduce_ctx(d_both, wgu, n_ctx, 5, True).astype(f32)
    grad_down = dot(activated, g_all, TN).astype(bf16)
    grad_gate_up = dot(n2_all, d_both, TN).astype(bf16)
    row_gate_up = lax.psum_scatter(grad_gate_up, "fsdp", scatter_dimension=0, tiled=True)
    all_gate_up = gather_ctx([row_gate_up], n_ctx, 7)[0]
    final_gate_up = assemble(all_gate_up, 2)

    grad_norm2 = jnp.sum(d_two * hidden * scale_two, 0)
    d_hidden = cotangent[0].astype(f32) + norm_back(d_two, hidden, scale_two, gain_two)
    d_branch = d_hidden.astype(bf16)
    db_all = gather_ctx([d_branch], n_ctx, 3)[0].reshape(all_rows, width)

    grad_out = dot(mixed_dealt, db_all, TN).astype(bf16)
    wo_own = lax.dynamic_slice(wo, (me * hw, 0), (hw, width))
    d_mixed = dot(db_all, wo_own, NT).astype(bf16)
    d_mixed = jnp.take(d_mixed.reshape(pieces, piece, hw), given_from, axis=0)
    d_mixed = d_mixed.reshape(all_rows, hw)
    d_proj = attend_back(
        queries, keys, values, d_mixed, cosine_table, sine_table, first_key, heads
    )
    d_one = reduce_ctx(d_proj, wq, n_ctx, 6, True).astype(f32)
    grad_qkv = dot(normed_one, d_proj, TN).astype(bf16)
    row_qkv = lax.psum_scatter(grad_qkv, "fsdp", scatter_dimension=0, tiled=True)

    own_float = x_own.astype(f32)
    scale_one = rms_scale(own_float)
    grad_norm1 = jnp.sum(d_one * own_float * scale_one, 0)
    dh_own = jnp.take(db_all.reshape(pieces, piece, width), own_given, axis=0)
    dh_own = dh_own.reshape(rows, width).astype(f32)
    grad_tokens = (dh_own + norm_back(d_one, own_float, scale_one, gain_one)).astype(bf16)[None]

    norms = lax.psum_scatter(
        jnp.stack([grad_norm1, grad_norm2]), "fsdp", scatter_dimension=1, tiled=True
    )
    norms = jnp.pad(norms, ((0, 6), (0, 0)))
    all_qkv, all_norms = gather_ctx([row_qkv, norms], n_ctx, 8)
    final_qkv = assemble(all_qkv, 3)
    final_norms = jnp.sum(all_norms, 0)

    grad_rows = jnp.concatenate([grad_down, grad_out], 0)
    col_rows = lax.psum_scatter(grad_rows, "fsdp", scatter_dimension=1, tiled=True)
    all_cols = gather_ctx([col_rows], n_ctx, 9)[0]
    owner_rows = all_cols.reshape(n_fsdp, ratio * (ffs + hw), width // n_fsdp)
    swapped = lax.all_to_all(owner_rows, "fsdp", split_axis=0, concat_axis=0, tiled=True)
    final_down, final_out = assemble_rows(swapped, ratio, ffs)
    return (
        block_out,
        grad_tokens,
        final_norms[0],
        final_qkv,
        final_out,
        final_norms[1],
        final_gate_up,
        final_down,
    )


def solution(mesh):
    in_specs = (
        P("fsdp", "ctx", None),
        P("fsdp", "ctx", None),
        P("fsdp", None),
        P("fsdp", None, None),
        P("fsdp"),
        P("fsdp", None),
        P("fsdp", None),
        P("fsdp"),
        P("fsdp", None),
        P("fsdp", None),
    )
    out_specs = (
        P("fsdp", "ctx", None),
        P("fsdp", "ctx", None),
        P("fsdp"),
        P("fsdp", None),
        P("fsdp", None),
        P("fsdp"),
        P("fsdp", None),
        P("fsdp", None),
    )
    return jax.shard_map(shards, mesh=mesh, in_specs=in_specs, out_specs=out_specs, check_vma=False)
```

time: 1460 us -> 834 us (0.57)
  waiting for transfers between devices: 976 us -> 0.19 us
  Pallas kernels: 0 us -> 683 us
  local copies, waits for them, and re-layouts: 199 us -> 30.1 us
  matrix products: 140 us -> 54.8 us
  blocking collectives: 55.5 us -> 5.78 us
  other arithmetic: 49.7 us -> 29.7 us
    pallas_call x0 -> x15, Pallas kernels: none -> 683 us  [the longest x7 465 us: gather_ctx(): pl.pallas_call(functools.partial(gather_kernel, n, plans, parts), out_sha...]
    all_gather x8 -> x1, waiting for transfers between devices: 542 us -> 0.01 us  [shards(): wq = lax.all_gather(qkv_own.astype(bf16), 'fsdp', axis=0, tiled=True)]
    reduce_scatter x3 -> x0, waiting for transfers between devices: 250 us -> none  [the longest x1 90.7 us: shards(): lax.psum_scatter(down_part, 'ctx', scatter_dimension=0, tiled=True)]
    unnamed x33 -> x30, local copies, waits for them, and re-layouts: 94.7 us -> 2.5 us
    psum x1 -> x0, waiting for transfers between devices: 53.1 us -> none  [shards(): lax.psum(jnp.where(mine == me // ratio, down_own, jnp.zeros_like(down_own...]
    psum x1 -> x0, blocking collectives: 49.5 us -> none  [shards(): sums = lax.psum(jnp.stack([grad_norm1, grad_norm2]), ('ctx', 'fsdp'))]
    dot_general x5 -> x0, matrix products: 43.8 us -> none  [the longest x1 15.4 us: shards(): jnp.einsum('hqk,khd->qhd', d_scores, keys, preferred_element_type=f32)]
    reduce_scatter x1, waiting for transfers between devices: 41.2 us -> 0.01 us  [shards(): lax.psum_scatter(grad_qkv, 'fsdp', scatter_dimension=0, tiled=True)]
  transfers between devices with their start and end apart: 19 -> 9, of which waited for: 17 -> 0; matrix products, arithmetic and copies ran while one was open for 21% -> 9% of each run, Pallas kernels for 0% -> 62%
where the time goes in v3:
time: 834 us; the launch traced here: 830 us
  Pallas kernels  683 us (82%)
  matrix products  54.8 us (7%)
  local copies, waits for them, and re-layouts  30.1 us (4%)
  other arithmetic  29.7 us (4%)
  between operations  15.1 us (2%)
  starting transfers between devices  10.9 us (1%)
    pallas_call x7, Pallas kernels, gather_ctx(): pl.pallas_call(functools.partial(gather_kernel, n, plans, parts), out_sha...  465 us
    pallas_call x3, Pallas kernels, reduce_ctx(): pl.pallas_call(functools.partial(reduce_kernel, n, chunks, nt), out_shape...  163 us
    dot_general x8, matrix products, dot(): return lax.dot_general(a, b, (dims, ((), ())), preferred_element_type=f32)  54.8 us
    pallas_call x2, Pallas kernels, assemble(): pl.pallas_call(body, grid=(rows // block,), out_shape=jax.ShapeDtypeStruc...  22.5 us
  transfers between devices with their start and end apart: 9, of which 0 were waited for; matrix products, arithmetic and copies ran while one was open for 9% of the time, Pallas kernels for 62%

profile of v3, /device:TPU:0, one launch (start us, length us, event | category | flops | bytes accessed | tf_op | source)
XLA Modules:
  0.0 829.7 jit_solution(16728646100520305779)
XLA Ops:
  7.2 1.5 dynamic-slice_convert_fusion.5
  9.7 3.8 convert_element_type.104
  13.6 2.6 dynamic-slice_convert_fusion.2
  16.2 1.5 pad_maximum_fusion.2
  18.7 1.1 copy.51.first_ref
  19.8 49.6 %gather0.1 = bf16[8,128,2048]{2,1,0:T(8,128)(2,1)} custom-call(bf16[128,2048]{1,0:T(8,128)(2,1)} %bitcast.87), custom_call_target="tpu_custom_call" | custom-call | tf_op jit(solution)/shard_map/gather0/pallas_call | solution.py:272
  69.4 5.8 all_gather.12
  75.2 1.9 fusion.27
  77.1 1.3 pad_maximum_fusion.4
  79.3 3.0 fusion.1.n_ref
  82.4 12.4 %attend.1 = (bf16[1024,256]{1,0:T(8,128)(2,1)}, bf16[1024,256]{1,0:T(8,128)(2,1)}, bf16[1024,256]{1,0:T(8,128)(2,1)}, bf16[1024,256]{1,0:T(8,128)(2,1)}) custom-call(bf16[1024,2048]{1,0:T(8,128)(2,1)} %fusion.1.n_ref, bf16[2048,768]{1,0:T(8,128)(2,1)} %all-gather.4.cloned.1.call-done.w_ref, f32[1024,128]{1,0:T(8,128)} %get-tuple-element.65.cos_ref, ...), custom_call_target="tpu_custom_call" | custom-call | tf_op jit(solution)/shard_map/attend/pallas_call | solution.py:566
  94.8 1.6 gather_fusion.1
  97.3 4.7 all-to-all-start
  102.1 54.5 %gather1.1 = bf16[8,128,2048]{2,1,0:T(8,128)(2,1)} custom-call(bf16[128,2048]{1,0:T(8,128)(2,1)} %bitcast.97), custom_call_target="tpu_custom_call" | custom-call | tf_op jit(solution)/shard_map/gather1/pallas_call | solution.py:272
  156.7 2.8 gather_fusion
  159.4 4.6 dynamic-slice_convert_fusion.refs_1_
  164.5 4.7 multiply_reduce_fusion.1
  169.2 1.0 multiply_convert_fusion.1.refs_0_
  170.2 46.6 %gather2.1 = (bf16[8,128,2048]{2,1,0:T(8,128)(2,1)}, bf16[688,2048]{1,0:T(8,128)(2,1)}) custom-call(bf16[128,2048]{1,0:T(8,128)(2,1)} %multiply_convert_fusion.1.refs_0_, bf16[688,2048]{1,0:T(8,128)(2,1)} %dynamic-slice_convert_fusion.refs_1_), custom_call_target="tpu_custom_call" | custom-call | tf_op jit(solution)/shard_map/gather2/pallas_call | solution.py:272
  216.9 10.6 %fusion.31 = f32[1024,1376]{1,0:T(8,128)S(1)} fusion(bf16[1024,2048]{1,0:T(8,128)(2,1)} %bitcast.115, bf16[2048,1376]{1,0:T(8,128)(2,1)} %all-gather.8.cloned.1.call-done.w_ref), kind=kOutput, calls=%fused_computation.110 | convolution fusion | flops 5771362304 | bytes 15466496 | tf_op jit(solution)/shard_map/dot_general | solution.py:522
  227.5 5.7 fusion.4
  233.2 52.7 %reduce4.1 = bf16[128,2048]{1,0:T(8,128)(2,1)} custom-call(bf16[1024,688]{1,0:T(8,128)(2,1)} %get-tuple-element.47.x_ref, bf16[688,2048]{1,0:T(8,128)(2,1)} %get-tuple-element.22.w_ref), custom_call_target="tpu_custom_call" | custom-call | tf_op jit(solution)/shard_map/reduce4/pallas_call | solution.py:462
  285.9 7.5 convolution_convert_fusion.2
  293.4 2.5 pad_maximum_fusion.1.x_ref
  295.8 59.6 %reduce5.1 = bf16[128,2048]{1,0:T(8,128)(2,1)} custom-call(bf16[1024,1376]{1,0:T(8,128)(2,1)} %pad_maximum_fusion.1.x_ref, bf16[2048,1376]{1,0:T(8,128)(2,1)} %all-gather.8.cloned.1.call-done.w_ref), custom_call_target="tpu_custom_call" | custom-call | tf_op jit(solution)/shard_map/reduce5/pallas_call | solution.py:462
  355.4 1.4 fusion.18
  356.8 2.4 fusion.15
  359.2 46.2 %gather3.1 = bf16[8,128,2048]{2,1,0:T(8,128)(2,1)} custom-call(bf16[128,2048]{1,0:T(8,128)(2,1)} %get-tuple-element.48.refs_0_), custom_call_target="tpu_custom_call" | custom-call | tf_op jit(solution)/shard_map/gather3/pallas_call | solution.py:272
  405.4 3.8 convolution_convert_fusion.3
  409.2 2.4 pad_maximum_fusion
  412.0 3.8 convolution_convert_fusion.4
  417.3 11.2 %attend_back.1.x_ref = bf16[1024,768]{1,0:T(8,128)(2,1)} custom-call(bf16[1024,256]{1,0:T(8,128)(2,1)} %get-tuple-element.23.q_ref, bf16[1024,256]{1,0:T(8,128)(2,1)} %get-tuple-element.24.k_ref, bf16[1024,256]{1,0:T(8,128)(2,1)} %get-tuple-element.25.v_ref, bf16[1024,256]{1,0:T(8,128)(2,1)} %bitcast.96, f32[1024,128]{1,0:T(8,128)} %get-tuple-element.65.cos_ref, ...), custom_call_target="tpu_custom_call" | custom-call | tf_op jit(solution)/shard_map/attend_back/pallas_call | solution.py:609
  428.5 51.2 %reduce6.1 = bf16[128,2048]{1,0:T(8,128)(2,1)} custom-call(bf16[1024,768]{1,0:T(8,128)(2,1)} %attend_back.1.x_ref, bf16[2048,768]{1,0:T(8,128)(2,1)} %all-gather.4.cloned.1.call-done.w_ref), custom_call_target="tpu_custom_call" | custom-call | tf_op jit(solution)/shard_map/reduce6/pallas_call | solution.py:462
  479.7 1.4 fusion.23
  481.1 1.4 copy.60
  482.6 8.1 convolution_convert_fusion.1
  491.0 10.7 %convolution_convert_fusion = bf16[2048,1376]{0,1:T(8,128)(2,1)} fusion(bf16[1024,2048]{1,0:T(8,128)(2,1)} %bitcast.116, bf16[1024,1376]{1,0:T(8,128)(2,1)S(1)} %copy-done.1), kind=kOutput, calls=%fused_computation.8 | convolution fusion | flops 5774180352 | bytes 12648448 | tf_op jit(solution)/shard_map/dot_general | solution.py:522
  501.6 8.3 %copy.57 = bf16[2048,1376]{1,0:T(8,128)(2,1)} copy(bf16[2048,1376]{0,1:T(8,128)(2,1)} %convolution_convert_fusion) | data formatting | bytes 11272192 | tf_op jit(solution)/shard_map/convert_element_type | solution.py:733
  510.0 78.7 %gather9.1 = bf16[8,944,512]{2,1,0:T(8,128)(2,1)} custom-call(bf16[944,512]{1,0:T(8,128)(2,1)} %reduce-scatter.9.cloned.1.call-done.refs_0_), custom_call_target="tpu_custom_call" | custom-call | tf_op jit(solution)/shard_map/gather9/pallas_call | solution.py:272
  588.7 5.7 all-to-all-start.1
  594.4 2.8 gather_fusion.2
  597.4 1.3 fusion.26
  598.7 1.1 copy.61
  600.3 70.7 %gather8.1 = (bf16[8,512,768]{2,1,0:T(8,128)(2,1)}, f32[8,8,512]{2,1,0:T(8,128)}) custom-call(bf16[512,768]{1,0:T(8,128)(2,1)} %reduce-scatter.7.cloned.1.call-done.refs_0_, f32[8,512]{1,0:T(8,128)} %pad.4.refs_1_), custom_call_target="tpu_custom_call" | custom-call | tf_op jit(solution)/shard_map/gather8/pallas_call | solution.py:272
  672.0 8.8 %assemble.2 = f32[512,6144]{1,0:T(8,128)} custom-call(bf16[8,512,768]{2,1,0:T(8,128)(2,1)} %get-tuple-element.27.i_ref), custom_call_target="tpu_custom_call" | custom-call | tf_op jit(solution)/shard_map/assemble/pallas_call | solution.py:512
  681.4 118.3 %gather7.1.i_ref = bf16[8,512,1376]{2,1,0:T(8,128)(2,1)} custom-call(bf16[512,1376]{1,0:T(8,128)(2,1)} %reduce-scatter.11.cloned.1.call-done.refs_0_), custom_call_target="tpu_custom_call" | custom-call | tf_op jit(solution)/shard_map/gather7/pallas_call | solution.py:272
  799.7 13.7 %assemble.3 = f32[512,11008]{1,0:T(8,128)} custom-call(bf16[8,512,1376]{2,1,0:T(8,128)(2,1)} %gather7.1.i_ref), custom_call_target="tpu_custom_call" | custom-call | tf_op jit(solution)/shard_map/assemble/pallas_call | solution.py:512
  813.4 9.0 %assemble_rows.1 = (f32[1376,2048]{1,0:T(8,128)}, f32[512,2048]{1,0:T(8,128)}) custom-call(bf16[4,1888,512]{2,1,0:T(8,128)(2,1)} %all-to-all-done.1.i_ref), custom_call_target="tpu_custom_call" | custom-call | tf_op jit(solution)/shard_map/assemble_rows/pallas_call | solution.py:486
  (99 shorter events, 9.0 us)
Async XLA Ops:
  7.2 75.2 %all-gather.4.cloned.1.call-start = ((), (), s32[]{:S(2)}) async-start(), calls=%async_computation.6 | async-start | bytes 3932160 | tf_op jit(solution)/shard_map/all_gather | solution.py:662
  9.6 154.8 %all-gather.6.cloned.1.call-start = ((), (), s32[]{:S(2)}) async-start(), calls=%async_computation.7 | async-start | bytes 10485760 | tf_op jit(solution)/shard_map/all_gather | solution.py:668
  13.5 4.2 copy-start.13
  13.5 4.4 copy-start.11
  13.6 4.4 copy-start.12
  13.6 4.4 copy-start.10
  13.6 203.2 %all-gather.8.cloned.1.call-start = ((), (), s32[]{:S(2)}) async-start(), calls=%async_computation.8 | async-start | bytes 7208960 | tf_op jit(solution)/shard_map/all_gather | solution.py:676
  69.3 9.1 %copy-start = (bf16[8,128,2048]{2,1,0:T(8,128)(2,1)S(1)}, bf16[8,128,2048]{2,1,0:T(8,128)(2,1)}, u32[]{:S(2)}) copy-start(bf16[8,128,2048]{2,1,0:T(8,128)(2,1)} %gather0.1) | copy-start | bytes 12582916
  97.3 66.8 %all-to-all-start = ((bf16[8,128,256]{2,1,0:T(8,128)(2,1)}), bf16[8,128,256]{2,1,0:T(8,128)(2,1)S(1)}, u32[]{:S(2)}, u32[]{:S(2)}) async-start(bf16[8,128,256]{2,1,0:T(8,128)(2,1)} %bitcast.14), calls=%async_computation | async-start | bytes 1048576 | tf_op jit(solution)/shard_map/all_to_all | solution.py:706
  102.0 408.0 %reduce-scatter.9.cloned.1.call-start = ((), (), s32[]{:S(2)}) async-start(), calls=%async_computation.10 | async-start | bytes 4833280 | tf_op jit(solution)/shard_map/reduce_scatter | solution.py:771
  216.8 10.6 %copy-start.4 = (bf16[8,128,2048]{2,1,0:T(8,128)(2,1)S(1)}, bf16[8,128,2048]{2,1,0:T(8,128)(2,1)}, u32[]{:S(2)}) copy-start(bf16[8,128,2048]{2,1,0:T(8,128)(2,1)} %gather1.1) | copy-start | bytes 12582916
  216.8 10.6 %copy-start.5 = (bf16[688,2048]{1,0:T(8,128)(2,1)S(1)}, bf16[688,2048]{1,0:T(8,128)(2,1)}, u32[]{:S(2)}) copy-start(bf16[688,2048]{1,0:T(8,128)(2,1)} %get-tuple-element.22.w_ref) | copy-start | bytes 8454148
  285.9 7.5 copy-start.9
  295.8 61.0 %copy-start.7 = (bf16[1,128,2048]{2,1,0:T(8,128)(2,1)S(1)}, bf16[1,128,2048]{2,1,0:T(8,128)(2,1)}, u32[]{:S(2)}) copy-start(bf16[1,128,2048]{2,1,0:T(8,128)(2,1)} %param.15) | copy-start | bytes 1572868
  295.8 61.0 %copy-start.8 = (bf16[128,2048]{1,0:T(8,128)(2,1)S(1)}, bf16[128,2048]{1,0:T(8,128)(2,1)}, u32[]{:S(2)}) copy-start(bf16[128,2048]{1,0:T(8,128)(2,1)} %reduce4.1) | copy-start | bytes 1572868
  405.4 3.8 copy-start.6
  409.2 2.5 copy-start.2
  411.7 187.0 %reduce-scatter.13.cloned.1.call-start = ((), (), s32[]{:S(2)}) async-start(), calls=%async_computation.12 | async-start | bytes 1310720
  482.5 8.5 %copy-start.1 = (bf16[1024,1376]{1,0:T(8,128)(2,1)S(1)}, bf16[1024,1376]{1,0:T(8,128)(2,1)}, u32[]{:S(2)}) copy-start(bf16[1024,1376]{1,0:T(8,128)(2,1)} %pad_maximum_fusion.1.x_ref) | copy-start | bytes 8454148
  482.5 117.8 %reduce-scatter.7.cloned.1.call-start = ((), (), s32[]{:S(2)}) async-start(), calls=%async_computation.9 | async-start | bytes 3932160 | tf_op jit(solution)/shard_map/reduce_scatter | solution.py:753
  490.7 190.7 %reduce-scatter.11.cloned.1.call-start = ((), (), s32[]{:S(2)}) async-start(), calls=%async_computation.11 | async-start | bytes 7208960 | tf_op jit(solution)/shard_map/reduce_scatter | solution.py:734
  588.7 8.7 %copy-start.3 = (bf16[128,2048]{1,0:T(8,128)(2,1)S(1)}, bf16[128,2048]{1,0:T(8,128)(2,1)}, u32[]{:S(2)}) copy-start(bf16[128,2048]{1,0:T(8,128)(2,1)} %reduce6.1) | copy-start | bytes 1572868
  588.7 224.7 %all-to-all-start.1 = ((bf16[4,1888,512]{2,1,0:T(8,128)(2,1)}), bf16[4,1888,512]{2,1,0:T(8,128)(2,1)}, u32[]{:S(2)}, u32[]{:S(2)}) async-start(bf16[4,1888,512]{2,1,0:T(8,128)(2,1)} %bitcast.86), calls=%async_computation.3 | async-start | bytes 15466496 | tf_op jit(solution)/shard_map/all_to_all | solution.py:774
Sparse Core Ops, SparseCore 0:
  10.1 31.2 all-gather.3
  43.5 58.3 all-gather.5
  104.0 43.3 all-gather.7
  411.8 41.0 reduce-scatter.8
  482.6 23.3 reduce-scatter.12
  508.4 37.9 reduce-scatter.6
  549.6 60.2 reduce-scatter.10

commit v4 on v3

--- a/solution.py
+++ b/solution.py
@@ -34,15 +34,12 @@
     high = (2 * n_a - 2 - a) // n_a + (2 * n_b - 2 - b) // n_b
     total = low + high
     if fsdp:
-        n_y = lax.axis_size("fsdp") // 2
-        y, core = f // 2, f % 2
-        for cond, to in ((y > 0, f - 2), (y < n_y - 1, f + 2), (True, f + 1 - 2 * core)):
-            when(cond)(
-                lambda to=to: pl.semaphore_signal(
-                    bar, inc=1, device_id=(a * n_b + b, to), device_id_type=MESH
-                )
+        n_f = lax.axis_size("fsdp")
+        for m in range(1, n_f):
+            pl.semaphore_signal(
+                bar, inc=1, device_id=(a * n_b + b, (f + m) % n_f), device_id_type=MESH
             )
-        total = total + 1 + (y + n_y - 1) // n_y + (2 * n_y - 2 - y) // n_y
+        total = total + n_f - 1
     pl.semaphore_wait(bar, total)
 
 
@@ -285,6 +282,113 @@
     )(*xs)
 
 
+def cast_rows(src, dst):
+    rows = src.shape[0]
+    if rows % 16:
+        dst[...] = src[...].astype(dst.dtype)
+        return
+
+    def one(i, carry):
+        at = pl.ds(pl.multiple_of(i * 16, 16), 16)
+        dst[at, :] = src[at, :].astype(dst.dtype)
+        return carry
+
+    lax.fori_loop(0, rows // 16, one, 0)
+
+
+def first_kernel(n, chunks, ratio, *refs):
+    x, wo, wd, g, out, wo_out, wd_out, g_out = refs[:8]
+    held, wo_wide, wo_low, wd_wide, wd_low, g_held, local, s1, r1, s2, r2, gs, gr = refs[8:]
+    n_a, n_b, a, b, f = places(n)
+    c = a * n_b + b
+    n_f = lax.axis_size("fsdp")
+    ffs = wd_low.shape[0]
+    own = pl.ds(pl.multiple_of((c % ratio) * ffs, 8), ffs)
+    loads = [
+        pltpu.make_async_copy(src, dst, local.at[i])
+        for i, (src, dst) in enumerate(((x, held), (wo, wo_wide), (wd.at[own], wd_wide), (g, g_held)))
+    ]
+    stores = [
+        pltpu.make_async_copy(src, dst, local.at[i])
+        for i, (src, dst) in enumerate(
+            ((held, out.at[c]), (wo_low, wo_out), (wd_low, wd_out), (g_held, g_out.at[f]))
+        )
+    ]
+    for copy in loads:
+        copy.start()
+    greet(a, b, n_a, n_b, f, True)
+    steps, ends = [], []
+    for i, chunk in enumerate(chunks):
+        more, end = gather_steps(n, x, out, chunk, (s1.at[i], r1.at[i], s2.at[i], r2.at[i]))
+        steps.append(more)
+        ends.append(end)
+
+    def gain(m):
+        return pltpu.make_async_remote_copy(
+            src_ref=g,
+            dst_ref=g_out.at[f],
+            send_sem=gs.at[m],
+            recv_sem=gr.at[m],
+            device_id=(c, (f + m) % n_f),
+            device_id_type=MESH,
+        )
+
+    for t in range(n_a + n_b - 1):
+        for more in steps:
+            if t < len(more):
+                more[t]()
+        if t == 0:
+            for m in range(1, n_f):
+                gain(m).start()
+            loads[0].wait()
+            stores[0].start()
+            loads[3].wait()
+            stores[3].start()
+            loads[1].wait()
+            cast_rows(wo_wide, wo_low)
+            stores[1].start()
+        if t == 1:
+            loads[2].wait()
+            cast_rows(wd_wide, wd_low)
+            stores[2].start()
+    for copy in stores:
+        copy.wait()
+    for m in range(1, n_f):
+        gain(m).wait()
+    for end in ends:
+        end()
+
+
+def gather_first(x, w_out, w_down, gains, n, ratio, ffs, cid):
+    n_f = lax.axis_size("fsdp")
+    chunks = plan(x.shape[0])
+    low = [jax.ShapeDtypeStruct(w_out.shape, bf16), jax.ShapeDtypeStruct((ffs, w_down.shape[1]), bf16)]
+    sem = pltpu.SemaphoreType.DMA
+    return pl.pallas_call(
+        functools.partial(first_kernel, n, chunks, ratio),
+        out_shape=[jax.ShapeDtypeStruct((n,) + x.shape, x.dtype)]
+        + low
+        + [jax.ShapeDtypeStruct((n_f,) + gains.shape, gains.dtype)],
+        in_specs=[pl.BlockSpec(memory_space=pl.ANY)] * 4,
+        out_specs=[pl.BlockSpec(memory_space=pl.ANY)] * 4,
+        scratch_shapes=[
+            pltpu.VMEM(x.shape, x.dtype),
+            pltpu.VMEM(w_out.shape, f32),
+            pltpu.VMEM(w_out.shape, bf16),
+            pltpu.VMEM((ffs, w_down.shape[1]), f32),
+            pltpu.VMEM((ffs, w_down.shape[1]), bf16),
+            pltpu.VMEM(gains.shape, gains.dtype),
+            sem((4,)),
+        ]
+        + gather_sems(len(chunks))
+        + [sem((n_f,)), sem((n_f,))],
+        compiler_params=pltpu.CompilerParams(
+            collective_id=cid, has_side_effects=True, vmem_limit_bytes=60 << 20
+        ),
+        name=f"gather{cid}",
+    )(x, w_out, w_down, gains)
+
+
 def order_of(p, n):
     if n == 2:
         return (1 - p, p)
@@ -319,15 +423,18 @@
             src_ref=src, dst_ref=dst, send_sem=send, recv_sem=recv, device_id=(to, f), device_id_type=MESH
         )
 
+    def side1(d):
+        return d if n1 > 2 else 0
+
     def copy1(j, d, k):
         t = p1 + k if d == 0 else p1 - k
         to = p1 + 1 if d == 0 else p1 - 1
         src = part.at[slot(t, targets[j]), rows]
-        return remote(src, g1.at[d, k - 1, j], s1.at[d, k, j], r1.at[d, k - 1, j], slot(to, p2))
+        return remote(src, g1.at[side1(d), k - 1, j], s1.at[d, k, j], r1.at[d, k - 1, j], slot(to, p2))
 
     def come1(j, d, k):
         src = part.at[slot(p1, p2), rows]
-        return remote(src, g1.at[d, k, j], s1.at[d, k, j], r1.at[d, k, j], slot(p1, p2))
+        return remote(src, g1.at[side1(d), k, j], s1.at[d, k, j], r1.at[d, k, j], slot(p1, p2))
 
     def copy2(t, d):
         k = t - p2 if d == 0 else p2 - t
@@ -353,7 +460,7 @@
             @when(both(has1(d, k), from1[d]))
             def _():
                 come1(j, d, k).wait_recv()
-                add(slot(p1 + k if d == 0 else p1 - k, targets[j]), g1.at[d, k, j])
+                add(slot(p1 + k if d == 0 else p1 - k, targets[j]), g1.at[side1(d), k, j])
                 copy1(j, d, k).start()
 
     def last1(j):
@@ -362,7 +469,7 @@
             @when(from1[d])
             def _():
                 come1(j, d, 0).wait_recv()
-                add(slot(p1, targets[j]), g1.at[d, 0, j])
+                add(slot(p1, targets[j]), g1.at[side1(d), 0, j])
 
     def line2(j):
         t = targets[j]
@@ -415,62 +522,114 @@
     return start, steps, finish
 
 
-def reduce_kernel(n, chunks, nt, x_ref, w_ref, o_ref, part, *refs):
+def reduce_kernel(n, chunks, jobs, extras, count, *refs):
     n_a, n_b, a, b, f = places(n)
-    count = len(chunks)
-    rows = o_ref.shape[0]
-    bufs = [refs[2 * i : 2 * i + 2] for i in range(count)]
-    s1, r1, s2, r2 = refs[2 * count :]
-    todo = [
-        reduce_steps(n, part, chunk, bufs[i], (s1.at[i], r1.at[i], s2.at[i], r2.at[i]))
-        for i, chunk in enumerate(chunks)
-    ]
-
-    def term(t):
+    k, e = len(jobs), len(extras)
+    hbm, rest = refs[:count], refs[count:]
+    o_refs, p_refs, rest = rest[:k], rest[k : k + e], rest[k + e :]
+    held, parts, made, rest = rest[:count], rest[count : count + k], rest[count + k : count + k + e], rest[count + k + e :]
+    cuts = len(chunks)
+    bufs, rest = rest[: 2 * k * cuts], rest[2 * k * cuts :]
+    load, stored, s1, r1, s2, r2 = rest
+    rows = o_refs[0].shape[0]
+    first = sorted({i for x, w, _ in jobs for i in (x, w)})
+    order_in = first + [i for i in range(count) if i not in first]
+    loads = [pltpu.make_async_copy(hbm[i], held[i], load.at[i]) for i in range(count)]
+    for i in order_in:
+        loads[i].start()
+    todo = []
+    for i in range(k):
+        for m, chunk in enumerate(chunks):
+            at = i * cuts + m
+            sems = (s1.at[at], r1.at[at], s2.at[at], r2.at[at])
+            todo.append(reduce_steps(n, parts[i], chunk, bufs[2 * at : 2 * at + 2], sems))
+
+    def term(i, t):
+        x, w, nt = jobs[i]
         at = pl.multiple_of(t * rows, rows)
-        part[t] = dot(x_ref[pl.ds(at, rows), :], w_ref[...], NT if nt else NN).astype(part.dtype)
+        parts[i][t] = dot(held[x][pl.ds(at, rows), :], held[w][...], NT if nt else NN).astype(bf16)
+
+    tiles, stores = [], []
+    for i, (x, y) in enumerate(extras):
+        high = held[x].shape[1]
+        for lo in range(0, high, 256):
+            hi = min(lo + 256, high)
+
+            def tile(i=i, x=x, y=y, lo=lo, hi=hi):
+                made[i][lo:hi, :] = dot(held[x][:, lo:hi], held[y][...], TN).astype(bf16)
+
+            tiles.append(tile)
+        stores.append((len(tiles), i))
 
     order = order_of(a, n_a)
     greet(a, b, n_a, n_b, f)
+    for i in first:
+        loads[i].wait()
     for j in range(n_a):
-        for i in range(1, n_b):
-            term(order[j] * n_b + (b + i) % n_b)
-        for start, _, _ in todo:
-            start(j)
+        for i in range(k):
+            for m in range(1, n_b):
+                term(i, order[j] * n_b + (b + m) % n_b)
+            for start, _, _ in todo[i * cuts : (i + 1) * cuts]:
+                start(j)
+    for i in order_in[len(first) :]:
+        loads[i].wait()
+    done = 0
     for j in range(n_a):
-        term(order[j] * n_b + b)
+        for i in range(k):
+            term(i, order[j] * n_b + b)
+        upto = len(tiles) * (j + 1) // n_a
+        for at in range(done, upto):
+            tiles[at]()
+            for last, i in stores:
+                if last == at + 1:
+                    pltpu.make_async_copy(made[i], p_refs[i], stored.at[i]).start()
+        done = upto
         for _, steps, _ in todo:
             steps[j]()
     for _, steps, _ in todo:
         steps[n_a]()
-    o_ref[...] = part[a * n_b + b]
+    for i in range(k):
+        o_refs[i][...] = parts[i][a * n_b + b]
     for _, _, finish in todo:
         finish()
-
-
-def reduce_ctx(x, w, n, cid, nt):
+    for i in range(e):
+        pltpu.make_async_copy(made[i], p_refs[i], stored.at[i]).wait()
+
+
+def reduce_ctx(arrays, jobs, extras, n, cid):
     n_a, n_b = LINE, n // LINE
-    rows = x.shape[0] // n
-    width = w.shape[0] if nt else w.shape[1]
+    rows = arrays[jobs[0][0]].shape[0] // n
     half = rows // 2
     chunks = ((0, half, False), (half, half, False))
+    widths = [arrays[w].shape[0 if nt else 1] for _, w, nt in jobs]
     bufs = []
-    for _, count, _ in chunks:
-        bufs += [pltpu.VMEM((2, n_b - 1, n_a, count, width), bf16), pltpu.VMEM((2, n_a - 1, count, width), bf16)]
+    for width in widths:
+        for _, count, _ in chunks:
+            bufs += [
+                pltpu.VMEM((min(2, n_b - 1), n_b - 1, n_a, count, width), bf16),
+                pltpu.VMEM((2, n_a - 1, count, width), bf16),
+            ]
+    made = [(arrays[x].shape[1], arrays[y].shape[1]) for x, y in extras]
     sem = pltpu.SemaphoreType.DMA
-    k = len(chunks)
+    k = len(jobs) * len(chunks)
     return pl.pallas_call(
-        functools.partial(reduce_kernel, n, chunks, nt),
-        out_shape=jax.ShapeDtypeStruct((rows, width), bf16),
-        in_specs=[pl.BlockSpec(memory_space=pltpu.VMEM)] * 2,
-        out_specs=pl.BlockSpec(memory_space=pltpu.VMEM),
-        scratch_shapes=[pltpu.VMEM((n, rows, width), bf16)] + bufs
+        functools.partial(reduce_kernel, n, chunks, jobs, extras, len(arrays)),
+        out_shape=[jax.ShapeDtypeStruct((rows, width), bf16) for width in widths]
+        + [jax.ShapeDtypeStruct(shape, bf16) for shape in made],
+        in_specs=[pl.BlockSpec(memory_space=pl.ANY)] * len(arrays),
+        out_specs=[pl.BlockSpec(memory_space=pltpu.VMEM)] * len(widths)
+        + [pl.BlockSpec(memory_space=pl.ANY)] * len(made),
+        scratch_shapes=[pltpu.VMEM(x.shape, x.dtype) for x in arrays]
+        + [pltpu.VMEM((n, rows, width), bf16) for width in widths]
+        + [pltpu.VMEM(shape, bf16) for shape in made]
+        + bufs
+        + [sem((len(arrays),)), sem((max(1, len(made)),))]
         + [sem((k, 2, 4, 4)), sem((k, 2, 4, 4)), sem((k, 2, 4)), sem((k, 2, 4))],
         compiler_params=pltpu.CompilerParams(
             collective_id=cid, has_side_effects=True, vmem_limit_bytes=60 << 20
         ),
         name=f"reduce{cid}",
-    )(x, w)
+    )(*arrays)
 
 
 def assemble_rows(parts, ratio, ffs):
@@ -654,18 +813,19 @@
     ratio = n_ctx // n_fsdp
 
     x_own = tokens[0]
-    x_all = gather_ctx([x_own], n_ctx, 0)[0].reshape(all_rows, width)
+    gains = jnp.pad(jnp.stack([norm1_gain, norm2_gain]), ((0, 6), (0, 0)))
+    x_all, wo_own, down_own, gains = gather_first(
+        x_own, w_out, w_down, gains, n_ctx, ratio, ffs, 0
+    )
+    x_all = x_all.reshape(all_rows, width)
 
     qkv_own = jnp.concatenate(
         [lax.dynamic_slice(w_qkv, (0, i * width + me * hw), (kr, hw)) for i in range(3)], -1
     )
     wq = lax.all_gather(qkv_own.astype(bf16), "fsdp", axis=0, tiled=True)
-    gains = lax.all_gather(
-        jnp.stack([norm1_gain, norm2_gain]).astype(bf16), "fsdp", axis=1, tiled=True
-    )
-    gain_one = gains[0].astype(f32)
-    gain_two = gains[1].astype(f32)
-    wo = lax.all_gather(w_out.astype(bf16), "fsdp", axis=0, tiled=True)
+    gain_one = gains[:, 0].reshape(width).astype(bf16).astype(f32)
+    gain_two = gains[:, 1].reshape(width).astype(bf16).astype(f32)
+    wo = lax.all_gather(wo_own, "fsdp", axis=0, tiled=True)
     wg_own = jnp.concatenate(
         [
             lax.dynamic_slice(w_gate_up, (0, me * ffs), (kr, ffs)),
@@ -674,7 +834,6 @@
         -1,
     ).astype(bf16)
     wgu = lax.all_gather(wg_own, "fsdp", axis=0, tiled=True)
-    down_own = lax.dynamic_slice(w_down, ((me % ratio) * ffs, 0), (ffs, width)).astype(bf16)
     g_all = gather_ctx([cotangent[0]], n_ctx, 1)[0].reshape(all_rows, width)
 
     deal_table = deal[0]
@@ -721,19 +880,26 @@
     sigma = jax.nn.sigmoid(gate)
     gate_act = gate * sigma
     activated = (gate_act * up).astype(bf16)
-    down_own_rows = reduce_ctx(activated, wd, n_ctx, 4, False)
-    block_out = (hidden + down_own_rows.astype(f32)).astype(bf16)[None]
 
     d_act = dot(g_all, wd, NT)
     d_both = jnp.concatenate(
         [d_act * up * sigma * (1.0 + gate * (1.0 - sigma)), d_act * gate_act], -1
     ).astype(bf16)
-    d_two = reduce_ctx(d_both, wgu, n_ctx, 5, True).astype(f32)
-    grad_down = dot(activated, g_all, TN).astype(bf16)
-    grad_gate_up = dot(n2_all, d_both, TN).astype(bf16)
+    if n_ctx == 8:
+        arrays = [activated, wd, d_both, wgu, n2_all, g_all]
+        down_rows, d_two, grad_gate_up, grad_down = reduce_ctx(
+            arrays, ((0, 1, False), (2, 3, True)), ((4, 2), (0, 5)), n_ctx, 4
+        )
+    else:
+        down_rows, grad_down = reduce_ctx(
+            [activated, wd, g_all], ((0, 1, False),), ((0, 2),), n_ctx, 4
+        )
+        d_two, grad_gate_up = reduce_ctx(
+            [d_both, wgu, n2_all], ((0, 1, True),), ((2, 0),), n_ctx, 5
+        )
+    d_two = d_two.astype(f32)
+    block_out = (hidden + down_rows.astype(f32)).astype(bf16)[None]
     row_gate_up = lax.psum_scatter(grad_gate_up, "fsdp", scatter_dimension=0, tiled=True)
-    all_gate_up = gather_ctx([row_gate_up], n_ctx, 7)[0]
-    final_gate_up = assemble(all_gate_up, 2)
 
     grad_norm2 = jnp.sum(d_two * hidden * scale_two, 0)
     d_hidden = cotangent[0].astype(f32) + norm_back(d_two, hidden, scale_two, gain_two)
@@ -741,15 +907,15 @@
     db_all = gather_ctx([d_branch], n_ctx, 3)[0].reshape(all_rows, width)
 
     grad_out = dot(mixed_dealt, db_all, TN).astype(bf16)
-    wo_own = lax.dynamic_slice(wo, (me * hw, 0), (hw, width))
-    d_mixed = dot(db_all, wo_own, NT).astype(bf16)
+    wo_rows = lax.dynamic_slice(wo, (me * hw, 0), (hw, width))
+    d_mixed = dot(db_all, wo_rows, NT).astype(bf16)
     d_mixed = jnp.take(d_mixed.reshape(pieces, piece, hw), given_from, axis=0)
     d_mixed = d_mixed.reshape(all_rows, hw)
     d_proj = attend_back(
         queries, keys, values, d_mixed, cosine_table, sine_table, first_key, heads
     )
-    d_one = reduce_ctx(d_proj, wq, n_ctx, 6, True).astype(f32)
-    grad_qkv = dot(normed_one, d_proj, TN).astype(bf16)
+    d_one, grad_qkv = reduce_ctx([d_proj, wq, normed_one], ((0, 1, True),), ((2, 0),), n_ctx, 6)
+    d_one = d_one.astype(f32)
     row_qkv = lax.psum_scatter(grad_qkv, "fsdp", scatter_dimension=0, tiled=True)
 
     own_float = x_own.astype(f32)
@@ -763,15 +929,18 @@
         jnp.stack([grad_norm1, grad_norm2]), "fsdp", scatter_dimension=1, tiled=True
     )
     norms = jnp.pad(norms, ((0, 6), (0, 0)))
-    all_qkv, all_norms = gather_ctx([row_qkv, norms], n_ctx, 8)
-    final_qkv = assemble(all_qkv, 3)
-    final_norms = jnp.sum(all_norms, 0)
 
     grad_rows = jnp.concatenate([grad_down, grad_out], 0)
+    grad_rows, row_gate_up = lax.optimization_barrier((grad_rows, row_gate_up))
     col_rows = lax.psum_scatter(grad_rows, "fsdp", scatter_dimension=1, tiled=True)
     all_cols = gather_ctx([col_rows], n_ctx, 9)[0]
     owner_rows = all_cols.reshape(n_fsdp, ratio * (ffs + hw), width // n_fsdp)
     swapped = lax.all_to_all(owner_rows, "fsdp", split_axis=0, concat_axis=0, tiled=True)
+    row_gate_up, all_cols = lax.optimization_barrier((row_gate_up, all_cols))
+    all_gate_up, all_qkv, all_norms = gather_ctx([row_gate_up, row_qkv, norms], n_ctx, 8)
+    final_gate_up = assemble(all_gate_up, 2)
+    final_qkv = assemble(all_qkv, 3)
+    final_norms = jnp.sum(all_norms, 0)
     final_down, final_out = assemble_rows(swapped, ratio, ffs)
     return (
         block_out,

time: 834 us -> 782 us (0.938)
  matrix products: 54.8 us -> 28.4 us
  Pallas kernels: 683 us -> 669 us
  local copies, waits for them, and re-layouts: 30.1 us -> 18.1 us
  waiting for transfers between devices: 0.19 us -> 11.2 us
    pallas_call x7 -> x5, Pallas kernels: 465 us -> 413 us  [gather_ctx(): pl.pallas_call(functools.partial(gather_kernel, n, plans, parts), out_sha...]
    pallas_call x3, Pallas kernels: 163 us -> 202 us  [the longest x2 152 us: reduce_ctx(): pl.pallas_call(functools.partial(reduce_kernel, n, chunks, jobs, extras,...]
    dot_general x8 -> x5, matrix products: 54.8 us -> 28.4 us  [dot(): return lax.dot_general(a, b, (dims, ((), ())), preferred_element_type=f32)]
    convert_element_type x2 -> x0, local copies, waits for them, and re-layouts: 12.9 us -> none  [the longest x1 8.32 us: shards(): grad_gate_up = dot(n2_all, d_both, TN).astype(bf16)]
    all_to_all x1, waiting for transfers between devices: 0.01 us -> 10.3 us  [shards(): lax.all_to_all(mixed_dealt.reshape(n_ctx, rows, hw), 'ctx', split_axis=0,...]
  transfers between devices with their start and end apart: 9 -> 9, of which waited for: 0 -> 1; matrix products, arithmetic and copies ran while one was open for 9% -> 6% of each run, Pallas kernels for 62% -> 72%
where the time goes in v4:
time: 782 us; the launch traced here: 778 us
  Pallas kernels  669 us (86%)
  matrix products  28.4 us (4%)
  other arithmetic  25.1 us (3%)
  local copies, waits for them, and re-layouts  18.1 us (2%)
  between operations  14.8 us (2%)
  starting transfers between devices  11.2 us (1%)
  waiting for transfers between devices  11.2 us (1%)
    pallas_call x5, Pallas kernels, gather_ctx(): pl.pallas_call(functools.partial(gather_kernel, n, plans, parts), out_sha...  413 us
    pallas_call x2, Pallas kernels, reduce_ctx(): pl.pallas_call(functools.partial(reduce_kernel, n, chunks, jobs, extras,...  152 us
    pallas_call x1, Pallas kernels, gather_first(): pl.pallas_call(functools.partial(first_kernel, n, chunks, ratio), out_sha...  50.2 us
    dot_general x5, matrix products, dot(): return lax.dot_general(a, b, (dims, ((), ())), preferred_element_type=f32)  28.4 us
    pallas_call x2, Pallas kernels, assemble(): pl.pallas_call(body, grid=(rows // block,), out_shape=jax.ShapeDtypeStruc...  22.5 us
  transfers between devices with their start and end apart: 9, of which 1 were waited for; matrix products, arithmetic and copies ran while one was open for 6% of the time, Pallas kernels for 72%

profile of v4, /device:TPU:0, one launch (start us, length us, event | category | flops | bytes accessed | tf_op | source)
XLA Modules:
  0.0 777.8 jit_solution(16796397661191659068)
XLA Ops:
  7.2 1.5 dynamic-slice_convert_fusion.4
  8.7 0.9 pad_maximum_fusion.3
  9.7 1.3 select_maximum_fusion.refs_3_
  11.0 50.2 %gather0.1 = (bf16[8,128,2048]{2,1,0:T(8,128)(2,1)}, bf16[512,2048]{1,0:T(8,128)(2,1)}, bf16[688,2048]{1,0:T(8,128)(2,1)}, f32[4,8,512]{2,1,0:T(8,128)}) custom-call(bf16[128,2048]{1,0:T(8,128)(2,1)} %bitcast.85, f32[512,2048]{1,0:T(8,128)} %refs_1_.1, f32[1376,2048]{1,0:T(8,128)} %refs_2_.1, f32[8,512]{1,0:T(8,128)} %select_maximum_fusion.refs_3_), custom_call_target="tpu_custom_call" | custom-call | tf_op jit(solution)/shard_map/gather0/pallas_call | solution.py:367
  61.3 2.6 dynamic-slice_convert_fusion.1
  63.9 1.5 pad_maximum_fusion.2
  66.3 1.1 copy.39.first_ref
  67.4 47.0 %gather1.1 = bf16[8,128,2048]{2,1,0:T(8,128)(2,1)} custom-call(bf16[128,2048]{1,0:T(8,128)(2,1)} %bitcast.95), custom_call_target="tpu_custom_call" | custom-call | tf_op jit(solution)/shard_map/gather1/pallas_call | solution.py:269
  114.5 1.9 fusion.27
  116.4 1.3 pad_maximum_fusion.4
  117.7 0.9 multiply_reduce_fusion
  118.6 3.0 fusion.1.n_ref.refs_2_
  121.7 12.5 %attend.1 = (bf16[1024,256]{1,0:T(8,128)(2,1)}, bf16[1024,256]{1,0:T(8,128)(2,1)}, bf16[1024,256]{1,0:T(8,128)(2,1)}, bf16[1024,256]{1,0:T(8,128)(2,1)}) custom-call(bf16[1024,2048]{1,0:T(8,128)(2,1)} %fusion.1.n_ref.refs_2_, bf16[2048,768]{1,0:T(8,128)(2,1)} %all-gather.4.cloned.1.call-done.w_ref.refs_1_, f32[1024,128]{1,0:T(8,128)} %get-tuple-element.93.cos_ref, ...), custom_call_target="tpu_custom_call" | custom-call | tf_op jit(solution)/shard_map/attend/pallas_call | solution.py:725
  134.2 1.6 gather_fusion.1
  135.8 0.9 broadcast_select_fusion.2
  136.8 4.9 all-to-all-start
  141.8 2.8 gather_fusion
  144.7 10.3 %all-to-all-done = bf16[8,128,256]{2,1,0:T(8,128)(2,1)S(1)} async-done(((bf16[8,128,256]{2,1,0:T(8,128)(2,1)}), bf16[8,128,256]{2,1,0:T(8,128)(2,1)S(1)}, u32[]{:S(2)}, u32[]{:S(2)}) %all-to-all-start) | async-done | bytes 524320 | tf_op jit(solution)/shard_map/all_to_all | solution.py:865
  155.4 4.8 multiply_reduce_fusion.1
  160.2 1.0 multiply_convert_fusion.1.refs_0_
  161.2 47.5 %gather2.1 = (bf16[8,128,2048]{2,1,0:T(8,128)(2,1)}, bf16[688,2048]{1,0:T(8,128)(2,1)}) custom-call(bf16[128,2048]{1,0:T(8,128)(2,1)} %multiply_convert_fusion.1.refs_0_, bf16[688,2048]{1,0:T(8,128)(2,1)} %get-tuple-element.38.refs_1_), custom_call_target="tpu_custom_call" | custom-call | tf_op jit(solution)/shard_map/gather2/pallas_call | solution.py:269
  208.7 10.6 %fusion.31 = f32[1024,1376]{1,0:T(8,128)S(1)} fusion(bf16[1024,2048]{1,0:T(8,128)(2,1)} %bitcast.90, bf16[2048,1376]{1,0:T(8,128)(2,1)} %all-gather.8.cloned.1.call-done.refs_3_), kind=kOutput, calls=%fused_computation.107 | convolution fusion | flops 5771362304 | bytes 15466496 | tf_op jit(solution)/shard_map/dot_general | solution.py:681
  219.3 5.5 fusion.4
  224.8 2.5 pad_maximum_fusion.1.refs_2_
  227.2 99.5 %reduce4.1 = (bf16[128,2048]{1,0:T(8,128)(2,1)}, bf16[128,2048]{1,0:T(8,128)(2,1)}, bf16[2048,1376]{1,0:T(8,128)(2,1)}, bf16[688,2048]{1,0:T(8,128)(2,1)}) custom-call(bf16[1024,688]{1,0:T(8,128)(2,1)} %get-tuple-element.75.refs_0_, bf16[688,2048]{1,0:T(8,128)(2,1)} %get-tuple-element.40.refs_1_, bf16[1024,1376]{1,0:T(8,128)(2,1)} %pad_maximum_fusion.1.refs_2_, ...), custom_call_target="tpu_custom_call" | custom-call | tf_op jit(solution)/shard_map/reduce4/pallas_call | solution.py:615
  326.8 0.9 copy-done.7
  328.1 1.4 fusion.15
  329.5 50.3 %gather3.1 = bf16[8,128,2048]{2,1,0:T(8,128)(2,1)} custom-call(bf16[128,2048]{1,0:T(8,128)(2,1)} %get-tuple-element.76.refs_0_), custom_call_target="tpu_custom_call" | custom-call | tf_op jit(solution)/shard_map/gather3/pallas_call | solution.py:269
  379.8 3.8 convolution_convert_fusion
  383.6 2.4 pad_maximum_fusion
  386.8 3.8 convolution_convert_fusion.1
  391.2 0.9 broadcast_select_fusion
  392.1 10.6 %attend_back.1.refs_0_ = bf16[1024,768]{1,0:T(8,128)(2,1)} custom-call(bf16[1024,256]{1,0:T(8,128)(2,1)} %get-tuple-element.43.q_ref, bf16[1024,256]{1,0:T(8,128)(2,1)} %get-tuple-element.44.k_ref, bf16[1024,256]{1,0:T(8,128)(2,1)} %get-tuple-element.45.v_ref, bf16[1024,256]{1,0:T(8,128)(2,1)} %bitcast.94, f32[1024,128]{1,0:T(8,128)} %get-tuple-element.93.cos_ref, ...), custom_call_target="tpu_custom_call" | custom-call | tf_op jit(solution)/shard_map/attend_back/pallas_call | solution.py:768
  402.7 52.1 %reduce6.1 = (bf16[128,2048]{1,0:T(8,128)(2,1)}, bf16[2048,768]{1,0:T(8,128)(2,1)}) custom-call(bf16[1024,768]{1,0:T(8,128)(2,1)} %attend_back.1.refs_0_, bf16[2048,768]{1,0:T(8,128)(2,1)} %all-gather.4.cloned.1.call-done.w_ref.refs_1_, bf16[1024,2048]{1,0:T(8,128)(2,1)} %fusion.1.n_ref.refs_2_), custom_call_target="tpu_custom_call" | custom-call | tf_op jit(solution)/shard_map/reduce6/pallas_call | solution.py:615
  454.8 1.4 fusion.23
  456.2 1.3 copy.47
  457.6 0.7 reduce-scatter.11.cloned.1.call-update
  458.3 81.2 %gather9.1 = bf16[8,944,512]{2,1,0:T(8,128)(2,1)} custom-call(bf16[944,512]{1,0:T(8,128)(2,1)} %reduce-scatter.9.cloned.1.call-done.refs_0_), custom_call_target="tpu_custom_call" | custom-call | tf_op jit(solution)/shard_map/gather9/pallas_call | solution.py:269
  539.6 5.6 all-to-all-start.1
  545.2 2.8 gather_fusion.2
  548.1 1.3 fusion.26
  549.4 1.1 copy.48
  550.5 0.6 pad.8.refs_2_
  551.1 186.6 %gather8.1 = (bf16[8,512,1376]{2,1,0:T(8,128)(2,1)}, bf16[8,512,768]{2,1,0:T(8,128)(2,1)}, f32[8,8,512]{2,1,0:T(8,128)}) custom-call(bf16[512,1376]{1,0:T(8,128)(2,1)} %reduce-scatter.7.cloned.1.call-done.refs_0_, bf16[512,768]{1,0:T(8,128)(2,1)} %reduce-scatter.11.cloned.1.call-done.refs_1_, f32[8,512]{1,0:T(8,128)} %pad.8.refs_2_), custom_call_target="tpu_custom_call" | custom-call | tf_op jit(solution)/shard_map/gather8/pallas_call | solution.py:269
  737.7 0.9 reduce_sum.112
  738.7 8.8 %assemble.2 = f32[512,6144]{1,0:T(8,128)} custom-call(bf16[8,512,768]{2,1,0:T(8,128)(2,1)} %get-tuple-element.54.i_ref), custom_call_target="tpu_custom_call" | custom-call | tf_op jit(solution)/shard_map/assemble/pallas_call | solution.py:671
  747.4 13.7 %assemble.3 = f32[512,11008]{1,0:T(8,128)} custom-call(bf16[8,512,1376]{2,1,0:T(8,128)(2,1)} %get-tuple-element.56.i_ref), custom_call_target="tpu_custom_call" | custom-call | tf_op jit(solution)/shard_map/assemble/pallas_call | solution.py:671
  761.8 9.0 %assemble_rows.1 = (f32[1376,2048]{1,0:T(8,128)}, f32[512,2048]{1,0:T(8,128)}) custom-call(bf16[4,1888,512]{2,1,0:T(8,128)(2,1)} %all-to-all-done.1.i_ref), custom_call_target="tpu_custom_call" | custom-call | tf_op jit(solution)/shard_map/assemble_rows/pallas_call | solution.py:645
  (83 shorter events, 4.2 us)
Async XLA Ops:
  7.2 114.5 %all-gather.4.cloned.1.call-start = ((), (), s32[]{:S(2)}) async-start(), calls=%async_computation.6 | async-start | bytes 3932160 | tf_op jit(solution)/shard_map/all_gather | solution.py:825
  9.6 145.7 %all-gather.6.cloned.1.call-start = ((), (), s32[]{:S(2)}) async-start(), calls=%async_computation.7 | async-start | bytes 10485760 | tf_op jit(solution)/shard_map/all_gather | solution.py:828
  61.3 4.2 copy-start.11
  61.3 4.4 copy-start.10
  61.3 147.4 %all-gather.8.cloned.1.call-start = ((), (), s32[]{:S(2)}) async-start(), calls=%async_computation.8 | async-start | bytes 7208960 | tf_op jit(solution)/shard_map/all_gather | solution.py:836
  63.9 50.5 %copy-start.9 = (f32[4,8,512]{2,1,0:T(8,128)S(1)}, f32[4,8,512]{2,1,0:T(8,128)}, u32[]{:S(2)}) copy-start(f32[4,8,512]{2,1,0:T(8,128)} %get-tuple-element.35) | copy-start | bytes 196612
  114.4 3.3 copy-start
  136.8 18.3 %all-to-all-start = ((bf16[8,128,256]{2,1,0:T(8,128)(2,1)}), bf16[8,128,256]{2,1,0:T(8,128)(2,1)S(1)}, u32[]{:S(2)}, u32[]{:S(2)}) async-start(bf16[8,128,256]{2,1,0:T(8,128)(2,1)} %bitcast.16), calls=%async_computation | async-start | bytes 1048576 | tf_op jit(solution)/shard_map/all_to_all | solution.py:865
  141.7 244.4 %reduce-scatter.7.cloned.1.call-start = ((), (), s32[]{:S(2)}) async-start(), calls=%async_computation.9 | async-start | bytes 7208960 | tf_op jit(solution)/shard_map/reduce_scatter | solution.py:902
  208.7 10.6 %copy-start.1 = (bf16[8,128,2048]{2,1,0:T(8,128)(2,1)S(1)}, bf16[8,128,2048]{2,1,0:T(8,128)(2,1)}, u32[]{:S(2)}) copy-start(bf16[8,128,2048]{2,1,0:T(8,128)(2,1)} %gather1.1) | copy-start | bytes 12582916
  208.7 10.6 %copy-start.4 = (bf16[688,2048]{1,0:T(8,128)(2,1)S(1)}, bf16[688,2048]{1,0:T(8,128)(2,1)}, u32[]{:S(2)}) copy-start(bf16[688,2048]{1,0:T(8,128)(2,1)} %get-tuple-element.40.refs_1_) | copy-start | bytes 8454148
  326.7 1.0 copy-start.7
  326.7 1.4 copy-start.5
  326.7 1.4 copy-start.8
  326.8 131.6 %reduce-scatter.9.cloned.1.call-start = ((), (), s32[]{:S(2)}) async-start(), calls=%async_computation.10 | async-start | bytes 4833280 | tf_op jit(solution)/shard_map/reduce_scatter | solution.py:935
  379.8 3.8 copy-start.3
  383.6 3.0 copy-start.2
  386.1 163.3 %reduce-scatter.13.cloned.1.call-start = ((), (), s32[]{:S(2)}) async-start(), calls=%async_computation.12 | async-start | bytes 1310720
  457.6 93.6 %reduce-scatter.11.cloned.1.call-start = ((), (), s32[]{:S(2)}) async-start(), calls=%async_computation.11 | async-start | bytes 3932160 | tf_op jit(solution)/shard_map/reduce_scatter | solution.py:919
  539.5 8.6 %copy-start.6 = (bf16[128,2048]{1,0:T(8,128)(2,1)S(1)}, bf16[128,2048]{1,0:T(8,128)(2,1)}, u32[]{:S(2)}) copy-start(bf16[128,2048]{1,0:T(8,128)(2,1)} %get-tuple-element.46) | copy-start | bytes 1572868
  539.6 222.2 %all-to-all-start.1 = ((bf16[4,1888,512]{2,1,0:T(8,128)(2,1)}), bf16[4,1888,512]{2,1,0:T(8,128)(2,1)}, u32[]{:S(2)}, u32[]{:S(2)}) async-start(bf16[4,1888,512]{2,1,0:T(8,128)(2,1)} %bitcast.81), calls=%async_computation.4 | async-start | bytes 15466496 | tf_op jit(solution)/shard_map/all_to_all | solution.py:938
Sparse Core Ops, SparseCore 0:
  10.1 31.2 all-gather.3
  61.4 58.0 all-gather.5
  121.6 44.5 all-gather.7
  326.9 58.3 reduce-scatter.6
  388.5 42.4 reduce-scatter.8
  457.7 25.9 reduce-scatter.12
  486.3 37.9 reduce-scatter.10

commit v5 on v4

--- a/solution.py
+++ b/solution.py
@@ -387,6 +387,216 @@
         ),
         name=f"gather{cid}",
     )(x, w_out, w_down, gains)
+
+
+def attend_gather_kernel(n, chunks, heads, block, *refs):
+    x, n_hbm, w_hbm, cos_ref, sin_ref, first_ref, order_ref = refs[:7]
+    out, q_ref, k_ref, v_ref, dealt_ref, all_ref = refs[7:13]
+    held, n_ref, w_ref, mixed, local, s1, r1, s2, r2, sa, ra = refs[13:]
+    n_a, n_b, a, b, f = places(n)
+    c = a * n_b + b
+    all_rows = n_ref.shape[0]
+    rows = all_rows // n
+    hw = heads * HD
+    loads = [
+        pltpu.make_async_copy(src, dst, local.at[i])
+        for i, (src, dst) in enumerate(((x, held), (n_hbm, n_ref), (w_hbm, w_ref)))
+    ]
+    for copy in loads:
+        copy.start()
+    bar = pltpu.get_barrier_semaphore()
+    for m in range(1, n):
+        pl.semaphore_signal(bar, inc=1, device_id=((c + m) % n, f), device_id_type=MESH)
+    pl.semaphore_wait(bar, n - 1)
+    steps, ends = [], []
+    for i, chunk in enumerate(chunks):
+        more, end = gather_steps(n, x, out, chunk, (s1.at[i], r1.at[i], s2.at[i], r2.at[i]))
+        steps.append(more)
+        ends.append(end)
+
+    def run(t):
+        for more in steps:
+            if t < len(more):
+                more[t]()
+
+    def exchange(m):
+        to = (c + m) % n
+        return pltpu.make_async_remote_copy(
+            src_ref=dealt_ref.at[to],
+            dst_ref=all_ref.at[c],
+            send_sem=sa.at[m],
+            recv_sem=ra.at[m],
+            device_id=(to, f),
+            device_id_type=MESH,
+        )
+
+    def attend_block(at):
+        own = slice(at, at + block)
+        proj = dot(n_ref[own, :], w_ref[...], NN)
+        cos, sin = cos_ref[own, :], sin_ref[own, :]
+        for h in range(heads):
+            head = slice(h * HD, (h + 1) * HD)
+            for ref, base in ((q_ref, 0), (k_ref, hw)):
+                u = proj[:, base + h * HD : base + (h + 1) * HD]
+                ref[own, head] = (u * cos + turned(u) * sin).astype(bf16)
+        v_ref[own, :] = proj[:, 2 * hw :].astype(bf16)
+        for h in range(heads):
+            head = slice(h * HD, (h + 1) * HD)
+            seen = slice(0, at + block)
+            probs = masked_probs(q_ref[own, head], k_ref[seen, head], first_ref[own, :], at)
+            mixed[own, head] = dot(probs.astype(bf16), v_ref[seen, head], NN).astype(bf16)
+
+    run(0)
+    keep = pltpu.make_async_copy(held, out.at[c], local.at[0])
+    loads[0].wait()
+    keep.start()
+    loads[1].wait()
+    loads[2].wait()
+    for at in range(0, all_rows, block):
+        attend_block(at)
+        if at + block == all_rows // 2:
+            run(1)
+    for m in range(n):
+        own = slice(m * rows, (m + 1) * rows)
+        given = lax.broadcasted_iota(jnp.int32, (rows, all_rows), 1)
+        picks = jnp.where(given == order_ref[own, :], 1.0, 0.0).astype(bf16)
+        dealt_ref[m] = dot(picks, mixed[...], NN).astype(bf16)
+    for m in range(1, n):
+        exchange(m).start()
+    mine = pltpu.make_async_copy(dealt_ref.at[c], all_ref.at[c], local.at[1])
+    mine.start()
+    for t in range(2, n_a + n_b - 1):
+        run(t)
+    keep.wait()
+    mine.wait()
+    for m in range(1, n):
+        exchange(m).wait()
+    for end in ends:
+        end()
+
+
+def attend_gather(x, normed, wq, cos, sin, first, order, heads, n, cid, block=256):
+    all_rows = normed.shape[0]
+    rows = all_rows // n
+    hw = heads * HD
+    chunks = plan(x.shape[0])
+    one = jax.ShapeDtypeStruct((all_rows, hw), bf16)
+    split = jax.ShapeDtypeStruct((n, rows, hw), bf16)
+    hbm = pl.BlockSpec(memory_space=pl.ANY)
+    vmem = pl.BlockSpec(memory_space=pltpu.VMEM)
+    sem = pltpu.SemaphoreType.DMA
+    return pl.pallas_call(
+        functools.partial(attend_gather_kernel, n, chunks, heads, block),
+        out_shape=[jax.ShapeDtypeStruct((n,) + x.shape, x.dtype), one, one, one, split, split],
+        in_specs=[hbm] * 3 + [vmem] * 4,
+        out_specs=[hbm] + [vmem] * 4 + [hbm],
+        scratch_shapes=[
+            pltpu.VMEM(x.shape, x.dtype),
+            pltpu.VMEM(normed.shape, bf16),
+            pltpu.VMEM(wq.shape, bf16),
+            pltpu.VMEM((all_rows, hw), bf16),
+            sem((3,)),
+        ]
+        + gather_sems(len(chunks))
+        + [sem((n,)), sem((n,))],
+        compiler_params=pltpu.CompilerParams(
+            collective_id=cid, has_side_effects=True, vmem_limit_bytes=60 << 20
+        ),
+        name=f"attend{cid}",
+    )(x, normed, wq, cos, sin, first, order)
+
+
+def back_gather_kernel(n, chunks, heads, block, *refs):
+    x, db_hbm, wo_hbm, down_hbm, q_ref, k_ref, v_ref, mixed_ref = refs[:8]
+    cos_ref, sin_ref, first_ref, order_ref = refs[8:12]
+    out, proj_ref, rows_hbm = refs[12:15]
+    held, db, wo, down, rows_ref, dealt, given, dk_ref, dv_ref, local, s1, r1, s2, r2 = refs[15:]
+    n_a, n_b, a, b, f = places(n)
+    c = a * n_b + b
+    hw = heads * HD
+    all_rows = db.shape[0]
+    part = all_rows // n
+    ffs = down.shape[0]
+    own_rows = pl.ds(pl.multiple_of(c * hw, hw), hw)
+    loads = [
+        pltpu.make_async_copy(src, dst, local.at[i])
+        for i, (src, dst) in enumerate(((x, held), (db_hbm, db), (wo_hbm.at[own_rows], wo), (down_hbm, down)))
+    ]
+    for copy in loads:
+        copy.start()
+    greet(a, b, n_a, n_b, f)
+    steps, ends = [], []
+    for i, chunk in enumerate(chunks):
+        more, end = gather_steps(n, x, out, chunk, (s1.at[i], r1.at[i], s2.at[i], r2.at[i]))
+        steps.append(more)
+        ends.append(end)
+
+    def run(t):
+        for more in steps:
+            if t < len(more):
+                more[t]()
+
+    run(0)
+    keep = pltpu.make_async_copy(held, out.at[c], local.at[0])
+    loads[0].wait()
+    keep.start()
+    for copy in loads[1:]:
+        copy.wait()
+    dealt[...] = dot(db[...], wo[...], NT).astype(bf16)
+    for m in range(n):
+        own = slice(m * part, (m + 1) * part)
+        slots = lax.broadcasted_iota(jnp.int32, (part, all_rows), 1)
+        picks = jnp.where(slots == order_ref[own, :], 1.0, 0.0).astype(bf16)
+        given[own, :] = dot(picks, dealt[...], NN).astype(bf16)
+    rows_ref[:ffs, :] = down[...]
+    rows_ref[ffs:, :] = dot(mixed_ref[...], db[...], TN).astype(bf16)
+    stored = pltpu.make_async_copy(rows_ref, rows_hbm, local.at[1])
+    stored.start()
+    attend_back_kernel(
+        heads, block, q_ref, k_ref, v_ref, given, cos_ref, sin_ref, first_ref, proj_ref, dk_ref, dv_ref
+    )
+    for t in range(1, n_a + n_b - 1):
+        run(t)
+    keep.wait()
+    stored.wait()
+    for end in ends:
+        end()
+
+
+def back_gather(x, db, wo, down, q, k, v, mixed, cos, sin, first, order, heads, n, cid, block=256):
+    all_rows, width = db.shape
+    hw = heads * HD
+    chunks = plan(x.shape[0])
+    hbm = pl.BlockSpec(memory_space=pl.ANY)
+    vmem = pl.BlockSpec(memory_space=pltpu.VMEM)
+    both_rows = (down.shape[0] + hw, width)
+    return pl.pallas_call(
+        functools.partial(back_gather_kernel, n, chunks, heads, block),
+        out_shape=[
+            jax.ShapeDtypeStruct((n,) + x.shape, x.dtype),
+            jax.ShapeDtypeStruct((all_rows, 3 * hw), bf16),
+            jax.ShapeDtypeStruct(both_rows, bf16),
+        ],
+        in_specs=[hbm] * 4 + [vmem] * 8,
+        out_specs=[hbm, vmem, hbm],
+        scratch_shapes=[
+            pltpu.VMEM(x.shape, x.dtype),
+            pltpu.VMEM(db.shape, bf16),
+            pltpu.VMEM((hw, width), bf16),
+            pltpu.VMEM(down.shape, bf16),
+            pltpu.VMEM(both_rows, bf16),
+            pltpu.VMEM((all_rows, hw), bf16),
+            pltpu.VMEM((all_rows, hw), bf16),
+            pltpu.VMEM((all_rows, HD), f32),
+            pltpu.VMEM((all_rows, HD), f32),
+            pltpu.SemaphoreType.DMA((4,)),
+        ]
+        + gather_sems(len(chunks)),
+        compiler_params=pltpu.CompilerParams(
+            collective_id=cid, has_side_effects=True, vmem_limit_bytes=60 << 20
+        ),
+        name=f"back{cid}",
+    )(x, db, wo, down, q, k, v, mixed, cos, sin, first, order)
 
 
 def order_of(p, n):
@@ -699,37 +909,6 @@
     return raised / jnp.sum(raised, -1, keepdims=True)
 
 
-def attend_kernel(heads, block, n_ref, w_ref, cos_ref, sin_ref, first_ref, q_ref, k_ref, v_ref, o_ref):
-    rows = n_ref.shape[0]
-    hw = heads * HD
-    for at in range(0, rows, block):
-        own = slice(at, at + block)
-        proj = dot(n_ref[own, :], w_ref[...], NN)
-        cos, sin = cos_ref[own, :], sin_ref[own, :]
-        for h in range(heads):
-            head = slice(h * HD, (h + 1) * HD)
-            for ref, base in ((q_ref, 0), (k_ref, hw)):
-                u = proj[:, base + h * HD : base + (h + 1) * HD]
-                ref[own, head] = (u * cos + turned(u) * sin).astype(bf16)
-        v_ref[own, :] = proj[:, 2 * hw :].astype(bf16)
-        for h in range(heads):
-            head = slice(h * HD, (h + 1) * HD)
-            seen = slice(0, at + block)
-            probs = masked_probs(q_ref[own, head], k_ref[seen, head], first_ref[own, :], at)
-            o_ref[own, head] = dot(probs.astype(bf16), v_ref[seen, head], NN).astype(bf16)
-
-
-def attend(normed, wq, cos, sin, first, heads, block=256):
-    rows = normed.shape[0]
-    one = jax.ShapeDtypeStruct((rows, heads * HD), bf16)
-    return pl.pallas_call(
-        functools.partial(attend_kernel, heads, block),
-        out_shape=[one] * 4,
-        compiler_params=pltpu.CompilerParams(vmem_limit_bytes=60 << 20),
-        name="attend",
-    )(normed, wq, cos, sin, first)
-
-
 def attend_back_kernel(
     heads, block, q_ref, k_ref, v_ref, d_ref, cos_ref, sin_ref, first_ref, o_ref, dk_ref, dv_ref
 ):
@@ -763,17 +942,6 @@
         o_ref[:, 2 * hw + h * HD : 2 * hw + (h + 1) * HD] = dv_ref[...].astype(bf16)
 
 
-def attend_back(q, k, v, d_mixed, cos, sin, first, heads, block=256):
-    rows = q.shape[0]
-    return pl.pallas_call(
-        functools.partial(attend_back_kernel, heads, block),
-        out_shape=jax.ShapeDtypeStruct((rows, 3 * heads * HD), bf16),
-        scratch_shapes=[pltpu.VMEM((rows, HD), f32), pltpu.VMEM((rows, HD), f32)],
-        compiler_params=pltpu.CompilerParams(vmem_limit_bytes=60 << 20),
-        name="attend_back",
-    )(q, k, v, d_mixed, cos, sin, first)
-
-
 def rope_tables(within):
     freq_index = jnp.arange(HD // 2, dtype=f32)
     inverse = rope_base ** (-2.0 * freq_index / HD)
@@ -834,7 +1002,6 @@
         -1,
     ).astype(bf16)
     wgu = lax.all_gather(wg_own, "fsdp", axis=0, tiled=True)
-    g_all = gather_ctx([cotangent[0]], n_ctx, 1)[0].reshape(all_rows, width)
 
     deal_table = deal[0]
     device_index = jnp.arange(n_ctx, dtype=jnp.int32)
@@ -857,14 +1024,12 @@
 
     x_float = x_all.astype(f32)
     normed_one = (x_float * rms_scale(x_float) * gain_one[None, :]).astype(bf16)
-    queries, keys, values, mixed = attend(
-        normed_one, wq, cosine_table, sine_table, first_key, heads
+    order = (dealt_from[:, None] * piece + jnp.arange(piece, dtype=jnp.int32)).reshape(all_rows, 1)
+    g_all, queries, keys, values, mixed_dealt, mixed_own = attend_gather(
+        cotangent[0], normed_one, wq, cosine_table, sine_table, first_key, order, heads, n_ctx, 1
     )
-    mixed = mixed.reshape(pieces, piece, hw)
-    mixed_dealt = jnp.take(mixed, dealt_from, axis=0)
-    mixed_own = lax.all_to_all(
-        mixed_dealt.reshape(n_ctx, rows, hw), "ctx", split_axis=0, concat_axis=2, tiled=True
-    ).reshape(rows, width)
+    g_all = g_all.reshape(all_rows, width)
+    mixed_own = mixed_own.transpose(1, 0, 2).reshape(rows, width)
     mixed_dealt = mixed_dealt.reshape(all_rows, hw)
 
     x_dealt = jnp.take(x_all.reshape(pieces, piece, width), own_dealt, axis=0)
@@ -906,13 +1071,25 @@
     d_branch = d_hidden.astype(bf16)
     db_all = gather_ctx([d_branch], n_ctx, 3)[0].reshape(all_rows, width)
 
-    grad_out = dot(mixed_dealt, db_all, TN).astype(bf16)
-    wo_rows = lax.dynamic_slice(wo, (me * hw, 0), (hw, width))
-    d_mixed = dot(db_all, wo_rows, NT).astype(bf16)
-    d_mixed = jnp.take(d_mixed.reshape(pieces, piece, hw), given_from, axis=0)
-    d_mixed = d_mixed.reshape(all_rows, hw)
-    d_proj = attend_back(
-        queries, keys, values, d_mixed, cosine_table, sine_table, first_key, heads
+    order_back = (given_from[:, None] * piece + jnp.arange(piece, dtype=jnp.int32)).reshape(
+        all_rows, 1
+    )
+    all_gate_up, d_proj, grad_rows = back_gather(
+        row_gate_up,
+        db_all,
+        wo,
+        grad_down,
+        queries,
+        keys,
+        values,
+        mixed_dealt,
+        cosine_table,
+        sine_table,
+        first_key,
+        order_back,
+        heads,
+        n_ctx,
+        7,
     )
     d_one, grad_qkv = reduce_ctx([d_proj, wq, normed_one], ((0, 1, True),), ((2, 0),), n_ctx, 6)
     d_one = d_one.astype(f32)
@@ -930,14 +1107,12 @@
     )
     norms = jnp.pad(norms, ((0, 6), (0, 0)))
 
-    grad_rows = jnp.concatenate([grad_down, grad_out], 0)
-    grad_rows, row_gate_up = lax.optimization_barrier((grad_rows, row_gate_up))
     col_rows = lax.psum_scatter(grad_rows, "fsdp", scatter_dimension=1, tiled=True)
     all_cols = gather_ctx([col_rows], n_ctx, 9)[0]
     owner_rows = all_cols.reshape(n_fsdp, ratio * (ffs + hw), width // n_fsdp)
     swapped = lax.all_to_all(owner_rows, "fsdp", split_axis=0, concat_axis=0, tiled=True)
-    row_gate_up, all_cols = lax.optimization_barrier((row_gate_up, all_cols))
-    all_gate_up, all_qkv, all_norms = gather_ctx([row_gate_up, row_qkv, norms], n_ctx, 8)
+    row_qkv, all_cols = lax.optimization_barrier((row_qkv, all_cols))
+    all_qkv, all_norms = gather_ctx([row_qkv, norms], n_ctx, 8)
     final_gate_up = assemble(all_gate_up, 2)
     final_qkv = assemble(all_qkv, 3)
     final_norms = jnp.sum(all_norms, 0)

time: 782 us -> 761 us (0.973)
    pallas_call x2, Pallas kernels: 23.2 us -> 182 us  [the longest x1 123 us: back_gather(): pl.pallas_call(functools.partial(back_gather_kernel, n, chunks, heads, bl...]
    pallas_call x5 -> x4, Pallas kernels: 413 us -> 255 us  [gather_ctx(): pl.pallas_call(functools.partial(gather_kernel, n, plans, parts), out_sha...]
    all_to_all x1 -> x0, waiting for transfers between devices: 10.3 us -> none  [shards(): lax.all_to_all(mixed_dealt.reshape(n_ctx, rows, hw), 'ctx', split_axis=0,...]
    dot_general x5 -> x3, matrix products: 28.4 us -> 20.8 us  [dot(): return lax.dot_general(a, b, (dims, ((), ())), preferred_element_type=f32)]
  transfers between devices with their start and end apart: 9 -> 8, of which waited for: 1 -> 1; matrix products, arithmetic and copies ran while one was open for 6% -> 5% of each run, Pallas kernels for 72% -> 58%
where the time goes in v5:
time: 761 us; the launch traced here: 757 us
  Pallas kernels  670 us (88%)
  matrix products  20.8 us (3%)
  other arithmetic  20.2 us (3%)
  local copies, waits for them, and re-layouts  19.6 us (3%)
  between operations  14.7 us (2%)
    pallas_call x4, Pallas kernels, gather_ctx(): pl.pallas_call(functools.partial(gather_kernel, n, plans, parts), out_sha...  255 us
    pallas_call x2, Pallas kernels, reduce_ctx(): pl.pallas_call(functools.partial(reduce_kernel, n, chunks, jobs, extras,...  151 us
    pallas_call x1, Pallas kernels, back_gather(): pl.pallas_call(functools.partial(back_gather_kernel, n, chunks, heads, bl...  123 us
    pallas_call x1, Pallas kernels, attend_gather(): pl.pallas_call(functools.partial(attend_gather_kernel, n, chunks, heads,...  59.5 us
    pallas_call x1, Pallas kernels, gather_first(): pl.pallas_call(functools.partial(first_kernel, n, chunks, ratio), out_sha...  50.2 us
    pallas_call x2, Pallas kernels, assemble(): pl.pallas_call(body, grid=(rows // block,), out_shape=jax.ShapeDtypeStruc...  22.6 us
    dot_general x3, matrix products, dot(): return lax.dot_general(a, b, (dims, ((), ())), preferred_element_type=f32)  20.8 us
  transfers between devices with their start and end apart: 8, of which 1 were waited for; matrix products, arithmetic and copies ran while one was open for 5% of the time, Pallas kernels for 58%

profile of v5, /device:TPU:0, one launch (start us, length us, event | category | flops | bytes accessed | tf_op | source)
XLA Modules:
  0.0 756.8 jit_solution(14746728849854211358)
XLA Ops:
  7.2 1.5 dynamic-slice_convert_fusion.4
  8.7 0.9 pad_maximum_fusion.2
  9.7 0.6 select_maximum_fusion.refs_3_
  10.3 50.2 %gather0.1 = (bf16[8,128,2048]{2,1,0:T(8,128)(2,1)}, bf16[512,2048]{1,0:T(8,128)(2,1)}, bf16[688,2048]{1,0:T(8,128)(2,1)}, f32[4,8,512]{2,1,0:T(8,128)}) custom-call(bf16[128,2048]{1,0:T(8,128)(2,1)} %bitcast.65, f32[512,2048]{1,0:T(8,128)} %refs_1_.1, f32[1376,2048]{1,0:T(8,128)} %refs_2_.1, f32[8,512]{1,0:T(8,128)} %select_maximum_fusion.refs_3_), custom_call_target="tpu_custom_call" | custom-call | tf_op jit(solution)/shard_map/gather0/pallas_call | solution.py:367
  60.7 2.6 dynamic-slice_convert_fusion.1
  63.3 1.5 pad_maximum_fusion.1
  64.8 0.6 reduce-scatter.7.cloned.1.call-start
  65.4 0.2 reduce-window.4
  66.2 1.1 add.198.refs_6_
  67.5 1.1 copy.41.refs_5_.refs_10_
  68.7 3.3 gather_fusion
  72.0 1.9 fusion.22
  73.9 1.3 pad_maximum_fusion.3
  75.2 0.9 multiply_reduce_fusion
  76.2 3.0 fusion.1.refs_1_.refs_2_
  79.3 59.5 %attend1.1 = (bf16[8,128,2048]{2,1,0:T(8,128)(2,1)}, bf16[1024,256]{1,0:T(8,128)(2,1)}, bf16[1024,256]{1,0:T(8,128)(2,1)}, bf16[1024,256]{1,0:T(8,128)(2,1)}, bf...) custom-call(bf16[128,2048]{1,0:T(8,128)(2,1)} %bitcast.73, bf16[1024,2048]{1,0:T(8,128)(2,1)} %fusion.1.refs_1_.refs_2_, ...), custom_call_target="tpu_custom_call" | custom-call | tf_op jit(solution)/shard_map/attend1/pallas_call | solution.py:488
  138.8 1.3 copy.43
  140.2 4.8 multiply_reduce_fusion.1
  145.0 1.0 multiply_convert_fusion.3.refs_0_
  145.9 48.4 %gather2.1 = (bf16[8,128,2048]{2,1,0:T(8,128)(2,1)}, bf16[688,2048]{1,0:T(8,128)(2,1)}) custom-call(bf16[128,2048]{1,0:T(8,128)(2,1)} %multiply_convert_fusion.3.refs_0_, bf16[688,2048]{1,0:T(8,128)(2,1)} %get-tuple-element.39.refs_1_), custom_call_target="tpu_custom_call" | custom-call | tf_op jit(solution)/shard_map/gather2/pallas_call | solution.py:269
  194.3 10.6 %fusion.25 = f32[1024,1376]{1,0:T(8,128)S(1)} fusion(bf16[1024,2048]{1,0:T(8,128)(2,1)} %bitcast.69, bf16[2048,1376]{1,0:T(8,128)(2,1)} %all-gather.8.cloned.1.call-done.refs_3_), kind=kOutput, calls=%fused_computation.92 | convolution fusion | flops 5771362304 | bytes 15466496 | tf_op jit(solution)/shard_map/dot_general | solution.py:891
  205.0 5.4 multiply_convert_fusion.1
  210.4 2.5 pad_maximum_fusion.refs_2_
  212.9 99.7 %reduce4.1 = (bf16[128,2048]{1,0:T(8,128)(2,1)}, bf16[128,2048]{1,0:T(8,128)(2,1)}, bf16[2048,1376]{1,0:T(8,128)(2,1)}, bf16[688,2048]{1,0:T(8,128)(2,1)}) custom-call(bf16[1024,688]{1,0:T(8,128)(2,1)} %get-tuple-element.78.refs_0_, bf16[688,2048]{1,0:T(8,128)(2,1)} %get-tuple-element.41.refs_1_, bf16[1024,1376]{1,0:T(8,128)(2,1)} %pad_maximum_fusion.refs_2_, ...), custom_call_target="tpu_custom_call" | custom-call | tf_op jit(solution)/shard_map/reduce4/pallas_call | solution.py:825
  312.7 1.1 add.199.refs_11_
  313.8 0.3 fusion.14
  314.2 1.4 fusion.11
  315.6 54.4 %gather3.1 = bf16[8,128,2048]{2,1,0:T(8,128)(2,1)} custom-call(bf16[128,2048]{1,0:T(8,128)(2,1)} %get-tuple-element.79.refs_0_), custom_call_target="tpu_custom_call" | custom-call | tf_op jit(solution)/shard_map/gather3/pallas_call | solution.py:269
  370.0 4.2 reduce-scatter.7.cloned.1.call-done.refs_0_
  374.2 122.6 %back7.1 = (bf16[8,512,1376]{2,1,0:T(8,128)(2,1)}, bf16[1024,768]{1,0:T(8,128)(2,1)}, bf16[944,2048]{1,0:T(8,128)(2,1)}) custom-call(bf16[512,1376]{1,0:T(8,128)(2,1)} %reduce-scatter.7.cloned.1.call-done.refs_0_, bf16[1024,2048]{1,0:T(8,128)(2,1)} %bitcast.62, bf16[2048,2048]{1,0:T(8,128)(2,1)} %all-gather.6.cloned.1.call-done.refs_2_, ...), custom_call_target="tpu_custom_call" | custom-call | tf_op jit(solution)/shard_map/back7/pallas_call | solution.py:573
  496.9 1.0 copy-done.1
  497.9 0.2 fusion.15
  498.1 51.3 %reduce6.1 = (bf16[128,2048]{1,0:T(8,128)(2,1)}, bf16[2048,768]{1,0:T(8,128)(2,1)}) custom-call(bf16[1024,768]{1,0:T(8,128)(2,1)} %get-tuple-element.51.refs_0_, bf16[2048,768]{1,0:T(8,128)(2,1)} %all-gather.4.cloned.1.call-done.refs_2_.refs_1_, bf16[1024,2048]{1,0:T(8,128)(2,1)} %fusion.1.refs_1_.refs_2_), custom_call_target="tpu_custom_call" | custom-call | tf_op jit(solution)/shard_map/reduce6/pallas_call | solution.py:825
  549.4 1.4 fusion.19
  550.8 1.3 copy.52
  552.3 0.7 reduce-scatter.9.cloned.1.call-update
  553.0 81.5 %gather9.1 = bf16[8,944,512]{2,1,0:T(8,128)(2,1)} custom-call(bf16[944,512]{1,0:T(8,128)(2,1)} %reduce-scatter.11.cloned.1.call-done.refs_0_), custom_call_target="tpu_custom_call" | custom-call | tf_op jit(solution)/shard_map/gather9/pallas_call | solution.py:269
  634.5 5.5 all-to-all-start
  640.0 2.8 gather_fusion.1
  642.9 13.8 %assemble.3 = f32[512,11008]{1,0:T(8,128)} custom-call(bf16[8,512,1376]{2,1,0:T(8,128)(2,1)} %get-tuple-element.59.i_ref), custom_call_target="tpu_custom_call" | custom-call | tf_op jit(solution)/shard_map/assemble/pallas_call | solution.py:881
  656.7 1.3 fusion.21
  658.0 1.1 copy.53
  659.1 0.6 pad.8.refs_1_
  659.7 70.7 %gather8.1 = (bf16[8,512,768]{2,1,0:T(8,128)(2,1)}, f32[8,8,512]{2,1,0:T(8,128)}) custom-call(bf16[512,768]{1,0:T(8,128)(2,1)} %reduce-scatter.9.cloned.1.call-done.refs_0_, f32[8,512]{1,0:T(8,128)} %pad.8.refs_1_), custom_call_target="tpu_custom_call" | custom-call | tf_op jit(solution)/shard_map/gather8/pallas_call | solution.py:269
  730.5 0.9 reduce_sum.112
  731.4 8.8 %assemble.2 = f32[512,6144]{1,0:T(8,128)} custom-call(bf16[8,512,768]{2,1,0:T(8,128)(2,1)} %get-tuple-element.57.i_ref), custom_call_target="tpu_custom_call" | custom-call | tf_op jit(solution)/shard_map/assemble/pallas_call | solution.py:881
  740.2 0.6 fusion.24
  740.7 9.0 %assemble_rows.1 = (f32[1376,2048]{1,0:T(8,128)}, f32[512,2048]{1,0:T(8,128)}) custom-call(bf16[4,1888,512]{2,1,0:T(8,128)(2,1)} %all-to-all-done.i_ref), custom_call_target="tpu_custom_call" | custom-call | tf_op jit(solution)/shard_map/assemble_rows/pallas_call | solution.py:855
  (75 shorter events, 1.7 us)
Async XLA Ops:
  7.2 2.5 copy-start.10
  7.2 2.5 copy-start.11
  7.2 72.1 %all-gather.4.cloned.1.call-start = ((), (), s32[]{:S(2)}) async-start(), calls=%async_computation.5 | async-start | bytes 3932160 | tf_op jit(solution)/shard_map/all_gather | solution.py:993
  9.7 130.5 %all-gather.6.cloned.1.call-start = ((), (), s32[]{:S(2)}) async-start(), calls=%async_computation.6 | async-start | bytes 10485760 | tf_op jit(solution)/shard_map/all_gather | solution.py:996
  60.6 4.8 copy-start.12
  60.6 5.0 copy-start.9
  60.6 133.7 %all-gather.8.cloned.1.call-start = ((), (), s32[]{:S(2)}) async-start(), calls=%async_computation.7 | async-start | bytes 7208960 | tf_op jit(solution)/shard_map/all_gather | solution.py:1004
  60.7 7.9 %copy-start.8 = (f32[4,8,512]{2,1,0:T(8,128)S(1)}, f32[4,8,512]{2,1,0:T(8,128)}, u32[]{:S(2)}) copy-start(f32[4,8,512]{2,1,0:T(8,128)} %get-tuple-element.36) | copy-start | bytes 196612
  64.8 309.4 %reduce-scatter.7.cloned.1.call-start = ((), (), s32[]{:S(2)}) async-start(), calls=%async_computation.8 | async-start | bytes 7208960 | tf_op jit(solution)/shard_map/reduce_scatter | solution.py:1067
  71.9 3.3 copy-start
  194.3 10.6 %copy-start.2 = (bf16[8,128,2048]{2,1,0:T(8,128)(2,1)S(1)}, bf16[8,128,2048]{2,1,0:T(8,128)(2,1)}, u32[]{:S(2)}) copy-start(bf16[8,128,2048]{2,1,0:T(8,128)(2,1)} %get-tuple-element.42) | copy-start | bytes 12582916
  194.3 10.6 %copy-start.3 = (bf16[688,2048]{1,0:T(8,128)(2,1)S(1)}, bf16[688,2048]{1,0:T(8,128)(2,1)}, u32[]{:S(2)}) copy-start(bf16[688,2048]{1,0:T(8,128)(2,1)} %get-tuple-element.41.refs_1_) | copy-start | bytes 8454148
  312.6 1.3 copy-start.6
  312.6 1.6 copy-start.4
  312.6 1.6 copy-start.7
  312.6 240.4 %reduce-scatter.11.cloned.1.call-start = ((), (), s32[]{:S(2)}) async-start(), calls=%async_computation.10 | async-start | bytes 4833280 | tf_op jit(solution)/shard_map/reduce_scatter | solution.py:1110
  496.8 1.0 copy-start.1
  496.9 161.1 %reduce-scatter.13.cloned.1.call-start = ((), (), s32[]{:S(2)}) async-start(), calls=%async_computation.11 | async-start | bytes 1310720
  552.2 107.5 %reduce-scatter.9.cloned.1.call-start = ((), (), s32[]{:S(2)}) async-start(), calls=%async_computation.9 | async-start | bytes 3932160 | tf_op jit(solution)/shard_map/reduce_scatter | solution.py:1096
  634.5 106.2 %all-to-all-start = ((bf16[4,1888,512]{2,1,0:T(8,128)(2,1)}), bf16[4,1888,512]{2,1,0:T(8,128)(2,1)}, u32[]{:S(2)}, u32[]{:S(2)}) async-start(bf16[4,1888,512]{2,1,0:T(8,128)(2,1)} %bitcast.61), calls=%async_computation.3 | async-start | bytes 15466496 | tf_op jit(solution)/shard_map/all_to_all | solution.py:1113
  642.9 13.8 %copy-start.5 = (bf16[128,2048]{1,0:T(8,128)(2,1)S(1)}, bf16[128,2048]{1,0:T(8,128)(2,1)}, u32[]{:S(2)}) copy-start(bf16[128,2048]{1,0:T(8,128)(2,1)} %get-tuple-element.52) | copy-start | bytes 1572868
Sparse Core Ops, SparseCore 0:
  10.2 31.2 all-gather.3
  60.7 57.9 all-gather.5
  120.9 46.0 all-gather.7
  312.7 61.4 reduce-scatter.6
  497.0 41.5 reduce-scatter.10
  552.3 24.2 reduce-scatter.12
  579.3 37.9 reduce-scatter.8

commit v6 on v5

--- a/solution.py
+++ b/solution.py
@@ -72,7 +72,7 @@
     return n_a, n_b, c // n_b, c % n_b, lax.axis_index("fsdp")
 
 
-def gather_steps(n, x, out, chunk, sems):
+def gather_steps(n, x, out, chunk, sems, late=None):
     n_a, n_b, a, b, f = places(n)
     first, count, swapped = chunk
     s1, r1, s2, r2 = sems
@@ -132,15 +132,25 @@
                 for d, cond in ((0, above2), (1, below2)):
                     when(cond)(lambda d=d: copy2(j, q1, 0, d).start())
 
+    def arrive2(m, d, onward, j, q1):
+        copy2(j, q1, m - 1, d).wait_recv()
+        if m < n2 - 1:
+            when(onward)(lambda: copy2(j, q1, m, d).start())
+
+    def arrivals2(m):
+        return [
+            (both(there2, there), functools.partial(arrive2, m, d, onward, j, q1), m, d, k < 2)
+            for j, k, _, q1, there in shards
+            for d, there2, onward in ((0, p2 >= m, above2), (1, p2 + m < n2, below2))
+        ]
+
     def line2(m):
-        for d, there2, onward in ((0, p2 >= m, above2), (1, p2 + m < n2, below2)):
-            for j, _, _, q1, there in shards:
-
-                @when(both(there2, there))
-                def _():
-                    copy2(j, q1, m - 1, d).wait_recv()
-                    if m < n2 - 1:
-                        when(onward)(lambda: copy2(j, q1, m, d).start())
+        for cond, arrive, _, _, _ in arrivals2(m):
+            when(cond)(arrive)
+
+    if late is not None:
+        for m in range(1, n2):
+            late.extend(arrivals2(m))
 
     def finish():
         for j, k, side, q1, there in shards:
@@ -599,6 +609,158 @@
     )(x, db, wo, down, q, k, v, mixed, cos, sin, first, order)
 
 
+def feed_kernel(n, chunks, halves, *refs):
+    x, down, w_hbm, g_hbm = refs[:4]
+    out, wd_out, act_ref, back_ref = refs[4:8]
+    held, down_held, shard, w, g, wd, pre, local, gsem, s1, r1, s2, r2, s3 = refs[8:]
+    n_a, n_b, a, b, f = places(n)
+    c = a * n_b + b
+    rows = x.shape[0]
+    pair = 2 * rows
+    ffs = wd.shape[0]
+    h = a // 2
+    mine = f == c // (n // lax.axis_size("fsdp"))
+    loads = [
+        pltpu.make_async_copy(src, dst, local.at[i])
+        for i, (src, dst) in enumerate(((x, held), (w_hbm, w), (down, down_held)))
+    ]
+    loads += [
+        pltpu.make_async_copy(
+            g_hbm.at[q * n_b + p], g.at[pl.ds((p * n_a + q) * rows, rows)], gsem.at[q * n_b + p]
+        )
+        for q in range(n_a)
+        for p in range(n_b)
+    ]
+    for copy in loads:
+        copy.start()
+    greet(a, b, n_a, n_b, f, True)
+    steps, parts, ends = [], [], []
+    for i, chunk in enumerate(chunks):
+        late = []
+        more, end = gather_steps(n, x, out, chunk, (s1.at[i], r1.at[i], s2.at[i], r2.at[i]), late)
+        steps.append(more)
+        parts.append(late)
+        ends.append(end)
+    spread = [
+        spread_steps(n, down, wd_out, half, [s3.at[i, j] for j in range(4)])
+        for i, half in enumerate(halves)
+    ]
+
+    def forward(p, half, buf):
+        fetches = [
+            pltpu.make_async_copy(
+                out.at[(2 * half + i) * n_b + p], shard.at[pl.ds(i * rows, rows)], local.at[3 + i]
+            )
+            for i in (0, 1)
+        ]
+        for copy in fetches:
+            copy.start()
+        for copy in fetches:
+            copy.wait()
+        pre[buf] = dot(shard[...], w[...], NN)
+
+    def backward(p, half, buf):
+        gate, up = pre[buf, :, :ffs], pre[buf, :, ffs:]
+        sigma = jax.nn.sigmoid(gate)
+        gate_act = gate * sigma
+        at = pl.multiple_of((p * n_a + 2 * half) * rows, pair)
+        d_act = dot(g[pl.ds(at, pair), :], wd[...], NT)
+        act = (gate_act * up).astype(bf16)
+        d_gate = (d_act * up * sigma * (1.0 + gate * (1.0 - sigma))).astype(bf16)
+        d_up = (d_act * gate_act).astype(bf16)
+        for i in (0, 1):
+            to = pl.ds(pl.multiple_of(((2 * half + i) * n_b + p) * rows, rows), rows)
+            own = slice(i * rows, (i + 1) * rows)
+            act_ref[to, :] = act[own]
+            back_ref[to, :ffs] = d_gate[own]
+            back_ref[to, ffs:] = d_up[own]
+
+    for more in steps:
+        more[0]()
+    for begin, _, _ in spread:
+        begin()
+    loads[0].wait()
+    keep = pltpu.make_async_copy(held, out.at[c], local.at[0])
+    keep.start()
+    loads[2].wait()
+    keep_down = pltpu.make_async_copy(down_held, wd_out, local.at[2])
+    pl.when(mine)(keep_down.start)
+    loads[1].wait()
+    keep.wait()
+    for k in range(1, n_a):
+        for more in steps:
+            more[k]()
+        if k == 1:
+            forward(b, h, 0)
+    forward(b, 1 - h, 1)
+    for _, onward, _ in spread:
+        onward()
+    pl.when(mine)(keep_down.wait)
+    fetch = pltpu.make_async_copy(wd_out, wd, local.at[5])
+    fetch.start()
+    fetch.wait()
+    for copy in loads[3:]:
+        copy.wait()
+    backward(b, h, 0)
+    backward(b, 1 - h, 1)
+    for m in range(1, n_b):
+        for d, p, there in ((0, b - m, b >= m), (1, b + m, b + m < n_b)):
+            for half, near in ((h, True), (1 - h, False)):
+                for late in zip(*parts):
+                    if late[0][2:] == (m, d, near):
+                        for cond, arrive, _, _, _ in late:
+                            pl.when(cond)(arrive)
+
+                @pl.when(there)
+                def _():
+                    forward(p, half, 0)
+                    backward(p, half, 0)
+
+    for _, _, end in spread:
+        end()
+    for end in ends:
+        end()
+
+
+def feed_gather(x, down, wgu, g, n, cid):
+    rows, width = x.shape
+    ffs = down.shape[0]
+    half = rows // 2
+    chunks = ((0, half, False), (half, half, False))
+    cut = ffs // 32 * 16
+    halves = ((0, ffs),) if ffs % 16 else ((0, cut), (cut, ffs - cut))
+    hbm = pl.BlockSpec(memory_space=pl.ANY)
+    vmem = pl.BlockSpec(memory_space=pltpu.VMEM)
+    return pl.pallas_call(
+        functools.partial(feed_kernel, n, chunks, halves),
+        out_shape=[
+            jax.ShapeDtypeStruct((n, rows, width), bf16),
+            jax.ShapeDtypeStruct((ffs, width), bf16),
+            jax.ShapeDtypeStruct((n * rows, ffs), bf16),
+            jax.ShapeDtypeStruct((n * rows, 2 * ffs), bf16),
+        ],
+        in_specs=[hbm] * 4,
+        out_specs=[hbm, hbm, vmem, vmem],
+        scratch_shapes=[
+            pltpu.VMEM((rows, width), bf16),
+            pltpu.VMEM((ffs, width), bf16),
+            pltpu.VMEM((2 * rows, width), bf16),
+            pltpu.VMEM(wgu.shape, bf16),
+            pltpu.VMEM((n * rows, width), bf16),
+            pltpu.VMEM((ffs, width), bf16),
+            pltpu.VMEM((2, 2 * rows, 2 * ffs), f32),
+            pltpu.SemaphoreType.DMA((6,)),
+            pltpu.SemaphoreType.DMA((n,)),
+        ]
+        + gather_sems(len(chunks))
+        + [pltpu.SemaphoreType.DMA((2, 4))],
+        compiler_params=pltpu.CompilerParams(
+            collective_id=cid, has_side_effects=True, vmem_limit_bytes=60 << 20
+        ),
+        name=f"feed{cid}",
+    )(x, down, wgu, g)
+
+
 def order_of(p, n):
     if n == 2:
         return (1 - p, p)
@@ -982,18 +1144,6 @@
 
     x_own = tokens[0]
     gains = jnp.pad(jnp.stack([norm1_gain, norm2_gain]), ((0, 6), (0, 0)))
-    x_all, wo_own, down_own, gains = gather_first(
-        x_own, w_out, w_down, gains, n_ctx, ratio, ffs, 0
-    )
-    x_all = x_all.reshape(all_rows, width)
-
-    qkv_own = jnp.concatenate(
-        [lax.dynamic_slice(w_qkv, (0, i * width + me * hw), (kr, hw)) for i in range(3)], -1
-    )
-    wq = lax.all_gather(qkv_own.astype(bf16), "fsdp", axis=0, tiled=True)
-    gain_one = gains[:, 0].reshape(width).astype(bf16).astype(f32)
-    gain_two = gains[:, 1].reshape(width).astype(bf16).astype(f32)
-    wo = lax.all_gather(wo_own, "fsdp", axis=0, tiled=True)
     wg_own = jnp.concatenate(
         [
             lax.dynamic_slice(w_gate_up, (0, me * ffs), (kr, ffs)),
@@ -1001,7 +1151,21 @@
         ],
         -1,
     ).astype(bf16)
+    first_x, wg_own = lax.optimization_barrier((x_own, wg_own))
+    x_all, wo_own, down_own, gains = gather_first(
+        first_x, w_out, w_down, gains, n_ctx, ratio, ffs, 0
+    )
+    x_all = x_all.reshape(all_rows, width)
+
+    qkv_own = jnp.concatenate(
+        [lax.dynamic_slice(w_qkv, (0, i * width + me * hw), (kr, hw)) for i in range(3)], -1
+    )
+    wq = lax.all_gather(qkv_own.astype(bf16), "fsdp", axis=0, tiled=True)
+    gain_one = gains[:, 0].reshape(width).astype(bf16).astype(f32)
+    gain_two = gains[:, 1].reshape(width).astype(bf16).astype(f32)
     wgu = lax.all_gather(wg_own, "fsdp", axis=0, tiled=True)
+    wo_own, wgu = lax.optimization_barrier((wo_own, wgu))
+    wo = lax.all_gather(wo_own, "fsdp", axis=0, tiled=True)
 
     deal_table = deal[0]
     device_index = jnp.arange(n_ctx, dtype=jnp.int32)
@@ -1036,20 +1200,8 @@
     hidden = x_dealt.reshape(rows, width).astype(f32) + dot(mixed_own, wo, NN)
     scale_two = rms_scale(hidden)
     normed_two = (hidden * scale_two * gain_two[None, :]).astype(bf16)
-    n2_all, wd = gather_ctx([normed_two], n_ctx, 2, spread=down_own)
+    n2_all, wd, activated, d_both = feed_gather(normed_two, down_own, wgu, g_all.reshape(n_ctx, rows, width), n_ctx, 2)
     n2_all = n2_all.reshape(all_rows, width)
-
-    both = dot(n2_all, wgu, NN)
-    gate = both[:, :ffs]
-    up = both[:, ffs:]
-    sigma = jax.nn.sigmoid(gate)
-    gate_act = gate * sigma
-    activated = (gate_act * up).astype(bf16)
-
-    d_act = dot(g_all, wd, NT)
-    d_both = jnp.concatenate(
-        [d_act * up * sigma * (1.0 + gate * (1.0 - sigma)), d_act * gate_act], -1
-    ).astype(bf16)
     if n_ctx == 8:
         arrays = [activated, wd, d_both, wgu, n2_all, g_all]
         down_rows, d_two, grad_gate_up, grad_down = reduce_ctx(

time: 761 us -> 755 us (level)
  matrix products: 20.8 us -> 4.74 us
  waiting for transfers between devices: 5.06 us -> 15.1 us
    pallas_call x0 -> x1, Pallas kernels: none -> 57.2 us  [feed_gather(): pl.pallas_call(functools.partial(feed_kernel, n, chunks, halves), out_sha...]
    pallas_call x4 -> x3, Pallas kernels: 255 us -> 199 us  [gather_ctx(): pl.pallas_call(functools.partial(gather_kernel, n, plans, parts), out_sha...]
    dot_general x3 -> x1, matrix products: 20.8 us -> 4.74 us  [dot(): return lax.dot_general(a, b, (dims, ((), ())), preferred_element_type=f32)]
    all_gather x1, waiting for transfers between devices: 0.01 us -> 9.05 us  [shards(): wq = lax.all_gather(qkv_own.astype(bf16), 'fsdp', axis=0, tiled=True)]
  transfers between devices with their start and end apart: 8 -> 8, of which waited for: 1 -> 2; matrix products, arithmetic and copies ran while one was open for 5% -> 4% of each run, Pallas kernels for 58% -> 51%
where the time goes in v6:
time: 755 us; the launch traced here: 750 us
  Pallas kernels  672 us (89%)
  local copies, waits for them, and re-layouts  19 us (3%)
  other arithmetic  18.6 us (2%)
  waiting for transfers between devices  15.1 us (2%)
  between operations  14.7 us (2%)
    pallas_call x3, Pallas kernels, gather_ctx(): pl.pallas_call(functools.partial(gather_kernel, n, plans, parts), out_sha...  199 us
    pallas_call x2, Pallas kernels, reduce_ctx(): pl.pallas_call(functools.partial(reduce_kernel, n, chunks, jobs, extras,...  152 us
    pallas_call x1, Pallas kernels, back_gather(): pl.pallas_call(functools.partial(back_gather_kernel, n, chunks, heads, bl...  123 us
    pallas_call x1, Pallas kernels, attend_gather(): pl.pallas_call(functools.partial(attend_gather_kernel, n, chunks, heads,...  60.1 us
    pallas_call x1, Pallas kernels, feed_gather(): pl.pallas_call(functools.partial(feed_kernel, n, chunks, halves), out_sha...  57.2 us
    pallas_call x1, Pallas kernels, gather_first(): pl.pallas_call(functools.partial(first_kernel, n, chunks, ratio), out_sha...  50.2 us
    pallas_call x2, Pallas kernels, assemble(): pl.pallas_call(body, grid=(rows // block,), out_shape=jax.ShapeDtypeStruc...  22.6 us
  transfers between devices with their start and end apart: 8, of which 2 were waited for; matrix products, arithmetic and copies ran while one was open for 4% of the time, Pallas kernels for 51%

profile of v6, /device:TPU:0, one launch (start us, length us, event | category | flops | bytes accessed | tf_op | source)
XLA Modules:
  0.0 750.5 jit_solution(13474869598051729789)
XLA Ops:
  7.2 2.6 dynamic-slice_convert_fusion.1
  9.8 1.5 pad_maximum_fusion
  11.4 1.5 dynamic-slice_convert_fusion.4
  12.9 0.9 pad_maximum_fusion.1
  13.9 0.6 select_maximum_fusion.refs_3_
  14.5 50.2 %gather0.1 = (bf16[8,128,2048]{2,1,0:T(8,128)(2,1)}, bf16[512,2048]{1,0:T(8,128)(2,1)}, bf16[688,2048]{1,0:T(8,128)(2,1)}, f32[4,8,512]{2,1,0:T(8,128)}) custom-call(bf16[128,2048]{1,0:T(8,128)(2,1)} %bitcast.62, f32[512,2048]{1,0:T(8,128)} %refs_1_.1, f32[1376,2048]{1,0:T(8,128)} %refs_2_.1, f32[8,512]{1,0:T(8,128)} %select_maximum_fusion.refs_3_), custom_call_target="tpu_custom_call" | custom-call | tf_op jit(solution)/shard_map/gather0/pallas_call | solution.py:377
  64.8 0.2 reduce-scatter.7.cloned.1.call-start
  65.1 0.2 reduce-window.4
  65.8 1.1 add.190.refs_6_
  67.1 1.0 copy.29.refs_5_.refs_10_
  68.1 0.9 convert.26
  69.1 2.8 gather_fusion
  71.9 1.9 fusion.21
  73.8 1.3 pad_maximum_fusion.2
  75.1 0.9 multiply_reduce_fusion
  76.1 3.0 fusion.1.refs_1_.refs_2_
  79.2 9.1 %all-gather.4.cloned.1.call-done.refs_2_.refs_1_ = bf16[2048,768]{1,0:T(8,128)(2,1)} async-done(((bf16[512,768]{1,0:T(8,128)(2,1)}), bf16[2048,768]{1,0:T(8,128)(2,1)}) %all-gather.4.cloned.1.call-update) | async-done | bytes 3145744 | tf_op jit(solution)/shard_map/all_gather | solution.py:1163
  88.3 60.1 %attend1.1 = (bf16[8,128,2048]{2,1,0:T(8,128)(2,1)}, bf16[1024,256]{1,0:T(8,128)(2,1)}, bf16[1024,256]{1,0:T(8,128)(2,1)}, bf16[1024,256]{1,0:T(8,128)(2,1)}, bf...) custom-call(bf16[128,2048]{1,0:T(8,128)(2,1)} %bitcast.67, bf16[1024,2048]{1,0:T(8,128)(2,1)} %fusion.1.refs_1_.refs_2_, ...), custom_call_target="tpu_custom_call" | custom-call | tf_op jit(solution)/shard_map/attend1/pallas_call | solution.py:498
  148.4 1.3 copy.31
  149.7 4.7 multiply_reduce_fusion.1
  154.5 1.0 multiply_convert_fusion.refs_0_
  155.4 57.2 %feed2.1 = (bf16[8,128,2048]{2,1,0:T(8,128)(2,1)}, bf16[688,2048]{1,0:T(8,128)(2,1)}, bf16[1024,688]{1,0:T(8,128)(2,1)}, bf16[1024,1376]{1,0:T(8,128)(2,1)}) custom-call(bf16[128,2048]{1,0:T(8,128)(2,1)} %multiply_convert_fusion.refs_0_, bf16[688,2048]{1,0:T(8,128)(2,1)} %get-tuple-element.48.refs_1_, ...), custom_call_target="tpu_custom_call" | custom-call | tf_op jit(solution)/shard_map/feed2/pallas_call | solution.py:734
  212.6 100.5 %reduce4.1 = (bf16[128,2048]{1,0:T(8,128)(2,1)}, bf16[128,2048]{1,0:T(8,128)(2,1)}, bf16[2048,1376]{1,0:T(8,128)(2,1)}, bf16[688,2048]{1,0:T(8,128)(2,1)}) custom-call(bf16[1024,688]{1,0:T(8,128)(2,1)} %get-tuple-element.51.refs_0_, bf16[688,2048]{1,0:T(8,128)(2,1)} %get-tuple-element.52.refs_1_, bf16[1024,1376]{1,0:T(8,128)(2,1)} %get-tuple-element.53.refs_2_, ...), custom_call_target="tpu_custom_call" | custom-call | tf_op jit(solution)/shard_map/reduce4/pallas_call | solution.py:987
  313.3 1.1 add.191.refs_11_
  314.4 0.3 fusion.13
  314.8 1.4 fusion.10
  316.2 46.4 %gather3.1 = bf16[8,128,2048]{2,1,0:T(8,128)(2,1)} custom-call(bf16[128,2048]{1,0:T(8,128)(2,1)} %get-tuple-element.88.refs_0_), custom_call_target="tpu_custom_call" | custom-call | tf_op jit(solution)/shard_map/gather3/pallas_call | solution.py:279
  362.5 5.2 reduce-scatter.7.cloned.1.call-done.refs_0_
  367.8 122.6 %back7.1 = (bf16[8,512,1376]{2,1,0:T(8,128)(2,1)}, bf16[1024,768]{1,0:T(8,128)(2,1)}, bf16[944,2048]{1,0:T(8,128)(2,1)}) custom-call(bf16[512,1376]{1,0:T(8,128)(2,1)} %reduce-scatter.7.cloned.1.call-done.refs_0_, bf16[1024,2048]{1,0:T(8,128)(2,1)} %bitcast.58, bf16[2048,2048]{1,0:T(8,128)(2,1)} %all-gather.8.cloned.1.call-done.refs_2_, ...), custom_call_target="tpu_custom_call" | custom-call | tf_op jit(solution)/shard_map/back7/pallas_call | solution.py:583
  490.5 1.0 copy-done.1
  491.4 0.2 fusion.14
  491.6 51.4 %reduce6.1 = (bf16[128,2048]{1,0:T(8,128)(2,1)}, bf16[2048,768]{1,0:T(8,128)(2,1)}) custom-call(bf16[1024,768]{1,0:T(8,128)(2,1)} %get-tuple-element.63.refs_0_, bf16[2048,768]{1,0:T(8,128)(2,1)} %all-gather.4.cloned.1.call-done.refs_2_.refs_1_, bf16[1024,2048]{1,0:T(8,128)(2,1)} %fusion.1.refs_1_.refs_2_), custom_call_target="tpu_custom_call" | custom-call | tf_op jit(solution)/shard_map/reduce6/pallas_call | solution.py:987
  543.0 1.4 fusion.18
  544.4 1.3 copy.34
  545.9 0.7 reduce-scatter.9.cloned.1.call-update
  546.6 81.5 %gather9.1 = bf16[8,944,512]{2,1,0:T(8,128)(2,1)} custom-call(bf16[944,512]{1,0:T(8,128)(2,1)} %reduce-scatter.11.cloned.1.call-done.refs_0_), custom_call_target="tpu_custom_call" | custom-call | tf_op jit(solution)/shard_map/gather9/pallas_call | solution.py:279
  628.1 5.5 all-to-all-start
  633.7 2.8 gather_fusion.1
  636.4 0.1 broadcast_select_fusion
  636.6 13.8 %assemble.3 = f32[512,11008]{1,0:T(8,128)} custom-call(bf16[8,512,1376]{2,1,0:T(8,128)(2,1)} %get-tuple-element.71.i_ref), custom_call_target="tpu_custom_call" | custom-call | tf_op jit(solution)/shard_map/assemble/pallas_call | solution.py:1043
  650.4 1.3 fusion.20
  651.7 1.1 copy.35
  652.7 0.6 pad.8.refs_1_
  653.3 70.7 %gather8.1 = (bf16[8,512,768]{2,1,0:T(8,128)(2,1)}, f32[8,8,512]{2,1,0:T(8,128)}) custom-call(bf16[512,768]{1,0:T(8,128)(2,1)} %reduce-scatter.9.cloned.1.call-done.refs_0_, f32[8,512]{1,0:T(8,128)} %pad.8.refs_1_), custom_call_target="tpu_custom_call" | custom-call | tf_op jit(solution)/shard_map/gather8/pallas_call | solution.py:279
  724.1 0.9 reduce_sum.112
  725.0 8.8 %assemble.2 = f32[512,6144]{1,0:T(8,128)} custom-call(bf16[8,512,768]{2,1,0:T(8,128)(2,1)} %get-tuple-element.69.i_ref), custom_call_target="tpu_custom_call" | custom-call | tf_op jit(solution)/shard_map/assemble/pallas_call | solution.py:1043
  733.8 0.6 fusion.23
  734.4 9.0 %assemble_rows.1 = (f32[1376,2048]{1,0:T(8,128)}, f32[512,2048]{1,0:T(8,128)}) custom-call(bf16[4,1888,512]{2,1,0:T(8,128)(2,1)} %all-to-all-done.i_ref), custom_call_target="tpu_custom_call" | custom-call | tf_op jit(solution)/shard_map/assemble_rows/pallas_call | solution.py:1017
  (66 shorter events, 1.6 us)
Async XLA Ops:
  7.2 57.6 %all-gather.6.cloned.1.call-start = ((), (), s32[]{:S(2)}) async-start(), calls=%async_computation.6 | async-start | bytes 7208960 | tf_op jit(solution)/shard_map/all_gather | solution.py:1166
  9.8 4.1 copy-start.7
  9.8 4.1 copy-start.8
  11.4 76.9 %all-gather.4.cloned.1.call-start = ((), (), s32[]{:S(2)}) async-start(), calls=%async_computation.5 | async-start | bytes 3932160 | tf_op jit(solution)/shard_map/all_gather | solution.py:1163
  13.8 135.9 %all-gather.8.cloned.1.call-start = ((), (), s32[]{:S(2)}) async-start(), calls=%async_computation.7 | async-start | bytes 10485760 | tf_op jit(solution)/shard_map/all_gather | solution.py:1168
  14.5 50.5 %copy-start.9 = (s32[1,3]{1,0:T(1,128)S(1)}, s32[1,3]{1,0:T(1,128)}, u32[]{:S(2)}) copy-start(s32[1,3]{1,0:T(1,128)} %param.14) | copy-start | bytes 40
  14.5 50.7 %copy-start.6 = (s32[1,8,8]{2,1,0:T(8,128)S(1)}, s32[1,8,8]{2,1,0:T(8,128)}, u32[]{:S(2)}) copy-start(s32[1,8,8]{2,1,0:T(8,128)} %param.15) | copy-start | bytes 772
  64.8 302.9 %reduce-scatter.7.cloned.1.call-start = ((), (), s32[]{:S(2)}) async-start(), calls=%async_computation.8 | async-start | bytes 7208960 | tf_op jit(solution)/shard_map/reduce_scatter | solution.py:1219
  71.9 3.3 copy-start
  313.1 1.3 copy-start.4
  313.2 1.6 copy-start.2
  313.2 1.6 copy-start.5
  313.2 233.4 %reduce-scatter.11.cloned.1.call-start = ((), (), s32[]{:S(2)}) async-start(), calls=%async_computation.10 | async-start | bytes 4833280 | tf_op jit(solution)/shard_map/reduce_scatter | solution.py:1262
  490.4 1.0 copy-start.1
  490.4 161.2 %reduce-scatter.13.cloned.1.call-start = ((), (), s32[]{:S(2)}) async-start(), calls=%async_computation.11 | async-start | bytes 1310720
  545.8 107.5 %reduce-scatter.9.cloned.1.call-start = ((), (), s32[]{:S(2)}) async-start(), calls=%async_computation.9 | async-start | bytes 3932160 | tf_op jit(solution)/shard_map/reduce_scatter | solution.py:1248
  628.1 106.2 %all-to-all-start = ((bf16[4,1888,512]{2,1,0:T(8,128)(2,1)}), bf16[4,1888,512]{2,1,0:T(8,128)(2,1)}, u32[]{:S(2)}, u32[]{:S(2)}) async-start(bf16[4,1888,512]{2,1,0:T(8,128)(2,1)} %bitcast.57), calls=%async_computation.3 | async-start | bytes 15466496 | tf_op jit(solution)/shard_map/all_to_all | solution.py:1265
  636.5 13.8 %copy-start.3 = (bf16[128,2048]{1,0:T(8,128)(2,1)S(1)}, bf16[128,2048]{1,0:T(8,128)(2,1)}, u32[]{:S(2)}) copy-start(bf16[128,2048]{1,0:T(8,128)(2,1)} %get-tuple-element.64) | copy-start | bytes 1572868
Sparse Core Ops, SparseCore 0:
  11.5 46.0 all-gather.5
  59.7 28.5 all-gather.3
  89.8 58.2 all-gather.7
  313.3 54.3 reduce-scatter.6
  490.6 41.5 reduce-scatter.10
  545.9 24.1 reduce-scatter.12
  572.9 37.9 reduce-scatter.8

commit v7 on v6

--- a/solution.py
+++ b/solution.py
@@ -307,8 +307,9 @@
 
 
 def first_kernel(n, chunks, ratio, *refs):
-    x, wo, wd, g, out, wo_out, wd_out, g_out = refs[:8]
-    held, wo_wide, wo_low, wd_wide, wd_low, g_held, local, s1, r1, s2, r2, gs, gr = refs[8:]
+    x, wo, wd, g, wq, out, wo_out, wd_out, g_out, wq_out = refs[:10]
+    held, wo_wide, wo_low, wd_wide, wd_low, g_held, wq_held, local = refs[10:18]
+    s1, r1, s2, r2, gs, gr, ys, yr, cs, cr = refs[18:]
     n_a, n_b, a, b, f = places(n)
     c = a * n_b + b
     n_f = lax.axis_size("fsdp")
@@ -316,12 +317,12 @@
     own = pl.ds(pl.multiple_of((c % ratio) * ffs, 8), ffs)
     loads = [
         pltpu.make_async_copy(src, dst, local.at[i])
-        for i, (src, dst) in enumerate(((x, held), (wo, wo_wide), (wd.at[own], wd_wide), (g, g_held)))
+        for i, (src, dst) in enumerate(((x, held), (wo, wo_wide), (wd.at[own], wd_wide), (g, g_held), (wq, wq_held)))
     ]
     stores = [
         pltpu.make_async_copy(src, dst, local.at[i])
         for i, (src, dst) in enumerate(
-            ((held, out.at[c]), (wo_low, wo_out), (wd_low, wd_out), (g_held, g_out.at[f]))
+            ((held, out.at[c]), (wo_low, wo_out), (wd_low, wd_out), (g_held, g_out.at[f]), (wq_held, wq_out.at[f]))
         )
     ]
     for copy in loads:
@@ -343,13 +344,43 @@
             device_id_type=MESH,
         )
 
+    def along(m):
+        return pltpu.make_async_remote_copy(
+            src_ref=wq,
+            dst_ref=wq_out.at[f],
+            send_sem=ys.at[m],
+            recv_sem=yr.at[m],
+            device_id=(c, (f + 2 * m) % n_f),
+            device_id_type=MESH,
+        )
+
+    def across(m):
+        at = (f + n_f - 2 * m) % n_f
+        return pltpu.make_async_remote_copy(
+            src_ref=wq if m == 0 else wq_out.at[at],
+            dst_ref=wq_out.at[at],
+            send_sem=cs.at[m],
+            recv_sem=cr.at[m],
+            device_id=(c, f + 1 - 2 * (f % 2)),
+            device_id_type=MESH,
+        )
+
+    for m in range(1, n_f // 2):
+        along(m).start()
+    across(0).start()
     for t in range(n_a + n_b - 1):
         for more in steps:
             if t < len(more):
                 more[t]()
+        if t == 2:
+            for m in range(1, n_f // 2):
+                along(m).wait_recv()
+                across(m).start()
         if t == 0:
             for m in range(1, n_f):
                 gain(m).start()
+            loads[4].wait()
+            stores[4].start()
             loads[0].wait()
             stores[0].start()
             loads[3].wait()
@@ -365,11 +396,15 @@
         copy.wait()
     for m in range(1, n_f):
         gain(m).wait()
+    for m in range(n_f // 2):
+        across(m).wait()
+        if m:
+            along(m).wait_send()
     for end in ends:
         end()
 
 
-def gather_first(x, w_out, w_down, gains, n, ratio, ffs, cid):
+def gather_first(x, w_out, w_down, gains, wq, n, ratio, ffs, cid):
     n_f = lax.axis_size("fsdp")
     chunks = plan(x.shape[0])
     low = [jax.ShapeDtypeStruct(w_out.shape, bf16), jax.ShapeDtypeStruct((ffs, w_down.shape[1]), bf16)]
@@ -378,9 +413,9 @@
         functools.partial(first_kernel, n, chunks, ratio),
         out_shape=[jax.ShapeDtypeStruct((n,) + x.shape, x.dtype)]
         + low
-        + [jax.ShapeDtypeStruct((n_f,) + gains.shape, gains.dtype)],
-        in_specs=[pl.BlockSpec(memory_space=pl.ANY)] * 4,
-        out_specs=[pl.BlockSpec(memory_space=pl.ANY)] * 4,
+        + [jax.ShapeDtypeStruct((n_f,) + y.shape, y.dtype) for y in (gains, wq)],
+        in_specs=[pl.BlockSpec(memory_space=pl.ANY)] * 5,
+        out_specs=[pl.BlockSpec(memory_space=pl.ANY)] * 5,
         scratch_shapes=[
             pltpu.VMEM(x.shape, x.dtype),
             pltpu.VMEM(w_out.shape, f32),
@@ -388,15 +423,16 @@
             pltpu.VMEM((ffs, w_down.shape[1]), f32),
             pltpu.VMEM((ffs, w_down.shape[1]), bf16),
             pltpu.VMEM(gains.shape, gains.dtype),
-            sem((4,)),
+            pltpu.VMEM(wq.shape, wq.dtype),
+            sem((5,)),
         ]
         + gather_sems(len(chunks))
-        + [sem((n_f,)), sem((n_f,))],
+        + [sem((n_f,))] * 6,
         compiler_params=pltpu.CompilerParams(
             collective_id=cid, has_side_effects=True, vmem_limit_bytes=60 << 20
         ),
         name=f"gather{cid}",
-    )(x, w_out, w_down, gains)
+    )(x, w_out, w_down, gains, wq)
 
 
 def attend_gather_kernel(n, chunks, heads, block, *refs):
@@ -1144,6 +1180,9 @@
 
     x_own = tokens[0]
     gains = jnp.pad(jnp.stack([norm1_gain, norm2_gain]), ((0, 6), (0, 0)))
+    qkv_own = jnp.concatenate(
+        [lax.dynamic_slice(w_qkv, (0, i * width + me * hw), (kr, hw)) for i in range(3)], -1
+    )
     wg_own = jnp.concatenate(
         [
             lax.dynamic_slice(w_gate_up, (0, me * ffs), (kr, ffs)),
@@ -1152,15 +1191,12 @@
         -1,
     ).astype(bf16)
     first_x, wg_own = lax.optimization_barrier((x_own, wg_own))
-    x_all, wo_own, down_own, gains = gather_first(
-        first_x, w_out, w_down, gains, n_ctx, ratio, ffs, 0
+    x_all, wo_own, down_own, gains, wq = gather_first(
+        first_x, w_out, w_down, gains, qkv_own.astype(bf16), n_ctx, ratio, ffs, 0
     )
     x_all = x_all.reshape(all_rows, width)
-
-    qkv_own = jnp.concatenate(
-        [lax.dynamic_slice(w_qkv, (0, i * width + me * hw), (kr, hw)) for i in range(3)], -1
-    )
-    wq = lax.all_gather(qkv_own.astype(bf16), "fsdp", axis=0, tiled=True)
+    wq = wq.reshape(width, 3 * hw)
+
     gain_one = gains[:, 0].reshape(width).astype(bf16).astype(f32)
     gain_two = gains[:, 1].reshape(width).astype(bf16).astype(f32)
     wgu = lax.all_gather(wg_own, "fsdp", axis=0, tiled=True)

time: 755 us -> 750 us (level)
    all_gather x1 -> x0, waiting for transfers between devices: 9.05 us -> none  [shards(): wq = lax.all_gather(qkv_own.astype(bf16), 'fsdp', axis=0, tiled=True)]
  transfers between devices with their start and end apart: 8 -> 7, of which waited for: 2 -> 2; matrix products, arithmetic and copies ran while one was open for 4% -> 4% of each run, Pallas kernels for 51% -> 51%
where the time goes in v7:
time: 750 us; the launch traced here: 746 us
  Pallas kernels  674 us (90%)
  local copies, waits for them, and re-layouts  19 us (3%)
  other arithmetic  18.9 us (3%)
  between operations  14.7 us (2%)
  waiting for transfers between devices  8.88 us (1%)
    pallas_call x3, Pallas kernels, gather_ctx(): pl.pallas_call(functools.partial(gather_kernel, n, plans, parts), out_sha...  199 us
    pallas_call x2, Pallas kernels, reduce_ctx(): pl.pallas_call(functools.partial(reduce_kernel, n, chunks, jobs, extras,...  153 us
    pallas_call x1, Pallas kernels, back_gather(): pl.pallas_call(functools.partial(back_gather_kernel, n, chunks, heads, bl...  123 us
    pallas_call x1, Pallas kernels, attend_gather(): pl.pallas_call(functools.partial(attend_gather_kernel, n, chunks, heads,...  60.3 us
    pallas_call x1, Pallas kernels, feed_gather(): pl.pallas_call(functools.partial(feed_kernel, n, chunks, halves), out_sha...  57.9 us
    pallas_call x1, Pallas kernels, gather_first(): pl.pallas_call(functools.partial(first_kernel, n, chunks, ratio), out_sha...  50.4 us
    pallas_call x2, Pallas kernels, assemble(): pl.pallas_call(body, grid=(rows // block,), out_shape=jax.ShapeDtypeStruc...  22.6 us
  transfers between devices with their start and end apart: 7, of which 2 were waited for; matrix products, arithmetic and copies ran while one was open for 4% of the time, Pallas kernels for 51%

profile of v7, /device:TPU:0, one launch (start us, length us, event | category | flops | bytes accessed | tf_op | source)
XLA Modules:
  0.0 746.2 jit_solution(12133795248492958781)
XLA Ops:
  7.2 2.6 dynamic-slice_convert_fusion.1
  9.8 1.5 pad_maximum_fusion
  11.4 0.6 select_maximum_fusion.refs_3_
  12.1 1.4 dynamic-slice_convert_fusion.4
  13.5 0.9 pad_maximum_fusion.1.refs_4_
  14.4 50.4 %gather0.1 = (bf16[8,128,2048]{2,1,0:T(8,128)(2,1)}, bf16[512,2048]{1,0:T(8,128)(2,1)}, bf16[688,2048]{1,0:T(8,128)(2,1)}, f32[4,8,512]{2,1,0:T(8,128)}, bf16[4,512,768]{2,1,0:T(8,128)(2,1)}) custom-call(bf16[128,2048]{1,0:T(8,128)(2,1)} %bitcast.65, f32[512,2048]{1,0:T(8,128)} %refs_1_.1, f32[1376,2048]{1,0:T(8,128)} %refs_2_.1, ...), custom_call_target="tpu_custom_call" | custom-call | tf_op jit(solution)/shard_map/gather0/pallas_call | solution.py:412
  64.9 4.8 all-gather.3.cloned.1.call-done.refs_2_.refs_3_
  69.7 0.2 reduce-scatter.7.cloned.1.call-start
  70.0 0.2 reduce-window.4
  70.7 1.1 add.190.refs_6_
  72.0 1.0 copy.29.refs_5_.refs_10_
  73.1 1.0 convert.29
  74.1 1.9 fusion.21
  76.0 1.3 pad_maximum_fusion.2
  77.3 0.9 multiply_reduce_fusion
  78.2 3.2 fusion.1.refs_1_.refs_2_
  81.4 60.3 %attend1.1 = (bf16[8,128,2048]{2,1,0:T(8,128)(2,1)}, bf16[1024,256]{1,0:T(8,128)(2,1)}, bf16[1024,256]{1,0:T(8,128)(2,1)}, bf16[1024,256]{1,0:T(8,128)(2,1)}, bf...) custom-call(bf16[128,2048]{1,0:T(8,128)(2,1)} %bitcast.70, bf16[1024,2048]{1,0:T(8,128)(2,1)} %fusion.1.refs_1_.refs_2_, ...), custom_call_target="tpu_custom_call" | custom-call | tf_op jit(solution)/shard_map/attend1/pallas_call | solution.py:534
  141.7 1.3 copy.31
  143.1 2.8 gather_fusion
  146.1 4.7 multiply_reduce_fusion.1
  150.8 1.0 multiply_convert_fusion.refs_0_
  151.8 57.9 %feed2.1 = (bf16[8,128,2048]{2,1,0:T(8,128)(2,1)}, bf16[688,2048]{1,0:T(8,128)(2,1)}, bf16[1024,688]{1,0:T(8,128)(2,1)}, bf16[1024,1376]{1,0:T(8,128)(2,1)}) custom-call(bf16[128,2048]{1,0:T(8,128)(2,1)} %multiply_convert_fusion.refs_0_, bf16[688,2048]{1,0:T(8,128)(2,1)} %get-tuple-element.50.refs_1_, ...), custom_call_target="tpu_custom_call" | custom-call | tf_op jit(solution)/shard_map/feed2/pallas_call | solution.py:770
  209.7 101.2 %reduce4.1 = (bf16[128,2048]{1,0:T(8,128)(2,1)}, bf16[128,2048]{1,0:T(8,128)(2,1)}, bf16[2048,1376]{1,0:T(8,128)(2,1)}, bf16[688,2048]{1,0:T(8,128)(2,1)}) custom-call(bf16[1024,688]{1,0:T(8,128)(2,1)} %get-tuple-element.53.refs_0_, bf16[688,2048]{1,0:T(8,128)(2,1)} %get-tuple-element.54.refs_1_, bf16[1024,1376]{1,0:T(8,128)(2,1)} %get-tuple-element.55.refs_2_, ...), custom_call_target="tpu_custom_call" | custom-call | tf_op jit(solution)/shard_map/reduce4/pallas_call | solution.py:1023
  311.1 1.1 add.191.refs_11_
  312.2 0.3 fusion.13
  312.6 1.4 fusion.10
  313.9 46.3 %gather3.1 = bf16[8,128,2048]{2,1,0:T(8,128)(2,1)} custom-call(bf16[128,2048]{1,0:T(8,128)(2,1)} %get-tuple-element.90.refs_0_), custom_call_target="tpu_custom_call" | custom-call | tf_op jit(solution)/shard_map/gather3/pallas_call | solution.py:279
  360.3 3.4 reduce-scatter.7.cloned.1.call-done.refs_0_
  363.6 122.6 %back7.1 = (bf16[8,512,1376]{2,1,0:T(8,128)(2,1)}, bf16[1024,768]{1,0:T(8,128)(2,1)}, bf16[944,2048]{1,0:T(8,128)(2,1)}) custom-call(bf16[512,1376]{1,0:T(8,128)(2,1)} %reduce-scatter.7.cloned.1.call-done.refs_0_, bf16[1024,2048]{1,0:T(8,128)(2,1)} %bitcast.59, bf16[2048,2048]{1,0:T(8,128)(2,1)} %all-gather.5.cloned.1.call-done.refs_2_, ...), custom_call_target="tpu_custom_call" | custom-call | tf_op jit(solution)/shard_map/back7/pallas_call | solution.py:619
  486.3 1.0 copy-done.1
  487.3 0.2 fusion.14
  487.5 51.4 %reduce6.1 = (bf16[128,2048]{1,0:T(8,128)(2,1)}, bf16[2048,768]{1,0:T(8,128)(2,1)}) custom-call(bf16[1024,768]{1,0:T(8,128)(2,1)} %get-tuple-element.65.refs_0_, bf16[2048,768]{1,0:T(8,128)(2,1)} %bitcast.64, bf16[1024,2048]{1,0:T(8,128)(2,1)} %fusion.1.refs_1_.refs_2_), custom_call_target="tpu_custom_call" | custom-call | tf_op jit(solution)/shard_map/reduce6/pallas_call | solution.py:1023
  538.9 1.4 fusion.18
  540.3 1.3 copy.34
  541.7 0.5 reduce-scatter.9.cloned.1.call-update
  542.3 81.5 %gather9.1 = bf16[8,944,512]{2,1,0:T(8,128)(2,1)} custom-call(bf16[944,512]{1,0:T(8,128)(2,1)} %reduce-scatter.11.cloned.1.call-done.refs_0_), custom_call_target="tpu_custom_call" | custom-call | tf_op jit(solution)/shard_map/gather9/pallas_call | solution.py:279
  623.8 5.5 all-to-all-start
  629.3 2.8 gather_fusion.1
  632.1 0.1 broadcast_select_fusion
  632.2 13.8 %assemble.3 = f32[512,11008]{1,0:T(8,128)} custom-call(bf16[8,512,1376]{2,1,0:T(8,128)(2,1)} %get-tuple-element.73.i_ref), custom_call_target="tpu_custom_call" | custom-call | tf_op jit(solution)/shard_map/assemble/pallas_call | solution.py:1079
  646.1 1.3 fusion.20
  647.3 1.1 copy.35
  648.4 0.6 pad.8.refs_1_
  649.0 70.7 %gather8.1 = (bf16[8,512,768]{2,1,0:T(8,128)(2,1)}, f32[8,8,512]{2,1,0:T(8,128)}) custom-call(bf16[512,768]{1,0:T(8,128)(2,1)} %reduce-scatter.9.cloned.1.call-done.refs_0_, f32[8,512]{1,0:T(8,128)} %pad.8.refs_1_), custom_call_target="tpu_custom_call" | custom-call | tf_op jit(solution)/shard_map/gather8/pallas_call | solution.py:279
  719.8 0.9 reduce_sum.112
  720.7 8.8 %assemble.2 = f32[512,6144]{1,0:T(8,128)} custom-call(bf16[8,512,768]{2,1,0:T(8,128)(2,1)} %get-tuple-element.71.i_ref), custom_call_target="tpu_custom_call" | custom-call | tf_op jit(solution)/shard_map/assemble/pallas_call | solution.py:1079
  729.5 0.6 fusion.23
  730.1 9.0 %assemble_rows.1 = (f32[1376,2048]{1,0:T(8,128)}, f32[512,2048]{1,0:T(8,128)}) custom-call(bf16[4,1888,512]{2,1,0:T(8,128)(2,1)} %all-to-all-done.i_ref), custom_call_target="tpu_custom_call" | custom-call | tf_op jit(solution)/shard_map/assemble_rows/pallas_call | solution.py:1053
  (63 shorter events, 1.5 us)
Async XLA Ops:
  7.2 4.3 copy-start.7
  7.2 4.3 copy-start.8
  7.2 62.5 %all-gather.3.cloned.1.call-start = ((), (), s32[]{:S(2)}) async-start(), calls=%async_computation.5 | async-start | bytes 7208960 | tf_op jit(solution)/shard_map/all_gather | solution.py:1202
  11.4 134.7 %all-gather.5.cloned.1.call-start = ((), (), s32[]{:S(2)}) async-start(), calls=%async_computation.6 | async-start | bytes 10485760 | tf_op jit(solution)/shard_map/all_gather | solution.py:1204
  14.4 55.5 %copy-start.9 = (s32[1,3]{1,0:T(1,128)S(1)}, s32[1,3]{1,0:T(1,128)}, u32[]{:S(2)}) copy-start(s32[1,3]{1,0:T(1,128)} %param.14) | copy-start | bytes 40
  14.4 55.7 %copy-start.6 = (s32[1,8,8]{2,1,0:T(8,128)S(1)}, s32[1,8,8]{2,1,0:T(8,128)}, u32[]{:S(2)}) copy-start(s32[1,8,8]{2,1,0:T(8,128)} %param.15) | copy-start | bytes 772
  69.7 293.9 %reduce-scatter.7.cloned.1.call-start = ((), (), s32[]{:S(2)}) async-start(), calls=%async_computation.7 | async-start | bytes 7208960 | tf_op jit(solution)/shard_map/reduce_scatter | solution.py:1255
  73.1 4.2 copy-start
  310.9 1.3 copy-start.4
  310.9 1.6 copy-start.2
  310.9 1.6 copy-start.5
  311.0 231.3 %reduce-scatter.11.cloned.1.call-start = ((), (), s32[]{:S(2)}) async-start(), calls=%async_computation.9 | async-start | bytes 4833280 | tf_op jit(solution)/shard_map/reduce_scatter | solution.py:1298
  486.3 1.0 copy-start.1
  486.3 161.0 %reduce-scatter.13.cloned.1.call-start = ((), (), s32[]{:S(2)}) async-start(), calls=%async_computation.10 | async-start | bytes 1310720
  541.7 107.4 %reduce-scatter.9.cloned.1.call-start = ((), (), s32[]{:S(2)}) async-start(), calls=%async_computation.8 | async-start | bytes 3932160 | tf_op jit(solution)/shard_map/reduce_scatter | solution.py:1284
  623.8 106.3 %all-to-all-start = ((bf16[4,1888,512]{2,1,0:T(8,128)(2,1)}), bf16[4,1888,512]{2,1,0:T(8,128)(2,1)}, u32[]{:S(2)}, u32[]{:S(2)}) async-start(bf16[4,1888,512]{2,1,0:T(8,128)(2,1)} %bitcast.58), calls=%async_computation.3 | async-start | bytes 15466496 | tf_op jit(solution)/shard_map/all_to_all | solution.py:1301
  632.2 13.8 %copy-start.3 = (bf16[128,2048]{1,0:T(8,128)(2,1)S(1)}, bf16[128,2048]{1,0:T(8,128)(2,1)}, u32[]{:S(2)}) copy-start(bf16[128,2048]{1,0:T(8,128)(2,1)} %get-tuple-element.66) | copy-start | bytes 1572868
Sparse Core Ops, SparseCore 0:
  11.5 58.1 all-gather.2
  71.3 59.0 all-gather.4
  311.1 52.5 reduce-scatter.6
  486.4 41.5 reduce-scatter.10
  541.8 24.1 reduce-scatter.12
  568.6 37.9 reduce-scatter.8
